TPU v7x, 32 devices: a whole 2x2x4 slice. The times are simulated.
32 devices in a mesh: ep: 8 (over z, y), tp: 4 (over x, core).
Axes of the slice: x: 2, y: 2, z: 4, core: 2. Of those that a mesh axis runs over, the one named last changes fastest.
Arguments:
- tokens: bfloat16 [4096, 1536], P(('ep', 'tp')), may hold values from -6 to 6
- norm_gain: float32 [1536], replicated, may hold values from 0.5 to 1.5
- query_matrix: bfloat16 [1536, 1536], P(None, 'tp'), may hold values from -0.15625 to 0.15625
- key_matrix: bfloat16 [1536, 512], P(None, 'tp'), may hold values from -0.15625 to 0.15625
- value_matrix: bfloat16 [1536, 512], P(None, 'tp'), may hold values from -0.15625 to 0.15625
- out_weight: bfloat16 [1536, 1536], P('tp'), may hold values from -1.25 to 1.25
- moe_gain: float32 [1536], replicated, may hold values from 0.5 to 1.5
- router_weight: bfloat16 [1536, 40], replicated, may hold values from -0.0390625 to 0.0390625
- gate_weight: bfloat16 [40, 1536, 512], P('ep', None, 'tp'), may hold values from -0.15625 to 0.15625
- up_weight: bfloat16 [40, 1536, 512], P('ep', None, 'tp'), may hold values from -0.15625 to 0.15625
- down_weight: bfloat16 [40, 512, 1536], P('ep', 'tp'), may hold values from -2 to 2
- cotangent: bfloat16 [4096, 1536], P(('ep', 'tp')), may hold values from -6 to 6
- expert_ids: int32 [4096, 8], P(('ep', 'tp')), may hold values from 0 to 39, all different within a row; in each aligned block of 128 rows (0 to 127, 128 to 255, ...) at most 32 rows name the same one
- segments: int32 [8, 512], P('ep'), may hold values from 0 to 3, never falling along the last dimension, each value on 1 to 256 neighbouring positions
- valid_mask: int32 [8, 512], P('ep'), may hold values from 0 to 1, as said below
Outputs:
- output: bfloat16 [4096, 1536], P(('ep', 'tp'))
- input_grad: float32 [4096, 1536], P(('ep', 'tp'))
- norm_gain_grad: float32 [1536], replicated
- query_grad: float32 [1536, 1536], P(None, 'tp')
- key_grad: float32 [1536, 512], P(None, 'tp')
- value_grad: float32 [1536, 512], P(None, 'tp')
- out_grad: float32 [1536, 1536], P('tp')
- moe_gain_grad: float32 [1536], replicated
- router_grad: float32 [1536, 40], replicated
- gate_grad: float32 [40, 1536, 512], P('ep', None, 'tp')
- up_grad: float32 [40, 1536, 512], P('ep', None, 'tp')
- down_grad: float32 [40, 512, 1536], P('ep', 'tp')
Inputs may be any that keep to these rules, and one draw needn't show every extreme that they name: `expert_ids`: each row names 8 different experts. Among the 128 rows of one device (aligned blocks of 128 rows) no expert is named by more than 32 rows, a bound that some block reaches. `segments`: document numbers never fall along a sequence; each document has 1 to 256 tokens, one exactly 256. `valid_mask`: in each sequence the ones form a prefix of 384 tokens or more; the first sequence has no padding.
All inputs are finite; a program needn't handle non-finite values.
Results may differ from a plain program's by a relative error of at most 0.015.
Values may be sent and summed in bfloat16 or wider, within the bound.
No kernel may reach another device: no remote copies, remote signals or barrier semaphores. Data moves between devices by JAX's collectives and lax.ppermute only.
A program may use at most 320 MiB of HBM per device.

v0:
```python
import math

import jax
import jax.numpy as jnp
from jax import lax
from jax.sharding import PartitionSpec as P

HEAD_SIZE_DIM = 64


EPS = 1e-06
HIGH_PRECISION = lax.Precision.HIGHEST


def rms_norm(activation, gain_vec):
    factor = lax.rsqrt(jnp.mean(activation * activation, axis=-1, keepdims=True) + EPS)
    return activation * factor * gain_vec


def rotate(vectors, cos_table, sin_table):
    half_size = vectors.shape[-1] // 2
    first_half = vectors[..., :half_size]
    second_half = vectors[..., half_size:]
    return jnp.concatenate(
        [
            first_half * cos_table - second_half * sin_table,
            second_half * cos_table + first_half * sin_table,
        ],
        axis=-1,
    )


def angle_tables(span_length, head_size):
    half_size = head_size // 2
    inverse = jnp.exp(
        -math.log(10000.0) * jnp.arange(half_size, dtype=jnp.float32) * 2.0 / head_size
    )
    angles = jnp.arange(span_length, dtype=jnp.float32)[:, None] * inverse[None, :]
    return (jnp.cos(angles), jnp.sin(angles))


def swiglu(gate_val, up_val):
    return jax.nn.silu(gate_val) * up_val


def softmax_rows(logits):
    return jax.nn.softmax(logits, axis=-1)


def block_mask(segment_row, live_row, offset, height):
    span_length = segment_row.shape[0]
    key_places = jnp.arange(span_length)
    query_places = offset + jnp.arange(height)
    same_doc = segment_row[:, None] == segment_row[None, :]
    causal = key_places[None, :] <= query_places[:, None]
    usable = (live_row[None, :] > 0) | (key_places[None, :] == query_places[:, None])
    return same_doc & causal & usable


def block_scores(query_block, key_val, allowed, factor):
    scores = (
        jnp.einsum("qgrd,kgd->grqk", query_block, key_val, preferred_element_type=jnp.float32)
        * factor
    )
    return jnp.where(allowed[None, None], scores, -1e30)


def group_rows(boxes):
    return lax.all_gather(boxes, "tp", axis=0, tiled=True)


def dispatch_rows(boxes):
    return lax.all_to_all(boxes, "ep", split_axis=1, concat_axis=1, tiled=True)


def return_rows(boxes):
    return lax.all_to_all(boxes, "ep", split_axis=1, concat_axis=1, tiled=True)


def local(
    tokens,
    norm_gain,
    query_matrix,
    key_matrix,
    value_matrix,
    out_weight,
    moe_gain,
    router_weight,
    gate_weight,
    up_weight,
    down_weight,
    cotangent,
    expert_ids,
    segments,
    valid_mask,
):
    quarter = tokens.shape[0]
    width = tokens.shape[1]
    groups = lax.axis_size("tp")
    owners = lax.axis_size("ep")
    my_part = lax.axis_index("tp")
    seq_len = quarter * groups
    head_size = HEAD_SIZE_DIM
    kv_heads = key_matrix.shape[1] // head_size
    q_heads = query_matrix.shape[1] // head_size
    group_factor = q_heads // kv_heads
    local_experts = gate_weight.shape[0]
    experts_all = router_weight.shape[1]
    chosen_count = expert_ids.shape[1]
    slots = max(8, 3 * quarter * chosen_count // (2 * experts_all) // 8 * 8)
    factor = 1.0 / math.sqrt(head_size)
    segment_row = segments[0]
    live_row = valid_mask[0]
    x_float = tokens.astype(jnp.float32)
    normed = rms_norm(x_float, norm_gain).astype(jnp.bfloat16)
    normed_all = lax.all_gather(normed, "tp", axis=0, tiled=True)
    query_unrotated = jnp.dot(normed_all, query_matrix, preferred_element_type=jnp.float32).reshape(
        seq_len, kv_heads, group_factor, head_size
    )
    key_unrotated = jnp.dot(normed_all, key_matrix, preferred_element_type=jnp.float32).reshape(
        seq_len, kv_heads, head_size
    )
    value_vectors = (
        jnp.dot(normed_all, value_matrix, preferred_element_type=jnp.float32)
        .astype(jnp.bfloat16)
        .reshape(seq_len, kv_heads, head_size)
    )
    cos_table, sin_table = angle_tables(seq_len, head_size)
    cos_query = cos_table[:, None, None, :]
    sin_query = sin_table[:, None, None, :]
    cos_key = cos_table[:, None, :]
    sin_key = sin_table[:, None, :]
    query_val = rotate(query_unrotated, cos_query, sin_query).astype(jnp.bfloat16)
    key_val = rotate(key_unrotated, cos_key, sin_key).astype(jnp.bfloat16)
    height = min(512, seq_len)
    offset = 0
    allowed = block_mask(segment_row, live_row, offset, height)
    scores = block_scores(query_val, key_val, allowed, factor)
    peak = jnp.max(scores, axis=-1, keepdims=True)
    expo = jnp.exp(scores - peak)
    denom = jnp.sum(expo, axis=-1, keepdims=True)
    weights = (expo / denom).astype(jnp.bfloat16)
    mixed = jnp.einsum("grqk,kgd->qgrd", weights, value_vectors, preferred_element_type=jnp.float32)
    outputs = mixed.reshape(height, q_heads * head_size)
    log_sums = [peak + jnp.log(denom)]
    attended = outputs.astype(jnp.bfloat16)
    branch = lax.psum_scatter(
        jnp.dot(attended, out_weight, preferred_element_type=jnp.float32),
        "tp",
        scatter_dimension=0,
        tiled=True,
    )
    middle = x_float + branch
    moe_in = rms_norm(middle, moe_gain).astype(jnp.bfloat16)
    logits = jnp.dot(moe_in, router_weight, preferred_element_type=jnp.float32)
    router = softmax_rows(logits)
    my_valid = lax.dynamic_slice_in_dim(live_row, my_part * quarter, quarter, 0)
    valid_float = my_valid.astype(jnp.float32)
    picked = jnp.take_along_axis(router, expert_ids, axis=1) * valid_float[:, None]
    flat_ids = expert_ids.reshape(-1)
    flat_live = jnp.repeat(my_valid, chosen_count)
    onehot = (flat_ids[:, None] == jnp.arange(experts_all)[None, :]).astype(jnp.int32) * flat_live[
        :, None
    ]
    earlier = jnp.cumsum(onehot, axis=0) - onehot
    slot_of = jnp.sum(earlier * onehot, axis=1)
    target = jnp.where(flat_live > 0, flat_ids, experts_all)
    safe_target = jnp.minimum(target, experts_all - 1)

    def pack(row_block):
        boxes = jnp.zeros((experts_all, slots, width), jnp.bfloat16)
        boxes = boxes.at[target, slot_of].set(row_block, mode="drop")
        return boxes.reshape(1, owners, local_experts * slots, width)

    def unpack(boxes):
        flat_boxes = boxes.reshape(experts_all, slots, width)
        taken = flat_boxes[safe_target, slot_of]
        taken = jnp.where(flat_live[:, None] > 0, taken, jnp.zeros_like(taken))
        return taken.reshape(quarter, chosen_count, width)

    sent = pack(jnp.repeat(moe_in, chosen_count, axis=0))
    full_gate, full_up, full_down = (gate_weight, up_weight, down_weight)
    arrived = dispatch_rows(group_rows(sent))
    expert_rows = arrived.reshape(groups, owners, local_experts, slots, width)
    gate_val = jnp.einsum(
        "tsecd,edf->tsecf", expert_rows, gate_weight, preferred_element_type=jnp.float32
    )
    up_val = jnp.einsum(
        "tsecd,edf->tsecf", expert_rows, up_weight, preferred_element_type=jnp.float32
    )
    hidden = swiglu(gate_val, up_val).astype(jnp.bfloat16)
    result = jnp.einsum("tsecf,efd->tsecd", hidden, down_weight, preferred_element_type=jnp.float32)
    finished = lax.psum_scatter(
        result.reshape(1 * lax.axis_size("tp"), owners, local_experts * slots, width).astype(
            jnp.bfloat16
        ),
        "tp",
        scatter_dimension=0,
        tiled=True,
    )
    returned = lax.dynamic_slice_in_dim(return_rows(group_rows(finished)), my_part, 1, 0)
    result_rows = unpack(returned).astype(jnp.float32)
    output = (middle + jnp.sum(picked[:, :, None] * result_rows, axis=1)).astype(jnp.bfloat16)
    grad_out = cotangent.astype(jnp.float32)
    grad_picked = jnp.einsum("tkd,td->tk", result_rows, grad_out, precision=HIGH_PRECISION)
    onehot_float = (expert_ids[:, :, None] == jnp.arange(experts_all)[None, None, :]).astype(
        jnp.float32
    )
    grad_router = jnp.sum(onehot_float * (grad_picked * valid_float[:, None])[:, :, None], axis=1)
    _, soft_back = jax.vjp(softmax_rows, logits)
    grad_logits = soft_back(grad_router)[0]
    grad_result = (
        (picked[:, :, None] * grad_out[:, None, :])
        .astype(jnp.bfloat16)
        .reshape(quarter * chosen_count, width)
    )
    grad_sent = pack(grad_result)
    grad_arrived = dispatch_rows(group_rows(grad_sent))
    grad_rows = grad_arrived.reshape(groups, owners, local_experts, slots, width)
    gate_all = jnp.einsum(
        "tsecd,edf->tsecf", expert_rows, full_gate, preferred_element_type=jnp.float32
    )
    up_all = jnp.einsum(
        "tsecd,edf->tsecf", expert_rows, full_up, preferred_element_type=jnp.float32
    )
    hidden_all, swiglu_back = jax.vjp(swiglu, gate_all, up_all)
    hidden_low = hidden_all.astype(jnp.bfloat16)
    grad_hidden = jnp.einsum(
        "tsecd,efd->tsecf", grad_rows, full_down, preferred_element_type=jnp.float32
    )
    grad_gate_f, grad_up_f = swiglu_back(grad_hidden)
    grad_gate_rows = grad_gate_f.astype(jnp.bfloat16)
    grad_up_rows = grad_up_f.astype(jnp.bfloat16)
    down_grad = jnp.einsum(
        "tsecf,tsecd->efd", hidden_low, grad_rows, preferred_element_type=jnp.float32
    )
    gate_grad = jnp.einsum(
        "tsecd,tsecf->edf", expert_rows, grad_gate_rows, preferred_element_type=jnp.float32
    )
    up_grad = jnp.einsum(
        "tsecd,tsecf->edf", expert_rows, grad_up_rows, preferred_element_type=jnp.float32
    )
    summed = jnp.einsum(
        "tsecf,edf->tsecd", grad_gate_rows, gate_weight, preferred_element_type=jnp.float32
    )
    summed = summed + jnp.einsum(
        "tsecf,edf->tsecd", grad_up_rows, up_weight, preferred_element_type=jnp.float32
    )
    grad_finished = lax.psum_scatter(
        summed.reshape(1 * lax.axis_size("tp"), owners, local_experts * slots, width).astype(
            jnp.bfloat16
        ),
        "tp",
        scatter_dimension=0,
        tiled=True,
    )
    grad_returned = lax.dynamic_slice_in_dim(return_rows(group_rows(grad_finished)), my_part, 1, 0)
    grad_copies = unpack(grad_returned).astype(jnp.float32)
    router_float = router_weight.astype(jnp.float32)
    grad_moe_in = jnp.sum(grad_copies, axis=1) + jnp.dot(
        grad_logits, router_float.T, precision=HIGH_PRECISION
    )
    router_grad = jnp.dot(moe_in.astype(jnp.float32).T, grad_logits, precision=HIGH_PRECISION)
    _, norm_two_back = jax.vjp(rms_norm, middle, moe_gain)
    grad_mid_norm, moe_gain_grad = norm_two_back(grad_moe_in)
    grad_middle = grad_out + grad_mid_norm
    grad_branch = lax.all_gather(grad_middle.astype(jnp.bfloat16), "tp", axis=0, tiled=True)
    out_grad = jnp.einsum("sh,sd->hd", attended, grad_branch, preferred_element_type=jnp.float32)
    grad_attended = jnp.einsum(
        "sd,hd->sh", grad_branch, out_weight, preferred_element_type=jnp.float32
    ).astype(jnp.bfloat16)
    grad_attended = grad_attended.reshape(seq_len, kv_heads, group_factor, head_size)
    query_parts = []
    key_total = jnp.zeros((seq_len, kv_heads, head_size), jnp.float32)
    value_total = jnp.zeros((seq_len, kv_heads, head_size), jnp.float32)
    for block_no, offset in enumerate(range(0, seq_len, height)):
        allowed = block_mask(segment_row, live_row, offset, height)
        scores = block_scores(query_val, key_val, allowed, factor)
        probs = jnp.where(allowed[None, None], jnp.exp(scores - log_sums[block_no]), 0.0)
        grad_probs = jnp.einsum(
            "qgrd,kgd->grqk", grad_attended, value_vectors, preferred_element_type=jnp.float32
        )
        centre = jnp.sum(probs * grad_probs, axis=-1, keepdims=True)
        grad_scores = (probs * (grad_probs - centre)).astype(jnp.bfloat16)
        query_parts.append(
            jnp.einsum("grqk,kgd->qgrd", grad_scores, key_val, preferred_element_type=jnp.float32)
            * factor
        )
        key_total = (
            jnp.einsum("grqk,qgrd->kgd", grad_scores, query_val, preferred_element_type=jnp.float32)
            * factor
        )
        value_total = jnp.einsum(
            "grqk,qgrd->kgd",
            probs.astype(jnp.bfloat16),
            grad_attended,
            preferred_element_type=jnp.float32,
        )
    grad_query_rot = query_parts[0]
    _, query_back = jax.vjp(lambda vectors: rotate(vectors, cos_query, sin_query), query_unrotated)
    _, key_back = jax.vjp(lambda vectors: rotate(vectors, cos_key, sin_key), key_unrotated)
    grad_q_pre = (
        query_back(grad_query_rot)[0].astype(jnp.bfloat16).reshape(seq_len, q_heads * head_size)
    )
    grad_k_pre = key_back(key_total)[0].astype(jnp.bfloat16).reshape(seq_len, kv_heads * head_size)
    grad_value = value_total.astype(jnp.bfloat16).reshape(seq_len, kv_heads * head_size)
    query_grad = jnp.einsum("sd,sh->dh", normed_all, grad_q_pre, preferred_element_type=jnp.float32)
    key_grad = jnp.einsum("sd,sh->dh", normed_all, grad_k_pre, preferred_element_type=jnp.float32)
    value_grad = jnp.einsum("sd,sh->dh", normed_all, grad_value, preferred_element_type=jnp.float32)
    summed = jnp.einsum("sh,dh->sd", grad_q_pre, query_matrix, preferred_element_type=jnp.float32)
    summed = summed + jnp.einsum(
        "sh,dh->sd", grad_k_pre, key_matrix, preferred_element_type=jnp.float32
    )
    summed = summed + jnp.einsum(
        "sh,dh->sd", grad_value, value_matrix, preferred_element_type=jnp.float32
    )
    grad_normed = lax.psum_scatter(
        summed.astype(jnp.bfloat16), "tp", scatter_dimension=0, tiled=True
    ).astype(jnp.float32)
    _, norm_one_back = jax.vjp(rms_norm, x_float, norm_gain)
    grad_x_norm, norm_gain_grad = norm_one_back(grad_normed)
    input_grad = grad_middle + grad_x_norm
    query_grad, key_grad, value_grad, out_grad = lax.psum(
        (query_grad, key_grad, value_grad, out_grad), "ep"
    )
    norm_gain_grad, moe_gain_grad, router_grad = lax.psum(
        (norm_gain_grad, moe_gain_grad, router_grad), ("ep", "tp")
    )
    return (
        output,
        input_grad,
        norm_gain_grad,
        query_grad,
        key_grad,
        value_grad,
        out_grad,
        moe_gain_grad,
        router_grad,
        gate_grad,
        up_grad,
        down_grad,
    )


def solution(mesh):
    in_specs = (
        P(("ep", "tp"), None),
        P(),
        P(None, "tp"),
        P(None, "tp"),
        P(None, "tp"),
        P("tp", None),
        P(),
        P(),
        P("ep", None, "tp"),
        P("ep", None, "tp"),
        P("ep", "tp", None),
        P(("ep", "tp"), None),
        P(("ep", "tp"), None),
        P("ep", None),
        P("ep", None),
    )
    out_specs = (
        P(("ep", "tp"), None),
        P(("ep", "tp"), None),
        P(),
        P(None, "tp"),
        P(None, "tp"),
        P(None, "tp"),
        P("tp", None),
        P(),
        P(),
        P("ep", None, "tp"),
        P("ep", None, "tp"),
        P("ep", "tp", None),
    )
    return jax.shard_map(local, mesh=mesh, in_specs=in_specs, out_specs=out_specs, check_vma=False)
```

profile of v0, /device:TPU:0, one launch (start us, length us, event | category | flops | bytes accessed | tf_op | source)
XLA Modules:
  0.0 2429.3 jit_solution(11049751359227529653)
XLA Ops:
  13.7 20.4 all-gather.7.cloned.1.call-done
  64.9 21.6 reduce-scatter.5.cloned.1.call-done
  104.7 100.1 %all-gather.13.cloned.1.call-done = bf16[4,8,160,1536]{3,2,1,0:T(8,128)(2,1)} async-done(((bf16[1,8,160,1536]{3,2,1,0:T(8,128)(2,1)}), bf16[4,8,160,1536]{3,2,1,0:T(8,128)(2,1)}) %all-gather.13.cloned.1.call-update) | async-done | bytes 15728656 | tf_op jit(solution)/shard_map/all_gather | solution.py:69
  231.7 100.5 %all-gather.9.cloned.1.call-done = bf16[4,8,160,1536]{3,2,1,0:T(8,128)(2,1)} async-done(((bf16[1,8,160,1536]{3,2,1,0:T(8,128)(2,1)}), bf16[4,8,160,1536]{3,2,1,0:T(8,128)(2,1)}) %all-gather.9.cloned.1.call-update) | async-done | bytes 15728656 | tf_op jit(solution)/shard_map/all_gather | solution.py:69
  332.1 13.2 copy.109
  345.4 219.3 %all-to-all-done.2 = bf16[4,8,160,1536]{3,2,0,1:T(8,128)(2,1)} async-done(((bf16[4,8,160,1536]{3,2,0,1:T(8,128)(2,1)}), bf16[4,8,160,1536]{3,2,0,1:T(8,128)(2,1)}, u32[]{:S(2)}, u32[]{:S(2)}) %all-to-all-start.2) | async-done | bytes 15728672 | tf_op jit(solution)/shard_map/all_to_all | solution.py:73
  582.5 328.5 %all-to-all-done = bf16[4,8,160,1536]{3,2,0,1:T(8,128)(2,1)} async-done(((bf16[4,8,160,1536]{3,2,0,1:T(8,128)(2,1)}), bf16[4,8,160,1536]{3,2,0,1:T(8,128)(2,1)}, u32[]{:S(2)}, u32[]{:S(2)}) %all-to-all-start) | async-done | bytes 15728672 | tf_op jit(solution)/shard_map/all_to_all | solution.py:73
  942.9 13.3 copy.113
  956.3 118.0 %reduce-scatter.7.cloned.1.call-done = bf16[1,8,160,1536]{3,2,1,0:T(8,128)(2,1)} async-done(((bf16[4,8,160,1536]{3,2,1,0:T(8,128)(2,1)}), bf16[1,8,160,1536]{3,2,1,0:T(8,128)(2,1)}) %reduce-scatter.7.cloned.1.call-update) | async-done | bytes 3932176 | tf_op jit(solution)/shard_map/reduce_scatter | solution.py:193
  1074.5 18.8 fusion.39
  1093.3 18.2 fusion.8
  1111.5 13.4 copy.118
  1125.0 50.9 %all-gather.11.cloned.1.call-done = bf16[4,8,160,1536]{3,2,1,0:T(8,128)(2,1)} async-done(((bf16[1,8,160,1536]{3,2,1,0:T(8,128)(2,1)}), bf16[4,8,160,1536]{3,2,1,0:T(8,128)(2,1)}) %all-gather.11.cloned.1.call-update) | async-done | bytes 15728656 | tf_op jit(solution)/shard_map/all_gather | solution.py:69
  1175.9 13.8 copy.114
  1195.9 102.7 %reduce-scatter.9.cloned.1.call-done = bf16[1,8,160,1536]{3,2,1,0:T(8,128)(2,1)} async-done(((bf16[4,8,160,1536]{3,2,1,0:T(8,128)(2,1)}), bf16[1,8,160,1536]{3,2,1,0:T(8,128)(2,1)}) %reduce-scatter.9.cloned.1.call-update) | async-done | bytes 3932176 | tf_op jit(solution)/shard_map/reduce_scatter | solution.py:249
  1298.6 101.6 %all-gather.15.cloned.1.call-done = bf16[4,8,160,1536]{3,2,1,0:T(8,128)(2,1)} async-done(((bf16[1,8,160,1536]{3,2,1,0:T(8,128)(2,1)}), bf16[4,8,160,1536]{3,2,1,0:T(8,128)(2,1)}) %all-gather.15.cloned.1.call-update) | async-done | bytes 15728656 | tf_op jit(solution)/shard_map/all_gather | solution.py:69
  1413.3 123.5 %all-to-all-done.1 = bf16[4,8,160,1536]{3,2,0,1:T(8,128)(2,1)} async-done(((bf16[4,8,160,1536]{3,2,0,1:T(8,128)(2,1)}), bf16[4,8,160,1536]{3,2,0,1:T(8,128)(2,1)}, u32[]{:S(2)}, u32[]{:S(2)}) %all-to-all-start.1) | async-done | bytes 15728672 | tf_op jit(solution)/shard_map/all_to_all | solution.py:77
  1542.8 340.0 %all-to-all-done.3 = bf16[4,8,160,1536]{3,2,0,1:T(8,128)(2,1)} async-done(((bf16[4,8,160,1536]{3,2,0,1:T(8,128)(2,1)}), bf16[4,8,160,1536]{3,2,0,1:T(8,128)(2,1)}, u32[]{:S(2)}, u32[]{:S(2)}) %all-to-all-start.3) | async-done | bytes 15728672 | tf_op jit(solution)/shard_map/all_to_all | solution.py:77
  1890.0 23.2 gather_fusion.1
  1913.2 23.2 gather_fusion
  1949.9 69.4 %all-gather.17.cloned.1.call-done = bf16[512,1536]{1,0:T(8,128)(2,1)} async-done(((bf16[128,1536]{1,0:T(8,128)(2,1)}), bf16[512,1536]{1,0:T(8,128)(2,1)}) %all-gather.17.cloned.1.call-update) | async-done | bytes 1572880 | tf_op jit(solution)/shard_map/all_gather | solution.py:267
  2082.1 39.3 %all-reduce.4 = (f32[1536]{0:T(1024)}, f32[1536]{0:T(1024)}) all-reduce(f32[1536]{0:T(1024)S(1)} %get-tuple-element.14, f32[1536]{0:T(1024)S(1)} %get-tuple-element.12), channel_id=1, replica_groups=mesh['ep'=8,'tp'=4] {'ep','tp'}, use_global_device_ids=true, to_apply=%region_23.24 | all-reduce | flops 3072 | bytes 24576 | tf_op jit(solution)/shard_map/psum | solution.py:326
  2123.8 71.4 %all-reduce.9.cloned.1.call-done = f32[1536,40]{0,1:T(8,128)} async-done(((f32[1536,40]{0,1:T(8,128)}), f32[1536,40]{0,1:T(8,128)}) %all-reduce.9.cloned.1.call-update) | async-done | bytes 245776 | tf_op jit(solution)/shard_map/psum | solution.py:326
  2195.2 219.5 %all-reduce.11.cloned.1.call-done = (f32[1536,384]{1,0:T(8,128)}, f32[1536,128]{1,0:T(8,128)}, f32[1536,128]{1,0:T(8,128)}, f32[384,1536]{1,0:T(8,128)}) async-done(((f32[1536,384]{1,0:T(8,128)}, f32[1536,128]{1,0:T(8,128)}, f32[1536,128]{1,0:T(8,128)}, f32[384,1536]{1,0:T(8,128)}), (f32[1536,384]{1,0:T(8,128)}, f32[1536,128]{1,0:T(8,128)}, f32[1536,128]{1,0:T(8,128)}, ...) | async-done | bytes 6291472 | tf_op jit(solution)/shard_map/psum | solution.py:323
  (320 shorter events, 249.3 us)
Async XLA Ops:
  7.2 915.5 %copy-start = (bf16[5,1536,128]{2,1,0:T(8,128)(2,1)S(1)}, bf16[5,1536,128]{2,1,0:T(8,128)(2,1)}, u32[]{:S(2)}) copy-start(bf16[5,1536,128]{2,1,0:T(8,128)(2,1)} %param.24) | copy-start | bytes 5898244
  7.2 26.9 %all-gather.7.cloned.1.call-start = ((), (), s32[]{:S(2)}) async-start(), calls=%async_computation.8 | async-start | bytes 1966080 | tf_op jit(solution)/shard_map/all_gather | solution.py:116
  11.6 75.0 %reduce-scatter.5.cloned.1.call-start = ((), (), s32[]{:S(2)}) async-start(), calls=%async_computation.9 | async-start | bytes 3932160 | tf_op jit(solution)/shard_map/reduce_scatter | solution.py:147
  48.4 156.5 %all-gather.13.cloned.1.call-start = ((), (), s32[]{:S(2)}) async-start(), calls=%async_computation.13 | async-start | bytes 19660800 | tf_op jit(solution)/shard_map/all_gather | solution.py:69
  88.1 135.6 %copy-start.14 = (bf16[128,1536]{1,0:T(8,128)(2,1)}, bf16[128,1536]{1,0:T(8,128)(2,1)S(1)}, u32[]{:S(2)}) copy-start(bf16[128,1536]{1,0:T(8,128)(2,1)S(1)} %multiply_convert_fusion) | copy-start | bytes 1179652
  218.0 346.7 %all-to-all-start.2 = ((bf16[4,8,160,1536]{3,2,0,1:T(8,128)(2,1)}), bf16[4,8,160,1536]{3,2,0,1:T(8,128)(2,1)}, u32[]{:S(2)}, u32[]{:S(2)}) async-start(bf16[4,8,160,1536]{3,2,0,1:T(8,128)(2,1)} %copy.115), calls=%async_computation.4 | async-start | bytes 31457280 | tf_op jit(solution)/shard_map/all_to_all | solution.py:73
  223.6 108.5 %all-gather.9.cloned.1.call-start = ((), (), s32[]{:S(2)}) async-start(), calls=%async_computation.10 | async-start | bytes 19660800 | tf_op jit(solution)/shard_map/all_gather | solution.py:69
  564.7 346.3 %all-to-all-start = ((bf16[4,8,160,1536]{3,2,0,1:T(8,128)(2,1)}), bf16[4,8,160,1536]{3,2,0,1:T(8,128)(2,1)}, u32[]{:S(2)}, u32[]{:S(2)}) async-start(bf16[4,8,160,1536]{3,2,0,1:T(8,128)(2,1)} %copy.109), calls=%async_computation.1 | async-start | bytes 31457280 | tf_op jit(solution)/shard_map/all_to_all | solution.py:73
  570.7 503.6 %reduce-scatter.7.cloned.1.call-start = ((), (), s32[]{:S(2)}) async-start(), calls=%async_computation.11 | async-start | bytes 19660800 | tf_op jit(solution)/shard_map/reduce_scatter | solution.py:193
  956.3 118.2 %copy-start.37 = (bf16[4,8,5,32,128]{4,3,1,0,2:T(8,128)(2,1)S(1)}, bf16[4,8,5,32,128]{4,3,1,0,2:T(8,128)(2,1)}, u32[]{:S(2)}) copy-start(bf16[4,8,5,32,128]{4,3,1,0,2:T(8,128)(2,1)} %get-tuple-element.29) | copy-start | bytes 3932164
  956.3 219.6 %all-gather.11.cloned.1.call-start = ((), (), s32[]{:S(2)}) async-start(), calls=%async_computation.12 | async-start | bytes 19660800 | tf_op jit(solution)/shard_map/all_gather | solution.py:69
  1074.4 224.1 %reduce-scatter.9.cloned.1.call-start = ((), (), s32[]{:S(2)}) async-start(), calls=%async_computation.14 | async-start | bytes 19660800 | tf_op jit(solution)/shard_map/reduce_scatter | solution.py:249
  1189.7 347.2 %all-to-all-start.1 = ((bf16[4,8,160,1536]{3,2,0,1:T(8,128)(2,1)}), bf16[4,8,160,1536]{3,2,0,1:T(8,128)(2,1)}, u32[]{:S(2)}, u32[]{:S(2)}) async-start(bf16[4,8,160,1536]{3,2,0,1:T(8,128)(2,1)} %copy.114), calls=%async_computation.3 | async-start | bytes 31457280 | tf_op jit(solution)/shard_map/all_to_all | solution.py:77
  1195.8 204.4 %all-gather.15.cloned.1.call-start = ((), (), s32[]{:S(2)}) async-start(), calls=%async_computation.15 | async-start | bytes 19660800 | tf_op jit(solution)/shard_map/all_gather | solution.py:69
  1413.3 129.4 %copy-start.76 = (f32[128]{0:T(128)S(1)}, f32[128]{0:T(128)}, u32[]{:S(2)}) copy-start(f32[128]{0:T(128)} %copy-done.75) | copy-start | bytes 1540
  1536.9 345.9 %all-to-all-start.3 = ((bf16[4,8,160,1536]{3,2,0,1:T(8,128)(2,1)}), bf16[4,8,160,1536]{3,2,0,1:T(8,128)(2,1)}, u32[]{:S(2)}, u32[]{:S(2)}) async-start(bf16[4,8,160,1536]{3,2,0,1:T(8,128)(2,1)} %copy.119), calls=%async_computation.6 | async-start | bytes 31457280 | tf_op jit(solution)/shard_map/all_to_all | solution.py:77
  1542.5 476.8 %all-gather.17.cloned.1.call-start = ((), (), s32[]{:S(2)}) async-start(), calls=%async_computation.16 | async-start | bytes 1966080 | tf_op jit(solution)/shard_map/all_gather | solution.py:267
  1542.8 347.2 %copy-start.2 = (s32[1024,1]{0,1:T(1,128)S(1)}, s32[1024,1]{0,1:T(1,128)}, u32[]{:S(2)}) copy-start(s32[1024,1]{0,1:T(1,128)} %get-tuple-element.41) | copy-start | bytes 12292
  1948.5 73.5 %copy-start.12 = (f32[128,1536]{1,0:T(8,128)}, f32[128,1536]{1,0:T(8,128)S(1)}, u32[]{:S(2)}) copy-start(f32[128,1536]{1,0:T(8,128)S(1)} %get-tuple-element.51) | copy-start | bytes 2359300
  1949.6 72.4 %copy-start.17 = (pred[512,512]{0,1:T(8,128)(4,1)S(1)}, pred[512,512]{0,1:T(8,128)(4,1)}, u32[]{:S(2)}) copy-start(pred[512,512]{0,1:T(8,128)(4,1)} %copy-done.16) | copy-start | bytes 786436
  1949.6 131.1 %reduce-scatter.11.cloned.1.call-start = ((), (), s32[]{:S(2)}) async-start(), calls=%async_computation.17 | async-start | bytes 1966080 | tf_op jit(solution)/shard_map/reduce_scatter | solution.py:317
  2037.1 158.1 %all-reduce.9.cloned.1.call-start = ((), (), s32[]{:S(2)}) async-start(), calls=%async_computation.18 | async-start | bytes 491520 | tf_op jit(solution)/shard_map/psum | solution.py:326
  2038.2 376.6 %all-reduce.11.cloned.1.call-start = ((), (), s32[]{:S(2)}) async-start(), calls=%async_computation.19 | async-start | bytes 12582912 | tf_op jit(solution)/shard_map/psum | solution.py:323
  2069.8 51.6 %copy-start.8 = (f32[128,1536]{1,0:T(8,128)S(1)}, f32[128,1536]{1,0:T(8,128)}, u32[]{:S(2)}) copy-start(f32[128,1536]{1,0:T(8,128)} %copy-done.6) | copy-start | bytes 2359300
  (83 other events, 816.2 us)
Sparse Core Ops, SparseCore 0:
  11.7 22.3 all-gather.6
  48.5 38.0 reduce-scatter.4
  104.8 99.9 all-gather.12
  231.8 100.3 all-gather.8
  956.4 117.9 reduce-scatter.6
  1075.9 99.9 all-gather.10
  1178.6 119.8 reduce-scatter.8
  1300.2 99.9 all-gather.14
  1949.7 69.5 all-gather.16
  2037.2 28.1 reduce-scatter.10
  2071.5 123.6 all-reduce.8
  2200.1 214.6 all-reduce.10
where the time goes:
time: 2440 us; the launch traced here: 2430 us
  waiting for transfers between devices  1990 us (82%)
  local copies, waits for them, and re-layouts  165 us (7%)
  matrix products  151 us (6%)
  other arithmetic  45.8 us (2%)
  blocking collectives  39.3 us (2%)
  starting transfers between devices  24.8 us (1%)
    all_to_all x2, waiting for transfers between devices, dispatch_rows(): return lax.all_to_all(boxes, 'ep', split_axis=1, concat_axis=1, tiled=True)  548 us
    all_to_all x2, waiting for transfers between devices, return_rows(): return lax.all_to_all(boxes, 'ep', split_axis=1, concat_axis=1, tiled=True)  464 us
    all_gather x4, waiting for transfers between devices, group_rows(): return lax.all_gather(boxes, 'tp', axis=0, tiled=True)  353 us
    psum x1, waiting for transfers between devices, local(): lax.psum((query_grad, key_grad, value_grad, out_grad), 'ep')  220 us
    reduce_scatter x1, waiting for transfers between devices, local(): lax.psum_scatter(result.reshape(1 * lax.axis_size('tp'), owners, local_ex...  118 us
    reduce_scatter x1, waiting for transfers between devices, local(): lax.psum_scatter(summed.reshape(1 * lax.axis_size('tp'), owners, local_ex...  103 us
    psum x1, waiting for transfers between devices, local(): lax.psum((norm_gain_grad, moe_gain_grad, router_grad), ('ep', 'tp'))  71.4 us
    all_gather x1, waiting for transfers between devices, local(): lax.all_gather(grad_middle.astype(jnp.bfloat16), 'tp', axis=0, tiled=True)  69.4 us
  transfers between devices with their start and end apart: 16, of which 15 were waited for; matrix products, arithmetic and copies ran while one was open for 7% of the time, Pallas kernels for 0%

commit v1 on v0

--- a/solution.py
+++ b/solution.py
@@ -159,11 +159,11 @@
     picked = jnp.take_along_axis(router, expert_ids, axis=1) * valid_float[:, None]
     flat_ids = expert_ids.reshape(-1)
     flat_live = jnp.repeat(my_valid, chosen_count)
-    onehot = (flat_ids[:, None] == jnp.arange(experts_all)[None, :]).astype(jnp.int32) * flat_live[
-        :, None
-    ]
-    earlier = jnp.cumsum(onehot, axis=0) - onehot
-    slot_of = jnp.sum(earlier * onehot, axis=1)
+    named = (expert_ids[:, :, None] == jnp.arange(experts_all)[None, None, :]).astype(jnp.float32)
+    chosen = (jnp.sum(named, axis=1) * valid_float[:, None]).astype(jnp.bfloat16)
+    before = (jnp.arange(quarter)[None, :] < jnp.arange(quarter)[:, None]).astype(jnp.bfloat16)
+    earlier = jnp.dot(before, chosen, preferred_element_type=jnp.float32)
+    slot_of = jnp.sum(named * earlier[:, None, :], axis=2).astype(jnp.int32).reshape(-1)
     target = jnp.where(flat_live > 0, flat_ids, experts_all)
     safe_target = jnp.minimum(target, experts_all - 1)
 
@@ -180,7 +180,7 @@
 
     sent = pack(jnp.repeat(moe_in, chosen_count, axis=0))
     full_gate, full_up, full_down = (gate_weight, up_weight, down_weight)
-    arrived = dispatch_rows(group_rows(sent))
+    arrived = group_rows(dispatch_rows(sent))
     expert_rows = arrived.reshape(groups, owners, local_experts, slots, width)
     gate_val = jnp.einsum(
         "tsecd,edf->tsecf", expert_rows, gate_weight, preferred_element_type=jnp.float32
@@ -198,7 +198,7 @@
         scatter_dimension=0,
         tiled=True,
     )
-    returned = lax.dynamic_slice_in_dim(return_rows(group_rows(finished)), my_part, 1, 0)
+    returned = return_rows(finished)
     result_rows = unpack(returned).astype(jnp.float32)
     output = (middle + jnp.sum(picked[:, :, None] * result_rows, axis=1)).astype(jnp.bfloat16)
     grad_out = cotangent.astype(jnp.float32)
@@ -215,7 +215,7 @@
         .reshape(quarter * chosen_count, width)
     )
     grad_sent = pack(grad_result)
-    grad_arrived = dispatch_rows(group_rows(grad_sent))
+    grad_arrived = group_rows(dispatch_rows(grad_sent))
     grad_rows = grad_arrived.reshape(groups, owners, local_experts, slots, width)
     gate_all = jnp.einsum(
         "tsecd,edf->tsecf", expert_rows, full_gate, preferred_element_type=jnp.float32
@@ -254,7 +254,7 @@
         scatter_dimension=0,
         tiled=True,
     )
-    grad_returned = lax.dynamic_slice_in_dim(return_rows(group_rows(grad_finished)), my_part, 1, 0)
+    grad_returned = return_rows(grad_finished)
     grad_copies = unpack(grad_returned).astype(jnp.float32)
     router_float = router_weight.astype(jnp.float32)
     grad_moe_in = jnp.sum(grad_copies, axis=1) + jnp.dot(

time: 2440 us -> 1270 us (0.52)
  waiting for transfers between devices: 1990 us -> 713 us
  blocking collectives: 39.3 us -> 224 us
  local copies, waits for them, and re-layouts: 165 us -> 105 us
    all_to_all x2 -> x0, waiting for transfers between devices: 548 us -> none  [dispatch_rows(): return lax.all_to_all(boxes, 'ep', split_axis=1, concat_axis=1, tiled=True)]
    all_to_all x2, waiting for transfers between devices: 464 us -> 59.6 us  [return_rows(): return lax.all_to_all(boxes, 'ep', split_axis=1, concat_axis=1, tiled=True)]
    all_gather x4 -> x2, waiting for transfers between devices: 353 us -> 88.1 us  [group_rows(): return lax.all_gather(boxes, 'tp', axis=0, tiled=True)]
    all_to_all x0 -> x2, blocking collectives: none -> 185 us  [dispatch_rows(): return lax.all_to_all(boxes, 'ep', split_axis=1, concat_axis=1, tiled=True)]
    reduce_scatter x1, waiting for transfers between devices: 118 us -> 63.9 us  [local(): lax.psum_scatter(result.reshape(1 * lax.axis_size('tp'), owners, local_ex...]
    all_gather x4 -> x0, local copies, waits for them, and re-layouts: 53.3 us -> none  [group_rows(): return lax.all_gather(boxes, 'tp', axis=0, tiled=True)]
    all_gather x1, waiting for transfers between devices: 69.4 us -> 37.2 us  [local(): lax.all_gather(grad_middle.astype(jnp.bfloat16), 'tp', axis=0, tiled=True)]
  transfers between devices with their start and end apart: 16 -> 12, of which waited for: 15 -> 9; matrix products, arithmetic and copies ran while one was open for 7% -> 12% of each run, Pallas kernels for 0% -> 0%
where the time goes in v1:
time: 1270 us; the launch traced here: 1260 us
  waiting for transfers between devices  713 us (56%)
  blocking collectives  224 us (18%)
  matrix products  159 us (13%)
  local copies, waits for them, and re-layouts  105 us (8%)
  other arithmetic  34.4 us (3%)
  between operations  15.8 us (1%)
    psum x1, waiting for transfers between devices, local(): lax.psum((query_grad, key_grad, value_grad, out_grad), 'ep')  220 us
    all_to_all x2, blocking collectives, dispatch_rows(): return lax.all_to_all(boxes, 'ep', split_axis=1, concat_axis=1, tiled=True)  185 us
    reduce_scatter x1, waiting for transfers between devices, local(): lax.psum_scatter(summed.reshape(1 * lax.axis_size('tp'), owners, local_ex...  117 us
    all_gather x2, waiting for transfers between devices, group_rows(): return lax.all_gather(boxes, 'tp', axis=0, tiled=True)  88.1 us
    psum x1, waiting for transfers between devices, local(): lax.psum((norm_gain_grad, moe_gain_grad, router_grad), ('ep', 'tp'))  72.9 us
    reduce_scatter x1, waiting for transfers between devices, local(): lax.psum_scatter(result.reshape(1 * lax.axis_size('tp'), owners, local_ex...  63.9 us
    all_to_all x2, waiting for transfers between devices, return_rows(): return lax.all_to_all(boxes, 'ep', split_axis=1, concat_axis=1, tiled=True)  59.6 us
    gather x2, local copies, waits for them, and re-layouts, unpack(): taken = flat_boxes[safe_target, slot_of]  46.4 us
  transfers between devices with their start and end apart: 12, of which 9 were waited for; matrix products, arithmetic and copies ran while one was open for 12% of the time, Pallas kernels for 0%

profile of v1, /device:TPU:0, one launch (start us, length us, event | category | flops | bytes accessed | tf_op | source)
XLA Modules:
  0.0 1263.3 jit_solution(1700003440100462715)
XLA Ops:
  13.7 20.4 %all-gather.5.cloned.1.call-done = bf16[512,1536]{1,0:T(8,128)(2,1)} async-done(((bf16[128,1536]{1,0:T(8,128)(2,1)}), bf16[512,1536]{1,0:T(8,128)(2,1)}) %all-gather.5.cloned.1.call-update) | async-done | bytes 1572880 | tf_op jit(solution)/shard_map/all_gather | solution.py:116
  52.4 34.1 %reduce-scatter.5.cloned.1.call-done = f32[128,1536]{1,0:T(8,128)} async-done(((f32[512,1536]{1,0:T(8,128)}), f32[128,1536]{1,0:T(8,128)}) %reduce-scatter.5.cloned.1.call-update) | async-done | bytes 786448 | tf_op jit(solution)/shard_map/reduce_scatter | solution.py:147
  106.1 93.2 %all_to_all.20 = bf16[1,8,160,1536]{3,2,0,1:T(8,128)(2,1)} all-to-all(bf16[1,8,160,1536]{3,2,0,1:T(8,128)(2,1)} %bitcast.213), channel_id=1, replica_groups=mesh['ep'=8,'tp'=4] {'ep'}, dimensions={1} | all-to-all | bytes 7864320 | tf_op jit(solution)/shard_map/all_to_all | solution.py:73
  207.6 91.4 %all_to_all.21 = bf16[1,8,160,1536]{3,2,0,1:T(8,128)(2,1)} all-to-all(bf16[1,8,160,1536]{3,2,0,1:T(8,128)(2,1)} %bitcast.214), channel_id=1, replica_groups=mesh['ep'=8,'tp'=4] {'ep'}, dimensions={1} | all-to-all | bytes 7864320 | tf_op jit(solution)/shard_map/all_to_all | solution.py:73
  299.1 11.9 fusion.2
  311.0 88.0 %all-gather.7.cloned.1.call-done = bf16[4,8,160,1536]{3,2,1,0:T(8,128)(2,1)} async-done(((bf16[1,8,160,1536]{3,2,1,0:T(8,128)(2,1)}), bf16[4,8,160,1536]{3,2,1,0:T(8,128)(2,1)}) %all-gather.7.cloned.1.call-update) | async-done | bytes 15728656 | tf_op jit(solution)/shard_map/all_gather | solution.py:69
  399.0 11.7 fusion.10
  410.8 10.7 fusion.43
  421.5 11.6 convert_bitcast_fusion
  433.1 13.3 %copy.102 = bf16[4,8,5,32,1536]{4,3,2,1,0:T(8,128)(2,1)} copy(bf16[4,8,5,32,1536]{4,3,1,0,2:T(8,128)(2,1)} %convert_bitcast_fusion) | data formatting | bytes 31457280 | tf_op jit(solution)/shard_map/convert_element_type | solution.py:194
  446.8 23.2 %fusion.49 = f32[5,4,8,32,1536]{4,3,2,1,0:T(8,128)} fusion(bf16[4,8,5,32,128]{4,3,1,0,2:T(8,128)(2,1)} %get-tuple-element.27, bf16[5,1536,128]{2,1,0:T(8,128)(2,1)} %param.23), kind=kOutput, calls=%fused_computation.69 | convolution fusion | flops 2013265920 | bytes 34734080 | tf_op jit(solution)/shard_map/tsecf,edf->tsecd/dot_general | solution.py:243
  470.0 18.9 %fusion.12 = bf16[4,8,5,32,1536]{4,3,1,0,2:T(8,128)(2,1)} fusion(f32[5,4,8,32,1536]{4,3,2,1,0:T(8,128)} %fusion.49, bf16[4,8,5,32,128]{4,3,1,0,2:T(8,128)(2,1)S(1)} %copy-done.30, bf16[5,1536,128]{2,1,0:T(8,128)(2,1)S(1)} %copy-done), kind=kOutput, calls=%fused_computation.19 | convolution fusion | flops 2028994560 | bytes 50462720 | tf_op jit(solution)/shard_map/tsecf,edf->tsecd/dot_general | solution.py:246
  489.0 13.4 %copy.106 = bf16[4,8,5,32,1536]{4,3,2,1,0:T(8,128)(2,1)} copy(bf16[4,8,5,32,1536]{4,3,1,0,2:T(8,128)(2,1)} %fusion.12) | data formatting | bytes 31457280 | tf_op jit(solution)/shard_map/convert_element_type | solution.py:250
  502.4 63.9 %reduce-scatter.7.cloned.1.call-done = bf16[1,8,160,1536]{3,2,1,0:T(8,128)(2,1)} async-done(((bf16[4,8,160,1536]{3,2,1,0:T(8,128)(2,1)}), bf16[1,8,160,1536]{3,2,1,0:T(8,128)(2,1)}) %reduce-scatter.7.cloned.1.call-update) | async-done | bytes 3932176 | tf_op jit(solution)/shard_map/reduce_scatter | solution.py:193
  571.9 117.0 %reduce-scatter.9.cloned.1.call-done = bf16[1,8,160,1536]{3,2,1,0:T(8,128)(2,1)} async-done(((bf16[4,8,160,1536]{3,2,1,0:T(8,128)(2,1)}), bf16[1,8,160,1536]{3,2,1,0:T(8,128)(2,1)}) %reduce-scatter.9.cloned.1.call-update) | async-done | bytes 3932176 | tf_op jit(solution)/shard_map/reduce_scatter | solution.py:249
  694.8 23.2 %gather_fusion = bf16[1024,1536]{1,0:T(8,128)(2,1)} fusion(bf16[40,32,1536]{2,1,0:T(8,128)(2,1)} %bitcast.29, s32[1024]{0:T(1024)S(1)} %bitcast.205), kind=kCustom, calls=%fused_computation | custom fusion | bytes 6299648 | tf_op jit(solution)/shard_map/gather | solution.py:177
  722.6 59.6 %all-to-all-done.3 = bf16[1,8,160,1536]{3,2,0,1:T(8,128)(2,1)} async-done(((bf16[1,8,160,1536]{3,2,0,1:T(8,128)(2,1)}), bf16[1,8,160,1536]{3,2,0,1:T(8,128)(2,1)}, u32[]{:S(2)}, u32[]{:S(2)}) %all-to-all-start.3) | async-done | bytes 3932192 | tf_op jit(solution)/shard_map/all_to_all | solution.py:77
  782.2 23.2 %gather_fusion.1 = bf16[1024,1536]{1,0:T(8,128)(2,1)} fusion(bf16[40,32,1536]{2,1,0:T(8,128)(2,1)} %bitcast.43, s32[1024]{0:T(1024)S(1)} %bitcast.206), kind=kCustom, calls=%fused_computation.1 | custom fusion | bytes 6299648 | tf_op jit(solution)/shard_map/gather | solution.py:177
  816.1 37.2 %all-gather.11.cloned.1.call-done = bf16[512,1536]{1,0:T(8,128)(2,1)} async-done(((bf16[128,1536]{1,0:T(8,128)(2,1)}), bf16[512,1536]{1,0:T(8,128)(2,1)}) %all-gather.11.cloned.1.call-update) | async-done | bytes 1572880 | tf_op jit(solution)/shard_map/all_gather | solution.py:267
  882.9 10.1 fusion.25
  903.1 10.0 fusion.22
  914.6 39.3 %all-reduce.4 = (f32[1536]{0:T(1024)}, f32[1536]{0:T(1024)}) all-reduce(f32[1536]{0:T(1024)S(1)} %get-tuple-element.14, f32[1536]{0:T(1024)S(1)} %copy-done.61), channel_id=1, replica_groups=mesh['ep'=8,'tp'=4] {'ep','tp'}, use_global_device_ids=true, to_apply=%region_22.23 | all-reduce | flops 3072 | bytes 24576 | tf_op jit(solution)/shard_map/psum | solution.py:326
  956.3 72.9 %all-reduce.9.cloned.1.call-done = f32[1536,40]{0,1:T(8,128)} async-done(((f32[1536,40]{0,1:T(8,128)}), f32[1536,40]{0,1:T(8,128)}) %all-reduce.9.cloned.1.call-update) | async-done | bytes 245776 | tf_op jit(solution)/shard_map/psum | solution.py:326
  1029.3 219.5 %all-reduce.11.cloned.1.call-done = (f32[1536,384]{1,0:T(8,128)}, f32[1536,128]{1,0:T(8,128)}, f32[1536,128]{1,0:T(8,128)}, f32[384,1536]{1,0:T(8,128)}) async-done(((f32[1536,384]{1,0:T(8,128)}, f32[1536,128]{1,0:T(8,128)}, f32[1536,128]{1,0:T(8,128)}, f32[384,1536]{1,0:T(8,128)}), (f32[1536,384]{1,0:T(8,128)}, f32[1536,128]{1,0:T(8,128)}, f32[1536,128]{1,0:T(8,128)}, ...) | async-done | bytes 6291472 | tf_op jit(solution)/shard_map/psum | solution.py:323
  (289 shorter events, 129.6 us)
Async XLA Ops:
  7.2 403.6 %copy-start = (bf16[5,1536,128]{2,1,0:T(8,128)(2,1)S(1)}, bf16[5,1536,128]{2,1,0:T(8,128)(2,1)}, u32[]{:S(2)}) copy-start(bf16[5,1536,128]{2,1,0:T(8,128)(2,1)} %param.24) | copy-start | bytes 5898244
  7.2 26.8 %all-gather.5.cloned.1.call-start = ((), (), s32[]{:S(2)}) async-start(), calls=%async_computation.8 | async-start | bytes 1966080 | tf_op jit(solution)/shard_map/all_gather | solution.py:116
  11.5 74.9 %reduce-scatter.5.cloned.1.call-start = ((), (), s32[]{:S(2)}) async-start(), calls=%async_computation.9 | async-start | bytes 3932160 | tf_op jit(solution)/shard_map/reduce_scatter | solution.py:147
  48.4 250.7 %all-gather.9.cloned.1.call-start = ((), (), s32[]{:S(2)}) async-start(), calls=%async_computation.12 | async-start | bytes 19660800 | tf_op jit(solution)/shard_map/all_gather | solution.py:69
  87.8 726.9 %copy-start.5 = (f32[128,1536]{1,0:T(8,128)}, f32[128,1536]{1,0:T(8,128)S(1)}, u32[]{:S(2)}) copy-start(f32[128,1536]{1,0:T(8,128)S(1)} %get-tuple-element.25) | copy-start | bytes 2359300
  88.0 111.4 %copy-start.11 = (bf16[128,1536]{1,0:T(8,128)(2,1)}, bf16[128,1536]{1,0:T(8,128)(2,1)S(1)}, u32[]{:S(2)}) copy-start(bf16[128,1536]{1,0:T(8,128)(2,1)S(1)} %multiply_convert_fusion) | copy-start | bytes 1179652
  88.3 725.1 %copy-start.62 = (f32[128]{0:T(128)}, f32[128]{0:T(128)S(1)}, u32[]{:S(2)}) copy-start(f32[128]{0:T(128)S(1)} %get-tuple-element.46) | copy-start | bytes 1540
  199.3 199.7 %all-gather.7.cloned.1.call-start = ((), (), s32[]{:S(2)}) async-start(), calls=%async_computation.10 | async-start | bytes 19660800 | tf_op jit(solution)/shard_map/all_gather | solution.py:69
  299.0 267.4 %reduce-scatter.7.cloned.1.call-start = ((), (), s32[]{:S(2)}) async-start(), calls=%async_computation.11 | async-start | bytes 19660800 | tf_op jit(solution)/shard_map/reduce_scatter | solution.py:193
  446.4 242.5 %reduce-scatter.9.cloned.1.call-start = ((), (), s32[]{:S(2)}) async-start(), calls=%async_computation.13 | async-start | bytes 19660800 | tf_op jit(solution)/shard_map/reduce_scatter | solution.py:249
  566.4 122.5 %all-to-all-start.1 = ((bf16[1,8,160,1536]{3,2,0,1:T(8,128)(2,1)}), bf16[1,8,160,1536]{3,2,0,1:T(8,128)(2,1)}, u32[]{:S(2)}, u32[]{:S(2)}) async-start(bf16[1,8,160,1536]{3,2,0,1:T(8,128)(2,1)} %bitcast.216), calls=%async_computation.3 | async-start | bytes 7864320 | tf_op jit(solution)/shard_map/all_to_all | solution.py:77
  688.9 93.3 %all-to-all-start.3 = ((bf16[1,8,160,1536]{3,2,0,1:T(8,128)(2,1)}), bf16[1,8,160,1536]{3,2,0,1:T(8,128)(2,1)}, u32[]{:S(2)}, u32[]{:S(2)}) async-start(bf16[1,8,160,1536]{3,2,0,1:T(8,128)(2,1)} %bitcast.215), calls=%async_computation.6 | async-start | bytes 7864320 | tf_op jit(solution)/shard_map/all_to_all | solution.py:77
  694.6 158.7 %all-gather.11.cloned.1.call-start = ((), (), s32[]{:S(2)}) async-start(), calls=%async_computation.14 | async-start | bytes 1966080 | tf_op jit(solution)/shard_map/all_gather | solution.py:267
  722.6 90.8 %copy-start.46 = (f32[128,40]{0,1:T(8,128)}, f32[128,40]{0,1:T(8,128)S(1)}, u32[]{:S(2)}) copy-start(f32[128,40]{0,1:T(8,128)S(1)} %select_reduce_fusion) | copy-start | bytes 61444
  722.6 90.7 %copy-start.76 = (f32[128]{0:T(128)}, f32[128]{0:T(128)S(1)}, u32[]{:S(2)}) copy-start(f32[128]{0:T(128)S(1)} %neg.19) | copy-start | bytes 1540
  815.7 97.4 %reduce-scatter.11.cloned.1.call-start = ((), (), s32[]{:S(2)}) async-start(), calls=%async_computation.15 | async-start | bytes 1966080 | tf_op jit(solution)/shard_map/reduce_scatter | solution.py:317
  871.1 158.2 %all-reduce.9.cloned.1.call-start = ((), (), s32[]{:S(2)}) async-start(), calls=%async_computation.16 | async-start | bytes 491520 | tf_op jit(solution)/shard_map/psum | solution.py:326
  872.2 376.6 %all-reduce.11.cloned.1.call-start = ((), (), s32[]{:S(2)}) async-start(), calls=%async_computation.17 | async-start | bytes 12582912 | tf_op jit(solution)/shard_map/psum | solution.py:323
  903.0 50.8 %copy-start.80 = (f32[128]{0:T(128)S(1)}, f32[128]{0:T(128)}, u32[]{:S(2)}) copy-start(f32[128]{0:T(128)} %copy-done.79) | copy-start | bytes 1540
  903.1 50.8 %copy-start.6 = (f32[128,1536]{1,0:T(8,128)S(1)}, f32[128,1536]{1,0:T(8,128)}, u32[]{:S(2)}) copy-start(f32[128,1536]{1,0:T(8,128)} %copy-done.5) | copy-start | bytes 2359300
  903.1 50.8 %copy-start.10 = (f32[128,1536]{1,0:T(8,128)S(1)}, f32[128,1536]{1,0:T(8,128)}, u32[]{:S(2)}) copy-start(f32[128,1536]{1,0:T(8,128)} %copy-done.9) | copy-start | bytes 2359300
  903.1 50.8 %copy-start.17 = (bf16[128,1536]{1,0:T(8,128)(2,1)S(1)}, bf16[128,1536]{1,0:T(8,128)(2,1)}, u32[]{:S(2)}) copy-start(bf16[128,1536]{1,0:T(8,128)(2,1)} %param.26) | copy-start | bytes 1179652
  903.1 50.8 %copy-start.20 = (f32[128,1536]{1,0:T(8,128)S(1)}, f32[128,1536]{1,0:T(8,128)}, u32[]{:S(2)}) copy-start(f32[128,1536]{1,0:T(8,128)} %get-tuple-element.17) | copy-start | bytes 2359300
  903.1 50.8 %copy-start.55 = (f32[1536]{0:T(1024)S(1)}, f32[1536]{0:T(1024)}, u32[]{:S(2)}) copy-start(f32[1536]{0:T(1024)} %param.21) | copy-start | bytes 18436
  (75 other events, 639.3 us)
Sparse Core Ops, SparseCore 0:
  11.6 22.3 all-gather.4
  48.5 37.9 reduce-scatter.4
  199.5 98.0 all-gather.8
  299.2 99.8 all-gather.6
  446.5 119.8 reduce-scatter.6
  569.0 119.8 reduce-scatter.8
  815.9 37.3 all-gather.10
  871.2 28.1 reduce-scatter.10
  905.5 123.7 all-reduce.8
  1034.1 214.6 all-reduce.10

commit v2 on v1

--- a/solution.py
+++ b/solution.py
@@ -3,6 +3,8 @@
 import jax
 import jax.numpy as jnp
 from jax import lax
+from jax.experimental import pallas as pl
+from jax.experimental.pallas import tpu as pltpu
 from jax.sharding import PartitionSpec as P
 
 HEAD_SIZE_DIM = 64
@@ -75,6 +77,556 @@
 
 def return_rows(boxes):
     return lax.all_to_all(boxes, "ep", split_axis=1, concat_axis=1, tiled=True)
+
+
+def swap_core(value):
+    return lax.ppermute(value, "tp", [(i, i ^ 1) for i in range(4)])
+
+
+def swap_x(value):
+    return lax.ppermute(value, "tp", [(i, i ^ 2) for i in range(4)])
+
+
+def swap_y(value):
+    owners = lax.axis_size("ep")
+    return lax.ppermute(value, "ep", [(i, i ^ 1) for i in range(owners)])
+
+
+def shift_z(value, step):
+    owners = lax.axis_size("ep")
+    return lax.ppermute(value, "ep", [(i, (i + 2 * step) % owners) for i in range(owners)])
+
+
+def gather_tp(value):
+    if lax.axis_size("tp") != 4:
+        return lax.all_gather(value, "tp", axis=0, tiled=True)
+    me = lax.axis_index("tp")
+    other = swap_core(value)
+    across = swap_x(value)
+    across_other = swap_core(across)
+    rows = value.shape[0]
+    full = jnp.zeros((4 * rows,) + value.shape[1:], value.dtype)
+    for part, flip in ((value, 0), (other, 1), (across, 2), (across_other, 3)):
+        full = lax.dynamic_update_slice_in_dim(full, part, (me ^ flip) * rows, 0)
+    return full
+
+
+def scatter_tp(value, core_dtype):
+    if lax.axis_size("tp") != 4:
+        return lax.psum_scatter(value, "tp", scatter_dimension=0, tiled=True).astype(jnp.float32)
+    me = lax.axis_index("tp")
+    core, across = me % 2, me // 2
+    boxes = value.reshape((2, 2, value.shape[0] // 4) + value.shape[1:])
+    leave = lax.dynamic_index_in_dim(boxes, 1 - core, 1, keepdims=False).astype(core_dtype)
+    stay = lax.dynamic_index_in_dim(boxes, core, 1, keepdims=False)
+    both = stay.astype(jnp.float32) + swap_core(leave).astype(jnp.float32)
+    mine = lax.dynamic_index_in_dim(both, across, 0, keepdims=False)
+    theirs = lax.dynamic_index_in_dim(both, 1 - across, 0, keepdims=False)
+    return mine + swap_x(theirs.astype(jnp.bfloat16)).astype(jnp.float32)
+
+
+def gather_column(value):
+    half = value.shape[0] // 2
+    across = swap_x(value)
+    along = swap_y(value)
+    first = swap_y(across[:half])
+    last = swap_x(along[half:])
+    pieces = (value, across, along, first, last)
+    return pieces + tuple(swap_core(piece) for piece in pieces)
+
+
+def gather_planes(value):
+    planes = lax.axis_size("ep") // 2
+    chunks = [gather_column(value)]
+    for _ in range(1, planes):
+        value = shift_z(value, 1)
+        chunks.append(gather_column(value))
+    return chunks
+
+
+def add_low(left, right):
+    return (left.astype(jnp.float32) + right.astype(jnp.float32)).astype(jnp.bfloat16)
+
+
+def reduce_plane(own_core, other_core, step):
+    size = own_core.shape[0] // 4
+    arrived = swap_core(other_core)
+    part = lambda i: add_low(own_core[i * size : (i + 1) * size], arrived[i * size : (i + 1) * size])
+    from_x = swap_x(part(2))
+    from_y = swap_y(part(3))
+    first = add_low(part(0), from_x)
+    last = add_low(part(1), from_y)
+    half = size // 2
+    first_sum = add_low(first[:half], swap_y(first[half:]))
+    last_sum = add_low(last[:half], swap_x(last[half:]))
+    total = jnp.concatenate([first_sum, last_sum], axis=0)
+    return shift_z(total, -step) if step else total
+
+
+def butterfly_sum(value):
+    value = value + swap_core(value)
+    value = value + swap_x(value)
+    value = value + swap_y(value)
+    total = value
+    for step in range(1, lax.axis_size("ep") // 2):
+        total = total + shift_z(value, step)
+    return total
+
+
+FIRST_HALF = (0, 4, 1, 5)
+LAST_HALF = (2, 3, 6, 7)
+NT = (((1,), (1,)), ((), ()))
+TN = (((0,), (0,)), ((), ()))
+
+
+def dot_f32(left, right, dims=None):
+    if dims is None:
+        return jnp.dot(left, right, preferred_element_type=jnp.float32)
+    return lax.dot_general(left, right, dims, preferred_element_type=jnp.float32)
+
+
+def pick(index, table):
+    out = table[0]
+    for i in range(1, len(table)):
+        out = jnp.where(index == i, table[i], out)
+    return out
+
+
+def expert_kernel(sizes, *refs):
+    experts, slots, blocks, rows, routed = sizes
+    x_parts, g_parts = refs[:10], refs[10:20]
+    slot_ref, router_ref, gate_ref, up_ref, down_ref = refs[20:25]
+    own_ref, other_ref, xr_out, gr_out, dgu_ref, wh_ref, rg_ref = refs[25:32]
+    xs, gs, xr, gr, wgu, wd, back, picks, probs, weight, d_weight = refs[32:43]
+    x_sem, g_sem, w_sem, out_sem = refs[43:47]
+    units = wd.shape[1]
+    half = rows // 2
+    total = experts * slots
+    depth = blocks * slots
+    starts = []
+    for parts, scratch, sem in ((x_parts, xs, x_sem), (g_parts, gs, g_sem)):
+        for i, part in enumerate(parts):
+            side, place = i // 5, i % 5
+            block = side * 4 + min(place, 3)
+            offset = block * rows + (half if place == 4 else 0)
+            starts.append((part, scratch.at[pl.ds(offset, part.shape[0])], sem.at[block]))
+    for source, target, sem in starts[:10]:
+        pltpu.make_async_copy(source, target, sem).start()
+    for source, target, sem in starts[10:]:
+        pltpu.make_async_copy(source, target, sem).start()
+    for e in range(experts):
+        pltpu.make_async_copy(gate_ref.at[e], wgu.at[e, :, pl.ds(0, units)], w_sem.at[0, e]).start()
+        pltpu.make_async_copy(up_ref.at[e], wgu.at[e, :, pl.ds(units, units)], w_sem.at[1, e]).start()
+        pltpu.make_async_copy(down_ref.at[e], wd.at[e], w_sem.at[2, e]).start()
+    rg_ref[...] = jnp.zeros_like(rg_ref)
+
+    def block_rows(b):
+        return pl.ds(pl.multiple_of(b * rows, rows), rows)
+
+    def slot_rows(b):
+        return pl.ds(pl.multiple_of(b * slots, slots), slots)
+
+    def expand(table):
+        return jnp.concatenate(
+            [jnp.broadcast_to(table[e : e + 1, :], (slots, rows)) for e in range(experts)], axis=0
+        )
+
+    place = jnp.concatenate(
+        [lax.broadcasted_iota(jnp.int32, (slots, rows), 0)] * experts, axis=0
+    ).astype(jnp.float32)
+
+    def gather_x(b, carry):
+        pltpu.make_async_copy(xs.at[block_rows(b)], xs.at[block_rows(b)], x_sem.at[b]).wait()
+        x_block = xs[block_rows(b), :]
+        logits = dot_f32(router_ref[...], x_block, NT)
+        lane = lax.broadcasted_iota(jnp.int32, logits.shape, 0)
+        logits = jnp.where(lane < routed, logits, -1e30)
+        expo = jnp.exp(logits - jnp.max(logits, axis=0, keepdims=True))
+        prob = expo / jnp.sum(expo, axis=0, keepdims=True)
+        probs[b] = prob
+        hit = expand(slot_ref[b]) == place
+        chosen = jnp.sum(jnp.where(hit, expand(prob), 0.0), axis=1, keepdims=True)
+        chosen = jnp.broadcast_to(chosen, (total, rows))
+        one = hit.astype(jnp.float32).astype(jnp.bfloat16)
+        picks[b] = one
+        taken = dot_f32(one, x_block).astype(jnp.bfloat16)
+        for e in range(experts):
+            xr[e, slot_rows(b), :] = taken[e * slots : (e + 1) * slots]
+            weight[e, slot_rows(b), :] = chosen[e * slots : (e + 1) * slots]
+        back[b, pl.ds(total, router_ref.shape[0]), :] = router_ref[...]
+        return carry
+
+    def gather_g(b, carry):
+        pltpu.make_async_copy(gs.at[block_rows(b)], gs.at[block_rows(b)], g_sem.at[b]).wait()
+        taken = dot_f32(picks[b], gs[block_rows(b), :]).astype(jnp.bfloat16)
+        for e in range(experts):
+            gr[e, slot_rows(b), :] = taken[e * slots : (e + 1) * slots]
+        return carry
+
+    lax.fori_loop(0, blocks, gather_x, 0)
+    pltpu.make_async_copy(xr, xr_out, out_sem.at[0]).start()
+    lax.fori_loop(0, blocks, gather_g, 0)
+    pltpu.make_async_copy(gr, gr_out, out_sem.at[1]).start()
+
+    def one_expert(e, carry):
+        pltpu.make_async_copy(wgu.at[e, :, pl.ds(0, units)], wgu.at[e, :, pl.ds(0, units)], w_sem.at[0, e]).wait()
+        pltpu.make_async_copy(wgu.at[e, :, pl.ds(units, units)], wgu.at[e, :, pl.ds(units, units)], w_sem.at[1, e]).wait()
+        pltpu.make_async_copy(wd.at[e], wd.at[e], w_sem.at[2, e]).wait()
+        both = dot_f32(xr[e], wgu[e])
+        gate, up = both[:, :units], both[:, units:]
+        back_hidden = dot_f32(gr[e], wd[e], NT)
+        sig = 1.0 / (1.0 + jnp.exp(-gate))
+        silu = gate * sig
+        hidden = silu * up
+        d_weight[e] = jnp.broadcast_to(
+            jnp.sum(hidden.astype(jnp.bfloat16).astype(jnp.float32) * back_hidden, axis=1, keepdims=True),
+            (depth, rows),
+        )
+        share = weight[e]
+        d_hidden = share * back_hidden
+        d_gate = d_hidden * up * (sig * (1.0 + gate * (1.0 - sig)))
+        d_up = d_hidden * silu
+        d_both = jnp.concatenate([d_gate, d_up], axis=1).astype(jnp.bfloat16)
+        dgu_ref[e] = d_both
+        wh_ref[e] = (share * hidden).astype(jnp.bfloat16)
+        d_rows = dot_f32(d_both, wgu[e], NT).astype(jnp.bfloat16)
+        for b in range(blocks):
+            back[b, pl.ds(pl.multiple_of(e * slots, slots), slots), :] = d_rows[b * slots : (b + 1) * slots]
+        return carry
+
+    lax.fori_loop(0, experts, one_expert, 0)
+
+    def scatter(b, carry):
+        one = picks[b]
+        d_slot = jnp.concatenate([d_weight[e, slot_rows(b), :] for e in range(experts)], axis=0)
+        spread = one.astype(jnp.float32) * d_slot
+        d_prob = jnp.concatenate(
+            [jnp.sum(spread[e * slots : (e + 1) * slots], axis=0, keepdims=True) for e in range(experts)]
+            + [jnp.zeros((router_ref.shape[0] - experts, rows), jnp.float32)],
+            axis=0,
+        )
+        prob = probs[b]
+        centre = jnp.sum(prob * d_prob, axis=0, keepdims=True)
+        d_logits = (prob * (d_prob - centre)).astype(jnp.bfloat16)
+        rg_ref[...] += dot_f32(d_logits, xs[block_rows(b), :])
+        result = dot_f32(jnp.concatenate([one, d_logits], axis=0), back[b], TN).astype(jnp.bfloat16)
+        kind = b % 4
+        first = pl.ds(pl.multiple_of(pick(kind, FIRST_HALF) * half, half), half)
+        last = pl.ds(pl.multiple_of(pick(kind, LAST_HALF) * half, half), half)
+
+        @pl.when(b < 4)
+        def _():
+            own_ref[first, :] = result[:half]
+            own_ref[last, :] = result[half:]
+
+        @pl.when(b >= 4)
+        def _():
+            other_ref[first, :] = result[:half]
+            other_ref[last, :] = result[half:]
+
+        return carry
+
+    lax.fori_loop(0, blocks, scatter, 0)
+    pltpu.make_async_copy(xr, xr_out, out_sem.at[0]).wait()
+    pltpu.make_async_copy(gr, gr_out, out_sem.at[1]).wait()
+
+
+def expert_call(x_parts, g_parts, slot, router_rows, gate_weight, up_weight, down_weight, routed, slots):
+    blocks = 8
+    rows, width = x_parts[0].shape
+    experts, _, units = gate_weight.shape
+    depth = blocks * slots
+    padded = router_rows.shape[0]
+    low, full = jnp.bfloat16, jnp.float32
+    any_spec = pl.BlockSpec(memory_space=pl.ANY)
+    vmem_spec = pl.BlockSpec(memory_space=pltpu.VMEM)
+    return pl.pallas_call(
+        lambda *refs: expert_kernel((experts, slots, blocks, rows, routed), *refs),
+        out_shape=(
+            jax.ShapeDtypeStruct((4 * rows, width), low),
+            jax.ShapeDtypeStruct((4 * rows, width), low),
+            jax.ShapeDtypeStruct((experts, depth, width), low),
+            jax.ShapeDtypeStruct((experts, depth, width), low),
+            jax.ShapeDtypeStruct((experts, depth, 2 * units), low),
+            jax.ShapeDtypeStruct((experts, depth, units), low),
+            jax.ShapeDtypeStruct((padded, width), full),
+        ),
+        in_specs=[any_spec] * 20 + [vmem_spec] * 2 + [any_spec] * 3,
+        out_specs=(vmem_spec, vmem_spec, any_spec, any_spec, vmem_spec, vmem_spec, vmem_spec),
+        scratch_shapes=[
+            pltpu.VMEM((blocks * rows, width), low),
+            pltpu.VMEM((blocks * rows, width), low),
+            pltpu.VMEM((experts, depth, width), low),
+            pltpu.VMEM((experts, depth, width), low),
+            pltpu.VMEM((experts, width, 2 * units), low),
+            pltpu.VMEM((experts, units, width), low),
+            pltpu.VMEM((blocks, experts * slots + padded, width), low),
+            pltpu.VMEM((blocks, experts * slots, rows), low),
+            pltpu.VMEM((blocks, padded, rows), full),
+            pltpu.VMEM((experts, depth, rows), full),
+            pltpu.VMEM((experts, depth, rows), full),
+            pltpu.SemaphoreType.DMA((blocks,)),
+            pltpu.SemaphoreType.DMA((blocks,)),
+            pltpu.SemaphoreType.DMA((3, experts)),
+            pltpu.SemaphoreType.DMA((2,)),
+        ],
+        compiler_params=pltpu.CompilerParams(vmem_limit_bytes=50 * 2**20),
+        cost_estimate=pl.CostEstimate(
+            flops=2 * experts * depth * width * units * 5, bytes_accessed=24 * 2**20, transcendentals=0
+        ),
+        name="expert_chunk",
+    )(*x_parts, *g_parts, slot, router_rows, gate_weight, up_weight, down_weight)
+
+
+def output_kernel(sizes, wh_ref, slot_ref, down_ref, own_ref, other_ref, rows_ref):
+    experts, slots, blocks, rows = sizes
+    half = rows // 2
+
+    def one_expert(e, carry):
+        result = dot_f32(wh_ref[e], down_ref[e]).astype(jnp.bfloat16)
+        for b in range(blocks):
+            rows_ref[b, pl.ds(pl.multiple_of(e * slots, slots), slots), :] = result[b * slots : (b + 1) * slots]
+        return carry
+
+    lax.fori_loop(0, experts, one_expert, 0)
+    place = lax.broadcasted_iota(jnp.int32, (slots, rows), 0).astype(jnp.float32)
+
+    def scatter(b, carry):
+        table = slot_ref[b]
+        one = jnp.concatenate(
+            [(table[e : e + 1, :] == place).astype(jnp.float32) for e in range(experts)], axis=0
+        ).astype(jnp.bfloat16)
+        result = dot_f32(one, rows_ref[b], TN).astype(jnp.bfloat16)
+        kind = b % 4
+        first = pl.ds(pl.multiple_of(pick(kind, FIRST_HALF) * half, half), half)
+        last = pl.ds(pl.multiple_of(pick(kind, LAST_HALF) * half, half), half)
+
+        @pl.when(b < 4)
+        def _():
+            own_ref[first, :] = result[:half]
+            own_ref[last, :] = result[half:]
+
+        @pl.when(b >= 4)
+        def _():
+            other_ref[first, :] = result[:half]
+            other_ref[last, :] = result[half:]
+
+        return carry
+
+    lax.fori_loop(0, blocks, scatter, 0)
+
+
+def output_call(weighted, slot, down_weight, slots):
+    experts, depth, units = weighted.shape
+    width = down_weight.shape[2]
+    blocks, _, rows = slot.shape
+    vmem_spec = pl.BlockSpec(memory_space=pltpu.VMEM)
+    return pl.pallas_call(
+        lambda *refs: output_kernel((experts, slots, blocks, rows), *refs),
+        out_shape=(jax.ShapeDtypeStruct((4 * rows, width), jnp.bfloat16),) * 2,
+        in_specs=[vmem_spec] * 3,
+        out_specs=(vmem_spec,) * 2,
+        scratch_shapes=[pltpu.VMEM((blocks, experts * slots, width), jnp.bfloat16)],
+        compiler_params=pltpu.CompilerParams(vmem_limit_bytes=40 * 2**20),
+        cost_estimate=pl.CostEstimate(
+            flops=2 * experts * depth * width * units * 3, bytes_accessed=6 * 2**20, transcendentals=0
+        ),
+        name="output_chunk",
+    )(weighted, slot, down_weight)
+
+
+def weight_kernel(count, *refs):
+    xr, gr, dgu, wh = (refs[i * count : (i + 1) * count] for i in range(4))
+    gate_ref, up_ref, down_ref = refs[4 * count :]
+    units = gate_ref.shape[2]
+    both = sum(dot_f32(x[0], d[0], TN) for x, d in zip(xr, dgu))
+    gate_ref[0] = both[:, :units]
+    up_ref[0] = both[:, units:]
+    down_ref[0] = sum(dot_f32(h[0], g[0], TN) for h, g in zip(wh, gr))
+
+
+def weight_call(xr, gr, dgu, wh):
+    count = len(xr)
+    experts, depth, width = xr[0].shape
+    units = wh[0].shape[2]
+    spec = lambda array: pl.BlockSpec((1,) + array.shape[1:], lambda e: (e, 0, 0))
+    operands = [*xr, *gr, *dgu, *wh]
+    up_like = jax.ShapeDtypeStruct((experts, width, units), jnp.float32)
+    down_like = jax.ShapeDtypeStruct((experts, units, width), jnp.float32)
+    return pl.pallas_call(
+        lambda *refs: weight_kernel(count, *refs),
+        grid=(experts,),
+        out_shape=(up_like, up_like, down_like),
+        in_specs=[spec(a) for a in operands],
+        out_specs=(spec(up_like), spec(up_like), spec(down_like)),
+        compiler_params=pltpu.CompilerParams(vmem_limit_bytes=50 * 2**20),
+        cost_estimate=pl.CostEstimate(
+            flops=2 * experts * depth * count * width * units * 3,
+            bytes_accessed=45 * 2**20,
+            transcendentals=0,
+        ),
+        name="expert_weights",
+    )(*operands)
+
+
+def gathered_experts(
+    moe_in, router_weight, gate_weight, up_weight, down_weight, cotangent, expert_ids, my_valid, slots
+):
+    rows = moe_in.shape[0]
+    local_experts = gate_weight.shape[0]
+    experts_all = router_weight.shape[1]
+    owner = lax.axis_index("ep")
+    planes = lax.axis_size("ep") // 2
+    ids = jnp.where(my_valid[:, None] > 0, expert_ids, -1).T[None]
+    for swap in (swap_x, swap_y, swap_core):
+        ids = jnp.concatenate([ids, swap(ids)], axis=0)
+    ids = jnp.stack([ids] + [shift_z(ids, step) for step in range(1, planes)])
+    mine = owner * local_experts + jnp.arange(local_experts)
+    named = jnp.any(ids[:, :, None] == mine[None, None, :, None, None], axis=-2)
+    before = (jnp.arange(rows)[:, None] < jnp.arange(rows)[None, :]).astype(jnp.bfloat16)
+    earlier = jnp.dot(named.astype(jnp.bfloat16), before, preferred_element_type=jnp.float32)
+    slot = jnp.where(named, earlier, -1.0)
+    slot = jnp.pad(slot, ((0, 0), (0, 0), (0, -local_experts % 8), (0, 0)), constant_values=-1.0)
+    padded = -(-experts_all // 16) * 16
+    router_rows = jnp.roll(router_weight.T, -owner * local_experts, axis=0)
+    router_rows = jnp.pad(router_rows, ((0, padded - experts_all), (0, 0)))
+    g_chunks = gather_planes(cotangent)
+    x_chunks = gather_planes(moe_in)
+    kept, d_input = [], 0.0
+    for i in range(planes):
+        own, other, *rest = expert_call(
+            x_chunks[i], g_chunks[i], slot[i], router_rows, gate_weight, up_weight, down_weight, experts_all, slots
+        )
+        kept.append(rest)
+        d_input = d_input + reduce_plane(own, other, i).astype(jnp.float32)
+    xr, gr, dgu, wh, router_parts = zip(*kept)
+    expert_sum = 0.0
+    for i in range(planes):
+        own, other = output_call(wh[i], slot[i], down_weight, slots)
+        expert_sum = expert_sum + reduce_plane(own, other, i).astype(jnp.float32)
+    gate_grad, up_grad, down_grad = weight_call(xr, gr, dgu, wh)
+    router_part = jnp.roll(sum(router_parts)[:experts_all], owner * local_experts, axis=0)
+    return expert_sum, d_input, router_part, gate_grad, up_grad, down_grad
+
+
+def routed_experts(
+    moe_in, router_weight, gate_weight, up_weight, down_weight, cotangent, expert_ids, my_valid, slots
+):
+    quarter, width = moe_in.shape
+    owners, groups = lax.axis_size("ep"), lax.axis_size("tp")
+    local_experts = gate_weight.shape[0]
+    experts_all = router_weight.shape[1]
+    chosen_count = expert_ids.shape[1]
+    logits = jnp.dot(moe_in, router_weight, preferred_element_type=jnp.float32)
+    router = softmax_rows(logits)
+    valid_float = my_valid.astype(jnp.float32)
+    picked = jnp.take_along_axis(router, expert_ids, axis=1) * valid_float[:, None]
+    flat_ids = expert_ids.reshape(-1)
+    flat_live = jnp.repeat(my_valid, chosen_count)
+    named = (expert_ids[:, :, None] == jnp.arange(experts_all)[None, None, :]).astype(jnp.float32)
+    chosen = (jnp.sum(named, axis=1) * valid_float[:, None]).astype(jnp.bfloat16)
+    before = (jnp.arange(quarter)[None, :] < jnp.arange(quarter)[:, None]).astype(jnp.bfloat16)
+    earlier = jnp.dot(before, chosen, preferred_element_type=jnp.float32)
+    slot_of = jnp.sum(named * earlier[:, None, :], axis=2).astype(jnp.int32).reshape(-1)
+    target = jnp.where(flat_live > 0, flat_ids, experts_all)
+    safe_target = jnp.minimum(target, experts_all - 1)
+
+    def pack(row_block):
+        boxes = jnp.zeros((experts_all, slots, width), jnp.bfloat16)
+        boxes = boxes.at[target, slot_of].set(row_block, mode="drop")
+        return boxes.reshape(1, owners, local_experts * slots, width)
+
+    def unpack(boxes):
+        flat_boxes = boxes.reshape(experts_all, slots, width)
+        taken = flat_boxes[safe_target, slot_of]
+        taken = jnp.where(flat_live[:, None] > 0, taken, jnp.zeros_like(taken))
+        return taken.reshape(quarter, chosen_count, width)
+
+    sent = pack(jnp.repeat(moe_in, chosen_count, axis=0))
+    arrived = group_rows(dispatch_rows(sent))
+    expert_rows = arrived.reshape(groups, owners, local_experts, slots, width)
+    gate_val = jnp.einsum(
+        "tsecd,edf->tsecf", expert_rows, gate_weight, preferred_element_type=jnp.float32
+    )
+    up_val = jnp.einsum(
+        "tsecd,edf->tsecf", expert_rows, up_weight, preferred_element_type=jnp.float32
+    )
+    hidden = swiglu(gate_val, up_val).astype(jnp.bfloat16)
+    result = jnp.einsum("tsecf,efd->tsecd", hidden, down_weight, preferred_element_type=jnp.float32)
+    finished = lax.psum_scatter(
+        result.reshape(1 * lax.axis_size("tp"), owners, local_experts * slots, width).astype(
+            jnp.bfloat16
+        ),
+        "tp",
+        scatter_dimension=0,
+        tiled=True,
+    )
+    returned = return_rows(finished)
+    result_rows = unpack(returned).astype(jnp.float32)
+    expert_sum = jnp.sum(picked[:, :, None] * result_rows, axis=1)
+    grad_out = cotangent.astype(jnp.float32)
+    grad_picked = jnp.einsum("tkd,td->tk", result_rows, grad_out, precision=HIGH_PRECISION)
+    onehot_float = (expert_ids[:, :, None] == jnp.arange(experts_all)[None, None, :]).astype(
+        jnp.float32
+    )
+    grad_router = jnp.sum(onehot_float * (grad_picked * valid_float[:, None])[:, :, None], axis=1)
+    _, soft_back = jax.vjp(softmax_rows, logits)
+    grad_logits = soft_back(grad_router)[0]
+    grad_result = (
+        (picked[:, :, None] * grad_out[:, None, :])
+        .astype(jnp.bfloat16)
+        .reshape(quarter * chosen_count, width)
+    )
+    grad_sent = pack(grad_result)
+    grad_arrived = group_rows(dispatch_rows(grad_sent))
+    grad_rows = grad_arrived.reshape(groups, owners, local_experts, slots, width)
+    gate_all = jnp.einsum(
+        "tsecd,edf->tsecf", expert_rows, gate_weight, preferred_element_type=jnp.float32
+    )
+    up_all = jnp.einsum(
+        "tsecd,edf->tsecf", expert_rows, up_weight, preferred_element_type=jnp.float32
+    )
+    hidden_all, swiglu_back = jax.vjp(swiglu, gate_all, up_all)
+    hidden_low = hidden_all.astype(jnp.bfloat16)
+    grad_hidden = jnp.einsum(
+        "tsecd,efd->tsecf", grad_rows, down_weight, preferred_element_type=jnp.float32
+    )
+    grad_gate_f, grad_up_f = swiglu_back(grad_hidden)
+    grad_gate_rows = grad_gate_f.astype(jnp.bfloat16)
+    grad_up_rows = grad_up_f.astype(jnp.bfloat16)
+    down_grad = jnp.einsum(
+        "tsecf,tsecd->efd", hidden_low, grad_rows, preferred_element_type=jnp.float32
+    )
+    gate_grad = jnp.einsum(
+        "tsecd,tsecf->edf", expert_rows, grad_gate_rows, preferred_element_type=jnp.float32
+    )
+    up_grad = jnp.einsum(
+        "tsecd,tsecf->edf", expert_rows, grad_up_rows, preferred_element_type=jnp.float32
+    )
+    summed = jnp.einsum(
+        "tsecf,edf->tsecd", grad_gate_rows, gate_weight, preferred_element_type=jnp.float32
+    )
+    summed = summed + jnp.einsum(
+        "tsecf,edf->tsecd", grad_up_rows, up_weight, preferred_element_type=jnp.float32
+    )
+    grad_finished = lax.psum_scatter(
+        summed.reshape(1 * lax.axis_size("tp"), owners, local_experts * slots, width).astype(
+            jnp.bfloat16
+        ),
+        "tp",
+        scatter_dimension=0,
+        tiled=True,
+    )
+    grad_returned = return_rows(grad_finished)
+    grad_copies = unpack(grad_returned).astype(jnp.float32)
+    router_float = router_weight.astype(jnp.float32)
+    grad_moe_in = jnp.sum(grad_copies, axis=1) + jnp.dot(
+        grad_logits, router_float.T, precision=HIGH_PRECISION
+    )
+    router_part = jnp.dot(
+        grad_logits.T, moe_in.astype(jnp.float32), precision=HIGH_PRECISION
+    )
+    return expert_sum, grad_moe_in, router_part, gate_grad, up_grad, down_grad
 
 
 def local(
@@ -113,7 +665,7 @@
     live_row = valid_mask[0]
     x_float = tokens.astype(jnp.float32)
     normed = rms_norm(x_float, norm_gain).astype(jnp.bfloat16)
-    normed_all = lax.all_gather(normed, "tp", axis=0, tiled=True)
+    normed_all = gather_tp(normed)
     query_unrotated = jnp.dot(normed_all, query_matrix, preferred_element_type=jnp.float32).reshape(
         seq_len, kv_heads, group_factor, head_size
     )
@@ -144,127 +696,27 @@
     outputs = mixed.reshape(height, q_heads * head_size)
     log_sums = [peak + jnp.log(denom)]
     attended = outputs.astype(jnp.bfloat16)
-    branch = lax.psum_scatter(
-        jnp.dot(attended, out_weight, preferred_element_type=jnp.float32),
-        "tp",
-        scatter_dimension=0,
-        tiled=True,
+    branch = scatter_tp(
+        jnp.dot(attended, out_weight, preferred_element_type=jnp.float32), jnp.float32
     )
     middle = x_float + branch
     moe_in = rms_norm(middle, moe_gain).astype(jnp.bfloat16)
-    logits = jnp.dot(moe_in, router_weight, preferred_element_type=jnp.float32)
-    router = softmax_rows(logits)
     my_valid = lax.dynamic_slice_in_dim(live_row, my_part * quarter, quarter, 0)
-    valid_float = my_valid.astype(jnp.float32)
-    picked = jnp.take_along_axis(router, expert_ids, axis=1) * valid_float[:, None]
-    flat_ids = expert_ids.reshape(-1)
-    flat_live = jnp.repeat(my_valid, chosen_count)
-    named = (expert_ids[:, :, None] == jnp.arange(experts_all)[None, None, :]).astype(jnp.float32)
-    chosen = (jnp.sum(named, axis=1) * valid_float[:, None]).astype(jnp.bfloat16)
-    before = (jnp.arange(quarter)[None, :] < jnp.arange(quarter)[:, None]).astype(jnp.bfloat16)
-    earlier = jnp.dot(before, chosen, preferred_element_type=jnp.float32)
-    slot_of = jnp.sum(named * earlier[:, None, :], axis=2).astype(jnp.int32).reshape(-1)
-    target = jnp.where(flat_live > 0, flat_ids, experts_all)
-    safe_target = jnp.minimum(target, experts_all - 1)
-
-    def pack(row_block):
-        boxes = jnp.zeros((experts_all, slots, width), jnp.bfloat16)
-        boxes = boxes.at[target, slot_of].set(row_block, mode="drop")
-        return boxes.reshape(1, owners, local_experts * slots, width)
-
-    def unpack(boxes):
-        flat_boxes = boxes.reshape(experts_all, slots, width)
-        taken = flat_boxes[safe_target, slot_of]
-        taken = jnp.where(flat_live[:, None] > 0, taken, jnp.zeros_like(taken))
-        return taken.reshape(quarter, chosen_count, width)
-
-    sent = pack(jnp.repeat(moe_in, chosen_count, axis=0))
-    full_gate, full_up, full_down = (gate_weight, up_weight, down_weight)
-    arrived = group_rows(dispatch_rows(sent))
-    expert_rows = arrived.reshape(groups, owners, local_experts, slots, width)
-    gate_val = jnp.einsum(
-        "tsecd,edf->tsecf", expert_rows, gate_weight, preferred_element_type=jnp.float32
-    )
-    up_val = jnp.einsum(
-        "tsecd,edf->tsecf", expert_rows, up_weight, preferred_element_type=jnp.float32
-    )
-    hidden = swiglu(gate_val, up_val).astype(jnp.bfloat16)
-    result = jnp.einsum("tsecf,efd->tsecd", hidden, down_weight, preferred_element_type=jnp.float32)
-    finished = lax.psum_scatter(
-        result.reshape(1 * lax.axis_size("tp"), owners, local_experts * slots, width).astype(
-            jnp.bfloat16
-        ),
-        "tp",
-        scatter_dimension=0,
-        tiled=True,
-    )
-    returned = return_rows(finished)
-    result_rows = unpack(returned).astype(jnp.float32)
-    output = (middle + jnp.sum(picked[:, :, None] * result_rows, axis=1)).astype(jnp.bfloat16)
+    gathers = groups == 4 and owners % 2 == 0 and local_experts * slots >= quarter
+    if gathers:
+        expert_sum, grad_moe_in, router_part, gate_grad, up_grad, down_grad = gathered_experts(
+            moe_in, router_weight, gate_weight, up_weight, down_weight, cotangent, expert_ids, my_valid, slots
+        )
+    else:
+        expert_sum, grad_moe_in, router_part, gate_grad, up_grad, down_grad = routed_experts(
+            moe_in, router_weight, gate_weight, up_weight, down_weight, cotangent, expert_ids, my_valid, slots
+        )
     grad_out = cotangent.astype(jnp.float32)
-    grad_picked = jnp.einsum("tkd,td->tk", result_rows, grad_out, precision=HIGH_PRECISION)
-    onehot_float = (expert_ids[:, :, None] == jnp.arange(experts_all)[None, None, :]).astype(
-        jnp.float32
-    )
-    grad_router = jnp.sum(onehot_float * (grad_picked * valid_float[:, None])[:, :, None], axis=1)
-    _, soft_back = jax.vjp(softmax_rows, logits)
-    grad_logits = soft_back(grad_router)[0]
-    grad_result = (
-        (picked[:, :, None] * grad_out[:, None, :])
-        .astype(jnp.bfloat16)
-        .reshape(quarter * chosen_count, width)
-    )
-    grad_sent = pack(grad_result)
-    grad_arrived = group_rows(dispatch_rows(grad_sent))
-    grad_rows = grad_arrived.reshape(groups, owners, local_experts, slots, width)
-    gate_all = jnp.einsum(
-        "tsecd,edf->tsecf", expert_rows, full_gate, preferred_element_type=jnp.float32
-    )
-    up_all = jnp.einsum(
-        "tsecd,edf->tsecf", expert_rows, full_up, preferred_element_type=jnp.float32
-    )
-    hidden_all, swiglu_back = jax.vjp(swiglu, gate_all, up_all)
-    hidden_low = hidden_all.astype(jnp.bfloat16)
-    grad_hidden = jnp.einsum(
-        "tsecd,efd->tsecf", grad_rows, full_down, preferred_element_type=jnp.float32
-    )
-    grad_gate_f, grad_up_f = swiglu_back(grad_hidden)
-    grad_gate_rows = grad_gate_f.astype(jnp.bfloat16)
-    grad_up_rows = grad_up_f.astype(jnp.bfloat16)
-    down_grad = jnp.einsum(
-        "tsecf,tsecd->efd", hidden_low, grad_rows, preferred_element_type=jnp.float32
-    )
-    gate_grad = jnp.einsum(
-        "tsecd,tsecf->edf", expert_rows, grad_gate_rows, preferred_element_type=jnp.float32
-    )
-    up_grad = jnp.einsum(
-        "tsecd,tsecf->edf", expert_rows, grad_up_rows, preferred_element_type=jnp.float32
-    )
-    summed = jnp.einsum(
-        "tsecf,edf->tsecd", grad_gate_rows, gate_weight, preferred_element_type=jnp.float32
-    )
-    summed = summed + jnp.einsum(
-        "tsecf,edf->tsecd", grad_up_rows, up_weight, preferred_element_type=jnp.float32
-    )
-    grad_finished = lax.psum_scatter(
-        summed.reshape(1 * lax.axis_size("tp"), owners, local_experts * slots, width).astype(
-            jnp.bfloat16
-        ),
-        "tp",
-        scatter_dimension=0,
-        tiled=True,
-    )
-    grad_returned = return_rows(grad_finished)
-    grad_copies = unpack(grad_returned).astype(jnp.float32)
-    router_float = router_weight.astype(jnp.float32)
-    grad_moe_in = jnp.sum(grad_copies, axis=1) + jnp.dot(
-        grad_logits, router_float.T, precision=HIGH_PRECISION
-    )
-    router_grad = jnp.dot(moe_in.astype(jnp.float32).T, grad_logits, precision=HIGH_PRECISION)
+    output = (middle + expert_sum).astype(jnp.bfloat16)
     _, norm_two_back = jax.vjp(rms_norm, middle, moe_gain)
     grad_mid_norm, moe_gain_grad = norm_two_back(grad_moe_in)
     grad_middle = grad_out + grad_mid_norm
-    grad_branch = lax.all_gather(grad_middle.astype(jnp.bfloat16), "tp", axis=0, tiled=True)
+    grad_branch = gather_tp(grad_middle.astype(jnp.bfloat16))
     out_grad = jnp.einsum("sh,sd->hd", attended, grad_branch, preferred_element_type=jnp.float32)
     grad_attended = jnp.einsum(
         "sd,hd->sh", grad_branch, out_weight, preferred_element_type=jnp.float32
@@ -314,18 +766,24 @@
     summed = summed + jnp.einsum(
         "sh,dh->sd", grad_value, value_matrix, preferred_element_type=jnp.float32
     )
-    grad_normed = lax.psum_scatter(
-        summed.astype(jnp.bfloat16), "tp", scatter_dimension=0, tiled=True
-    ).astype(jnp.float32)
+    grad_normed = scatter_tp(summed, jnp.bfloat16)
     _, norm_one_back = jax.vjp(rms_norm, x_float, norm_gain)
     grad_x_norm, norm_gain_grad = norm_one_back(grad_normed)
     input_grad = grad_middle + grad_x_norm
-    query_grad, key_grad, value_grad, out_grad = lax.psum(
-        (query_grad, key_grad, value_grad, out_grad), "ep"
-    )
-    norm_gain_grad, moe_gain_grad, router_grad = lax.psum(
-        (norm_gain_grad, moe_gain_grad, router_grad), ("ep", "tp")
-    )
+    weights = jnp.concatenate(
+        [part.astype(jnp.bfloat16) for part in (query_grad, key_grad, value_grad)], axis=1
+    )
+    weights = lax.psum(weights, "ep").astype(jnp.float32)
+    query_grad, key_grad, value_grad = jnp.split(
+        weights, (query_grad.shape[1], query_grad.shape[1] + key_grad.shape[1]), axis=1
+    )
+    out_grad = lax.psum(out_grad.astype(jnp.bfloat16), "ep").astype(jnp.float32)
+    small = jnp.concatenate([router_part, moe_gain_grad[None]], axis=0)
+    if gathers:
+        small, norm_gain_grad = butterfly_sum(small), butterfly_sum(norm_gain_grad[None])[0]
+    else:
+        small, norm_gain_grad = lax.psum((small, norm_gain_grad), ("ep", "tp"))
+    router_grad, moe_gain_grad = small[:experts_all].T, small[experts_all]
     return (
         output,
         input_grad,

time: 1270 us -> 741 us (0.58)
  waiting for transfers between devices: 713 us -> 381 us
  blocking collectives: 224 us -> 0 us
  matrix products: 159 us -> 19.2 us
  Pallas kernels: 0 us -> 111 us
  starting transfers between devices: 12.6 us -> 111 us
  local copies, waits for them, and re-layouts: 105 us -> 43.2 us
  other arithmetic: 34.4 us -> 50.8 us
    ppermute x0 -> x152, waiting for transfers between devices: none -> 276 us  [the longest x39 113 us: swap_x(): return lax.ppermute(value, 'tp', [(i, i ^ 2) for i in range(4)])]
    reduce_scatter x4 -> x0, waiting for transfers between devices: 215 us -> none  [the longest x1 117 us: local(): lax.psum_scatter(summed.reshape(1 * lax.axis_size('tp'), owners, local_ex...]
    psum x2 -> x1, waiting for transfers between devices: 292 us -> 104 us  [local(): weights = lax.psum(weights, 'ep').astype(jnp.float32)]
    all_to_all x2 -> x0, blocking collectives: 185 us -> none  [dispatch_rows(): return lax.all_to_all(boxes, 'ep', split_axis=1, concat_axis=1, tiled=True)]
    all_gather x4 -> x0, waiting for transfers between devices: 146 us -> none  [the longest x2 88.1 us: group_rows(): return lax.all_gather(boxes, 'tp', axis=0, tiled=True)]
    dot_general x14 -> x1, matrix products: 125 us -> 0.15 us  [gathered_experts(): jnp.dot(named.astype(jnp.bfloat16), before, preferred_element_type=jnp.fl...]
    pallas_call x0 -> x9, Pallas kernels: none -> 111 us  [the longest x4 73.2 us: expert_call(): pl.pallas_call(lambda *refs: expert_kernel((experts, slots, blocks, rows,...]
    ppermute x0 -> x152, starting transfers between devices: none -> 111 us  [the longest x39 41.6 us: swap_x(): return lax.ppermute(value, 'tp', [(i, i ^ 2) for i in range(4)])]
  transfers between devices with their start and end apart: 12 -> 153, of which waited for: 9 -> 62; matrix products, arithmetic and copies ran while one was open for 12% -> 10% of each run, Pallas kernels for 0% -> 15%
where the time goes in v2:
time: 741 us; the launch traced here: 732 us
  waiting for transfers between devices  381 us (51%)
  starting transfers between devices  111 us (15%)
  Pallas kernels  111 us (15%)
  other arithmetic  50.8 us (7%)
  local copies, waits for them, and re-layouts  43.2 us (6%)
  matrix products  19.2 us (3%)
  between operations  16.9 us (2%)
    ppermute x39, waiting for transfers between devices, swap_x(): return lax.ppermute(value, 'tp', [(i, i ^ 2) for i in range(4)])  113 us
    psum x1, waiting for transfers between devices, local(): weights = lax.psum(weights, 'ep').astype(jnp.float32)  104 us
    ppermute x35, waiting for transfers between devices, swap_y(): return lax.ppermute(value, 'ep', [(i, i ^ 1) for i in range(owners)])  104 us
    pallas_call x4, Pallas kernels, expert_call(): pl.pallas_call(lambda *refs: expert_kernel((experts, slots, blocks, rows,...  73.2 us
    ppermute x21, waiting for transfers between devices, shift_z(): lax.ppermute(value, 'ep', [(i, (i + 2 * step) % owners) for i in range(ow...  57.1 us
    ppermute x39, starting transfers between devices, swap_x(): return lax.ppermute(value, 'tp', [(i, i ^ 2) for i in range(4)])  41.6 us
    ppermute x35, starting transfers between devices, swap_y(): return lax.ppermute(value, 'ep', [(i, i ^ 1) for i in range(owners)])  33.5 us
    ppermute x21, starting transfers between devices, shift_z(): lax.ppermute(value, 'ep', [(i, (i + 2 * step) % owners) for i in range(ow...  25.8 us
  transfers between devices with their start and end apart: 153, of which 62 were waited for; matrix products, arithmetic and copies ran while one was open for 10% of the time, Pallas kernels for 15%

profile of v2, /device:TPU:0, one launch (start us, length us, event | category | flops | bytes accessed | tf_op | source)
XLA Modules:
  0.0 732.2 jit_solution(17206381601451355784)
XLA Ops:
  13.3 9.4 %collective-permute-done.1 = bf16[128,1536]{1,0:T(8,128)(2,1)} collective-permute-done((bf16[128,1536]{1,0:T(8,128)(2,1)}, bf16[128,1536]{1,0:T(8,128)(2,1)}, u32[]{:S(2)}, u32[]{:S(2)}) %collective-permute-start.1) | collective-permute-done | bytes 393248 | tf_op jit(solution)/shard_map/ppermute | solution.py:87
  63.3 10.0 %collective-permute-done.26 = s32[8,8,128]{2,1,0:T(8,128)S(1)} collective-permute-done((s32[8,8,128]{2,1,0:T(8,128)S(1)}, s32[8,8,128]{2,1,0:T(8,128)S(1)}, u32[]{:S(2)}, u32[]{:S(2)}) %collective-permute-start.26) | collective-permute-done | bytes 32800 | tf_op jit(solution)/shard_map/ppermute | solution.py:97
  101.6 7.2 collective-permute-done.97.refs_11_
  139.4 6.8 collective-permute-done.34.refs_0_
  173.3 9.1 %collective-permute-done.37.refs_3_ = bf16[64,1536]{1,0:T(8,128)(2,1)S(1)} collective-permute-done((bf16[64,1536]{1,0:T(8,128)(2,1)S(1)}, bf16[64,1536]{1,0:T(8,128)(2,1)S(1)}, u32[]{:S(2)}, u32[]{:S(2)}) %collective-permute-start.37) | collective-permute-done | bytes 196640 | tf_op jit(solution)/shard_map/ppermute | solution.py:92
  196.2 18.0 %expert_chunk.4 = (bf16[512,1536]{1,0:T(8,128)(2,1)}, bf16[512,1536]{1,0:T(8,128)(2,1)}, bf16[5,256,1536]{2,1,0:T(8,128)(2,1)}, bf16[5,256,1536]{2,1,0:T(8,128)(...) custom-call(bf16[128,1536]{1,0:T(8,128)(2,1)S(1)} %multiply_convert_fusion.refs_0_, ...), custom_call_target="tpu_custom_call" | custom-call | flops 2516582400 | bytes 25165824 | tf_op jit(solution)/shard_map/expert_chunk/pallas_call | solution.py:343
  224.1 18.5 %expert_chunk.5 = (bf16[512,1536]{1,0:T(8,128)(2,1)}, bf16[512,1536]{1,0:T(8,128)(2,1)}, bf16[5,256,1536]{2,1,0:T(8,128)(2,1)}, bf16[5,256,1536]{2,1,0:T(8,128)(...) custom-call(bf16[128,1536]{1,0:T(8,128)(2,1)} %collective-permute-done.34.refs_0_, ...), custom_call_target="tpu_custom_call" | custom-call | flops 2516582400 | bytes 25165824 | tf_op jit(solution)/shard_map/expert_chunk/pallas_call | solution.py:343
  249.3 18.3 %expert_chunk.6 = (bf16[512,1536]{1,0:T(8,128)(2,1)}, bf16[512,1536]{1,0:T(8,128)(2,1)}, bf16[5,256,1536]{2,1,0:T(8,128)(2,1)}, bf16[5,256,1536]{2,1,0:T(8,128)(...) custom-call(bf16[128,1536]{1,0:T(8,128)(2,1)} %collective-permute-done.60.refs_0_, ...), custom_call_target="tpu_custom_call" | custom-call | flops 2516582400 | bytes 25165824 | tf_op jit(solution)/shard_map/expert_chunk/pallas_call | solution.py:343
  273.7 18.5 %expert_chunk.7 = (bf16[512,1536]{1,0:T(8,128)(2,1)}, bf16[512,1536]{1,0:T(8,128)(2,1)}, bf16[5,256,1536]{2,1,0:T(8,128)(2,1)}, bf16[5,256,1536]{2,1,0:T(8,128)(...) custom-call(bf16[128,1536]{1,0:T(8,128)(2,1)} %collective-permute-done.86.refs_0_, ...), custom_call_target="tpu_custom_call" | custom-call | flops 2516582400 | bytes 25165824 | tf_op jit(solution)/shard_map/expert_chunk/pallas_call | solution.py:343
  294.6 17.7 %expert_weights.1 = (f32[5,1536,128]{2,1,0:T(8,128)}, f32[5,1536,128]{2,1,0:T(8,128)}, f32[5,128,1536]{2,1,0:T(8,128)}) custom-call(bf16[5,256,1536]{2,1,0:T(8,128)(2,1)} %get-tuple-element.75.refs_0_, bf16[5,256,1536]{2,1,0:T(8,128)(2,1)} %get-tuple-element.76.refs_1_, bf16[5,256,1536]{2,1,0:T(8,128)(2,1)} %get-tuple-element.77.refs_2_, ...), custom_call_target="tpu_custom_call" | custom-call | flops 6039797760 | bytes 47185920 | tf_op jit(solution)/shard_map/expert_weights/pallas_call | solution.py:456
  320.1 9.7 %collective-permute-done.113 = bf16[128,1536]{1,0:T(8,128)(2,1)S(1)} collective-permute-done((bf16[128,1536]{1,0:T(8,128)(2,1)S(1)}, bf16[128,1536]{1,0:T(8,128)(2,1)S(1)}, u32[]{:S(2)}, u32[]{:S(2)}) %collective-permute-start.113) | collective-permute-done | bytes 393248 | tf_op jit(solution)/shard_map/ppermute | solution.py:87
  333.1 9.7 %collective-permute-done.30 = bf16[128,1536]{1,0:T(8,128)(2,1)S(1)} collective-permute-done((bf16[128,1536]{1,0:T(8,128)(2,1)S(1)}, bf16[128,1536]{1,0:T(8,128)(2,1)S(1)}, u32[]{:S(2)}, u32[]{:S(2)}) %collective-permute-start.30) | collective-permute-done | bytes 393248 | tf_op jit(solution)/shard_map/ppermute | solution.py:87
  359.4 8.6 %collective-permute-done.118 = bf16[128,1536]{1,0:T(8,128)(2,1)S(1)} collective-permute-done((bf16[128,1536]{1,0:T(8,128)(2,1)S(1)}, bf16[128,1536]{1,0:T(8,128)(2,1)S(1)}, u32[]{:S(2)}, u32[]{:S(2)}) %collective-permute-start.118) | collective-permute-done | bytes 393248 | tf_op jit(solution)/shard_map/ppermute | solution.py:87
  370.2 6.6 collective-permute-done.115
  392.8 7.2 collective-permute-done.119
  411.9 7.2 collective-permute-done.33
  464.1 9.1 %collective-permute-done.131 = bf16[64,1536]{1,0:T(8,128)(2,1)S(1)} collective-permute-done((bf16[64,1536]{1,0:T(8,128)(2,1)S(1)}, bf16[64,1536]{1,0:T(8,128)(2,1)S(1)}, u32[]{:S(2)}, u32[]{:S(2)}) %collective-permute-start.131) | collective-permute-done | bytes 196640 | tf_op jit(solution)/shard_map/ppermute | solution.py:92
  475.5 7.7 %collective-permute-done.108 = bf16[64,1536]{1,0:T(8,128)(2,1)S(1)} collective-permute-done((bf16[64,1536]{1,0:T(8,128)(2,1)S(1)}, bf16[64,1536]{1,0:T(8,128)(2,1)S(1)}, u32[]{:S(2)}, u32[]{:S(2)}) %collective-permute-start.108) | collective-permute-done | bytes 196640 | tf_op jit(solution)/shard_map/ppermute | solution.py:92
  483.7 7.2 collective-permute-done.84
  501.5 14.7 %collective-permute-done.128 = bf16[128,1536]{1,0:T(8,128)(2,1)S(1)} collective-permute-done((bf16[128,1536]{1,0:T(8,128)(2,1)S(1)}, bf16[128,1536]{1,0:T(8,128)(2,1)S(1)}, u32[]{:S(2)}, u32[]{:S(2)}) %collective-permute-start.128) | collective-permute-done | bytes 393248 | tf_op jit(solution)/shard_map/ppermute | solution.py:97
  521.4 8.9 %collective-permute-done.136 = bf16[128,1536]{1,0:T(8,128)(2,1)S(1)} collective-permute-done((bf16[128,1536]{1,0:T(8,128)(2,1)S(1)}, bf16[128,1536]{1,0:T(8,128)(2,1)S(1)}, u32[]{:S(2)}, u32[]{:S(2)}) %collective-permute-start.136) | collective-permute-done | bytes 393248 | tf_op jit(solution)/shard_map/ppermute | solution.py:87
  537.4 7.5 %collective-permute-done.148 = f32[41,1536]{1,0:T(8,128)S(1)} collective-permute-done((f32[41,1536]{1,0:T(8,128)S(1)}, f32[41,1536]{1,0:T(8,128)S(1)}, u32[]{:S(2)}, u32[]{:S(2)}) %collective-permute-start.148) | collective-permute-done | bytes 251936 | tf_op jit(solution)/shard_map/ppermute | solution.py:92
  580.4 9.8 %collective-permute-done.149 = f32[41,1536]{1,0:T(8,128)S(1)} collective-permute-done((f32[41,1536]{1,0:T(8,128)}, f32[41,1536]{1,0:T(8,128)S(1)}, u32[]{:S(2)}, u32[]{:S(2)}) %collective-permute-start.149) | collective-permute-done | bytes 251936 | tf_op jit(solution)/shard_map/ppermute | solution.py:97
  610.4 104.4 %all-reduce.9.cloned.1.call-done = (bf16[1536,640]{0,1:T(8,128)(2,1)}, bf16[384,1536]{1,0:T(8,128)(2,1)}) async-done(((bf16[1536,640]{0,1:T(8,128)(2,1)}, bf16[384,1536]{1,0:T(8,128)(2,1)}), (bf16[1536,640]{0,1:T(8,128)(2,1)}, bf16[384,1536]{1,0:T(8,128)(2,1)})) %all-reduce.9.cloned.1.call-update) | async-done | bytes 3145744 | tf_op jit(solution)/shard_map/psum | solution.py:776
  (777 shorter events, 363.5 us)
Async XLA Ops:
  7.2 707.5 %all-reduce.9.cloned.1.call-start = ((), (), s32[]{:S(2)}) async-start(), calls=%async_computation | async-start | bytes 6291456 | tf_op jit(solution)/shard_map/psum | solution.py:776
  36.0 45.9 %collective-permute-start.3 = (f32[2,128,1536]{2,1,0:T(8,128)}, f32[2,128,1536]{2,1,0:T(8,128)}, u32[]{:S(2)}, u32[]{:S(2)}) collective-permute-start(f32[2,128,1536]{2,1,0:T(8,128)} %dynamic-slice_bitcast_fusion), channel_id=1, source_target_pairs={{0,1},{1,0},{2,3},{3,2},{4,5},{5,4},{6,7},{7,6},{8,9},{9,8},{10,11... | collective-permute-start | bytes 4718600 | tf_op jit(solution)/shard_map/ppermute | solution.py:83
  185.3 37.3 %collective-permute-start.66 = (bf16[128,1536]{1,0:T(8,128)(2,1)}, bf16[128,1536]{1,0:T(8,128)(2,1)S(1)}, u32[]{:S(2)}, u32[]{:S(2)}) collective-permute-start(bf16[128,1536]{1,0:T(8,128)(2,1)} %collective-permute-done.61.refs_1_), channel_id=1, source_target_pairs={{0,1},{1,0},{2,3},{3,2},{4,5},{5,4},{6,7},{7,6},{8,9},{9,8},{10,11... | collective-permute-start | bytes 1179656 | tf_op jit(solution)/shard_map/ppermute | solution.py:83
  190.4 31.1 %collective-permute-start.43 = (bf16[64,1536]{1,0:T(8,128)(2,1)S(1)}, bf16[64,1536]{1,0:T(8,128)(2,1)S(1)}, u32[]{:S(2)}, u32[]{:S(2)}) collective-permute-start(bf16[64,1536]{1,0:T(8,128)(2,1)S(1)} %collective-permute-done.38.refs_4_), channel_id=1, source_target_pairs={{0,1},{1,0},{2,3},{3,2},{4,5},{5,4},{6,7},{7,6},{8,9},{9,8},{10,11... | collective-permute-start | bytes 589832 | tf_op jit(solution)/shard_map/ppermute | solution.py:83
  190.5 30.3 %collective-permute-start.63 = (bf16[64,1536]{1,0:T(8,128)(2,1)}, bf16[64,1536]{1,0:T(8,128)(2,1)S(1)}, u32[]{:S(2)}, u32[]{:S(2)}) collective-permute-start(bf16[64,1536]{1,0:T(8,128)(2,1)} %slice.524), channel_id=1, source_target_pairs={{0,4},{4,0},{8,12},{12,8},{16,20},{20,16},{24,28},{28,24},{1,5},{5... | collective-permute-start | bytes 589832 | tf_op jit(solution)/shard_map/ppermute | solution.py:92
  196.2 46.4 %collective-permute-start.67 = (bf16[128,1536]{1,0:T(8,128)(2,1)}, bf16[128,1536]{1,0:T(8,128)(2,1)}, u32[]{:S(2)}, u32[]{:S(2)}) collective-permute-start(bf16[128,1536]{1,0:T(8,128)(2,1)} %collective-permute-done.62.refs_2_), channel_id=1, source_target_pairs={{0,1},{1,0},{2,3},{3,2},{4,5},{5,4},{6,7},{7,6},{8,9},{9,8},{10,11... | collective-permute-start | bytes 1179656 | tf_op jit(solution)/shard_map/ppermute | solution.py:83
  272.1 44.9 %collective-permute-start.112 = (bf16[512,1536]{1,0:T(8,128)(2,1)}, bf16[512,1536]{1,0:T(8,128)(2,1)}, u32[]{:S(2)}, u32[]{:S(2)}) collective-permute-start(bf16[512,1536]{1,0:T(8,128)(2,1)} %get-tuple-element.64), channel_id=1, source_target_pairs={{0,1},{1,0},{2,3},{3,2},{4,5},{5,4},{6,7},{7,6},{8,9},{9,8},{10,11... | collective-permute-start | bytes 4718600 | tf_op jit(solution)/shard_map/ppermute | solution.py:83
  272.6 45.8 %collective-permute-start.29 = (bf16[512,1536]{1,0:T(8,128)(2,1)}, bf16[512,1536]{1,0:T(8,128)(2,1)}, u32[]{:S(2)}, u32[]{:S(2)}) collective-permute-start(bf16[512,1536]{1,0:T(8,128)(2,1)} %get-tuple-element.53), channel_id=1, source_target_pairs={{0,1},{1,0},{2,3},{3,2},{4,5},{5,4},{6,7},{7,6},{8,9},{9,8},{10,11... | collective-permute-start | bytes 4718600 | tf_op jit(solution)/shard_map/ppermute | solution.py:83
  272.7 58.6 %collective-permute-start.117 = (bf16[512,1536]{1,0:T(8,128)(2,1)}, bf16[512,1536]{1,0:T(8,128)(2,1)}, u32[]{:S(2)}, u32[]{:S(2)}) collective-permute-start(bf16[512,1536]{1,0:T(8,128)(2,1)} %get-tuple-element.66), channel_id=1, source_target_pairs={{0,1},{1,0},{2,3},{3,2},{4,5},{5,4},{6,7},{7,6},{8,9},{9,8},{10,11... | collective-permute-start | bytes 4718600 | tf_op jit(solution)/shard_map/ppermute | solution.py:83
  273.1 71.0 %collective-permute-start.54 = (bf16[512,1536]{1,0:T(8,128)(2,1)}, bf16[512,1536]{1,0:T(8,128)(2,1)}, u32[]{:S(2)}, u32[]{:S(2)}) collective-permute-start(bf16[512,1536]{1,0:T(8,128)(2,1)} %get-tuple-element.56), channel_id=1, source_target_pairs={{0,1},{1,0},{2,3},{3,2},{4,5},{5,4},{6,7},{7,6},{8,9},{9,8},{10,11... | collective-permute-start | bytes 4718600 | tf_op jit(solution)/shard_map/ppermute | solution.py:83
  273.2 105.4 %collective-permute-start.123 = (bf16[512,1536]{1,0:T(8,128)(2,1)}, bf16[512,1536]{1,0:T(8,128)(2,1)}, u32[]{:S(2)}, u32[]{:S(2)}) collective-permute-start(bf16[512,1536]{1,0:T(8,128)(2,1)} %get-tuple-element.68), channel_id=1, source_target_pairs={{0,1},{1,0},{2,3},{3,2},{4,5},{5,4},{6,7},{7,6},{8,9},{9,8},{10,11... | collective-permute-start | bytes 4718600 | tf_op jit(solution)/shard_map/ppermute | solution.py:83
  317.0 74.4 %collective-permute-start.80 = (bf16[512,1536]{1,0:T(8,128)(2,1)S(1)}, bf16[512,1536]{1,0:T(8,128)(2,1)S(1)}, u32[]{:S(2)}, u32[]{:S(2)}) collective-permute-start(bf16[512,1536]{1,0:T(8,128)(2,1)S(1)} %copy-done.48), channel_id=1, source_target_pairs={{0,1},{1,0},{2,3},{3,2},{4,5},{5,4},{6,7},{7,6},{8,9},{9,8},{10,11... | collective-permute-start | bytes 4718600 | tf_op jit(solution)/shard_map/ppermute | solution.py:83
  329.8 90.6 %collective-permute-start.129 = (bf16[512,1536]{1,0:T(8,128)(2,1)S(1)}, bf16[512,1536]{1,0:T(8,128)(2,1)S(1)}, u32[]{:S(2)}, u32[]{:S(2)}) collective-permute-start(bf16[512,1536]{1,0:T(8,128)(2,1)S(1)} %copy-done.154), channel_id=1, source_target_pairs={{0,1},{1,0},{2,3},{3,2},{4,5},{5,4},{6,7},{7,6},{8,9},{9,8},{10,11... | collective-permute-start | bytes 4718600 | tf_op jit(solution)/shard_map/ppermute | solution.py:83
  342.8 89.6 %collective-permute-start.106 = (bf16[512,1536]{1,0:T(8,128)(2,1)S(1)}, bf16[512,1536]{1,0:T(8,128)(2,1)S(1)}, u32[]{:S(2)}, u32[]{:S(2)}) collective-permute-start(bf16[512,1536]{1,0:T(8,128)(2,1)S(1)} %get-tuple-element.62), channel_id=1, source_target_pairs={{0,1},{1,0},{2,3},{3,2},{4,5},{5,4},{6,7},{7,6},{8,9},{9,8},{10,11... | collective-permute-start | bytes 4718600 | tf_op jit(solution)/shard_map/ppermute | solution.py:83
  386.4 35.1 %collective-permute-start.124 = (bf16[128,1536]{1,0:T(8,128)(2,1)S(1)}, bf16[128,1536]{1,0:T(8,128)(2,1)S(1)}, u32[]{:S(2)}, u32[]{:S(2)}) collective-permute-start(bf16[128,1536]{1,0:T(8,128)(2,1)S(1)} %add_convert_fusion.11), channel_id=1, source_target_pairs={{0,2},{1,3},{2,0},{3,1},{4,6},{5,7},{6,4},{7,5},{8,10},{9,11},{10,... | collective-permute-start | bytes 1179656 | tf_op jit(solution)/shard_map/ppermute | solution.py:87
  389.1 35.3 %collective-permute-start.120 = (bf16[128,1536]{1,0:T(8,128)(2,1)S(1)}, bf16[128,1536]{1,0:T(8,128)(2,1)S(1)}, u32[]{:S(2)}, u32[]{:S(2)}) collective-permute-start(bf16[128,1536]{1,0:T(8,128)(2,1)S(1)} %get-tuple-element.142), channel_id=1, source_target_pairs={{0,4},{4,0},{8,12},{12,8},{16,20},{20,16},{24,28},{28,24},{1,5},{5... | collective-permute-start | bytes 1179656 | tf_op jit(solution)/shard_map/ppermute | solution.py:92
  421.5 37.0 %collective-permute-start.130 = (bf16[128,1536]{1,0:T(8,128)(2,1)S(1)}, bf16[128,1536]{1,0:T(8,128)(2,1)S(1)}, u32[]{:S(2)}, u32[]{:S(2)}) collective-permute-start(bf16[128,1536]{1,0:T(8,128)(2,1)S(1)} %add_convert_fusion.5), channel_id=1, source_target_pairs={{0,2},{1,3},{2,0},{3,1},{4,6},{5,7},{6,4},{7,5},{8,10},{9,11},{10,... | collective-permute-start | bytes 1179656 | tf_op jit(solution)/shard_map/ppermute | solution.py:87
  424.4 35.3 %collective-permute-start.126 = (bf16[128,1536]{1,0:T(8,128)(2,1)S(1)}, bf16[128,1536]{1,0:T(8,128)(2,1)S(1)}, u32[]{:S(2)}, u32[]{:S(2)}) collective-permute-start(bf16[128,1536]{1,0:T(8,128)(2,1)S(1)} %get-tuple-element.144), channel_id=1, source_target_pairs={{0,4},{4,0},{8,12},{12,8},{16,20},{20,16},{24,28},{28,24},{1,5},{5... | collective-permute-start | bytes 1179656 | tf_op jit(solution)/shard_map/ppermute | solution.py:92
  454.9 45.5 %collective-permute-start.122 = (bf16[128,1536]{1,0:T(8,128)(2,1)S(1)}, bf16[128,1536]{1,0:T(8,128)(2,1)S(1)}, u32[]{:S(2)}, u32[]{:S(2)}) collective-permute-start(bf16[128,1536]{1,0:T(8,128)(2,1)S(1)} %pad_maximum_fusion.5), channel_id=1, source_target_pairs={{0,24},{4,28},{8,0},{12,4},{16,8},{20,12},{24,16},{28,20},{1,25},{... | collective-permute-start | bytes 1179656 | tf_op jit(solution)/shard_map/ppermute | solution.py:97
  458.5 145.4 %collective-permute-start.59 = (bf16[128,1536]{1,0:T(8,128)(2,1)}, bf16[128,1536]{1,0:T(8,128)(2,1)}, u32[]{:S(2)}, u32[]{:S(2)}) collective-permute-start(bf16[128,1536]{1,0:T(8,128)(2,1)} %pad_maximum_fusion.2), channel_id=1, source_target_pairs={{0,24},{4,28},{8,0},{12,4},{16,8},{20,12},{24,16},{28,20},{1,25},{... | collective-permute-start | bytes 1179656 | tf_op jit(solution)/shard_map/ppermute | solution.py:97
  459.6 31.3 %collective-permute-start.132 = (bf16[128,1536]{1,0:T(8,128)(2,1)S(1)}, bf16[128,1536]{1,0:T(8,128)(2,1)S(1)}, u32[]{:S(2)}, u32[]{:S(2)}) collective-permute-start(bf16[128,1536]{1,0:T(8,128)(2,1)S(1)} %get-tuple-element.146), channel_id=1, source_target_pairs={{0,4},{4,0},{8,12},{12,8},{16,20},{20,16},{24,28},{28,24},{1,5},{5... | collective-permute-start | bytes 1179656 | tf_op jit(solution)/shard_map/ppermute | solution.py:92
  496.8 108.3 %collective-permute-start.85 = (bf16[128,1536]{1,0:T(8,128)(2,1)}, bf16[128,1536]{1,0:T(8,128)(2,1)}, u32[]{:S(2)}, u32[]{:S(2)}) collective-permute-start(bf16[128,1536]{1,0:T(8,128)(2,1)} %pad_maximum_fusion.3), channel_id=1, source_target_pairs={{0,16},{4,20},{8,24},{12,28},{16,0},{20,4},{24,8},{28,12},{1,17},{... | collective-permute-start | bytes 1179656 | tf_op jit(solution)/shard_map/ppermute | solution.py:97
  545.6 33.3 %collective-permute-start.151 = (f32[41,1536]{1,0:T(8,128)}, f32[41,1536]{1,0:T(8,128)}, u32[]{:S(2)}, u32[]{:S(2)}) collective-permute-start(f32[41,1536]{1,0:T(8,128)} %add.520), channel_id=1, source_target_pairs={{0,24},{4,28},{8,0},{12,4},{16,8},{20,12},{24,16},{28,20},{1,25},{... | collective-permute-start | bytes 755720 | tf_op jit(solution)/shard_map/ppermute | solution.py:97
  546.0 33.0 %collective-permute-start.150 = (f32[41,1536]{1,0:T(8,128)}, f32[41,1536]{1,0:T(8,128)}, u32[]{:S(2)}, u32[]{:S(2)}) collective-permute-start(f32[41,1536]{1,0:T(8,128)} %add.520), channel_id=1, source_target_pairs={{0,16},{4,20},{8,24},{12,28},{16,0},{20,4},{24,8},{28,12},{1,17},{... | collective-permute-start | bytes 755720 | tf_op jit(solution)/shard_map/ppermute | solution.py:97
  (286 other events, 3111.1 us)
Sparse Core Ops, SparseCore 0:
  575.0 139.7 all-reduce.8

commit v3 on v1

--- a/solution.py
+++ b/solution.py
@@ -3,6 +3,8 @@
 import jax
 import jax.numpy as jnp
 from jax import lax
+from jax.experimental import pallas as pl
+from jax.experimental.pallas import tpu as pltpu
 from jax.sharding import PartitionSpec as P
 
 HEAD_SIZE_DIM = 64
@@ -77,7 +79,7 @@
     return lax.all_to_all(boxes, "ep", split_axis=1, concat_axis=1, tiled=True)
 
 
-def local(
+def local_routed(
     tokens,
     norm_gain,
     query_matrix,
@@ -342,6 +344,768 @@
     )
 
 
+def swap_core(value):
+    return lax.ppermute(value, "tp", [(i, i ^ 1) for i in range(4)])
+
+
+def swap_x(value):
+    return lax.ppermute(value, "tp", [(i, i ^ 2) for i in range(4)])
+
+
+def swap_y(value):
+    owners = lax.axis_size("ep")
+    return lax.ppermute(value, "ep", [(i, i ^ 1) for i in range(owners)])
+
+
+def shift_z(value, step):
+    owners = lax.axis_size("ep")
+    return lax.ppermute(value, "ep", [(i, (i + 2 * step) % owners) for i in range(owners)])
+
+
+def after(value, *others):
+    return lax.optimization_barrier((value,) + others)[0]
+
+
+def add_low(left, right):
+    return (left.astype(jnp.float32) + right.astype(jnp.float32)).astype(jnp.bfloat16)
+
+
+def gather_pieces(value):
+    across = swap_x(value)
+    other = swap_core(value)
+    return value, other, across, swap_core(across)
+
+
+def gather_tp(value):
+    me = lax.axis_index("tp")
+    rows = value.shape[0]
+    full = jnp.zeros((4 * rows,) + value.shape[1:], value.dtype)
+    for flip, part in enumerate(gather_pieces(value)):
+        full = lax.dynamic_update_slice_in_dim(full, part, (me ^ flip) * rows, 0)
+    return full
+
+
+def scatter_tp(value, core_dtype):
+    me = lax.axis_index("tp")
+    core, across = me % 2, me // 2
+    boxes = value.reshape((2, 2, value.shape[0] // 4) + value.shape[1:])
+    leave = lax.dynamic_index_in_dim(boxes, 1 - core, 1, keepdims=False).astype(core_dtype)
+    stay = lax.dynamic_index_in_dim(boxes, core, 1, keepdims=False)
+    both = stay.astype(jnp.float32) + swap_core(leave).astype(jnp.float32)
+    mine = lax.dynamic_index_in_dim(both, across, 0, keepdims=False)
+    theirs = lax.dynamic_index_in_dim(both, 1 - across, 0, keepdims=False).astype(jnp.bfloat16)
+    return mine + swap_x(theirs).astype(jnp.float32), theirs
+
+
+def reduce_first(own_core, other_core):
+    return own_core, swap_core(other_core)
+
+
+def reduce_sends(boxes):
+    own_core, arrived = boxes
+    return add_low(own_core[2], arrived[2]), add_low(own_core[3], arrived[3])
+
+
+def reduce_second(boxes, from_x, from_y):
+    own_core, arrived = boxes
+    half = own_core.shape[1] // 2
+    parts = []
+    for part, extra in ((0, from_x), (1, from_y)):
+        for rows in (slice(0, half), slice(half, 2 * half)):
+            total = own_core[part, rows].astype(jnp.float32) + arrived[part, rows].astype(jnp.float32)
+            parts.append((total + extra[rows].astype(jnp.float32)).astype(jnp.bfloat16))
+    return parts
+
+
+def join_kernel(first_ref, from_y_ref, last_ref, from_x_ref, out_ref):
+    half = first_ref.shape[0]
+    out_ref[:half] = add_low(first_ref[...], from_y_ref[...])
+    out_ref[half:] = add_low(last_ref[...], from_x_ref[...])
+
+
+def reduce_home(first, from_y, last, from_x, steps):
+    count = len(steps)
+    half, width = first.shape[0] // count, first.shape[1]
+    total = []
+    for i in range(count):
+        half_spec = pl.BlockSpec((half, width), lambda j, i=i: (i, 0))
+        total.append(
+            pl.pallas_call(
+                join_kernel,
+                grid=(1,),
+                in_specs=[half_spec] * 4,
+                out_specs=pl.BlockSpec((2 * half, width), lambda j: (0, 0)),
+                out_shape=jax.ShapeDtypeStruct((2 * half, width), first.dtype),
+                name="join_halves",
+            )(first, from_y, last, from_x)
+        )
+    return [shift_z(total[i], -step) if step else total[i] for i, step in enumerate(steps)]
+
+
+def butterfly_sum(value):
+    value = value + swap_core(value)
+    value = value + swap_x(value)
+    value = value + swap_y(value)
+    value = value + shift_z(value, 2)
+    owners = lax.axis_size("ep")
+    return value + lax.ppermute(value, "ep", [(i, i ^ 2) for i in range(owners)])
+
+
+def planes_of(boxes):
+    planes = boxes.shape[0]
+    plane = lax.axis_index("ep") // 2
+    return [lax.dynamic_index_in_dim(boxes, (plane + i) % planes, 0, keepdims=False) for i in range(planes)]
+
+
+def send_planes(parts):
+    return [shift_z(part.astype(jnp.bfloat16), i) for i, part in enumerate(parts) if i]
+
+
+def add_all(first, others):
+    return first.astype(jnp.float32) + sum(part.astype(jnp.float32) for part in others)
+
+
+def spread_planes(value):
+    planes = lax.axis_size("ep") // 2
+    return [value] + [shift_z(value, i) for i in range(1, planes)]
+
+
+def join_planes(parts):
+    planes, plane = len(parts), lax.axis_index("ep") // 2
+    full = jnp.zeros((planes,) + parts[0].shape, parts[0].dtype)
+    for i, part in enumerate(parts):
+        full = lax.dynamic_update_index_in_dim(full, part, (plane - i) % planes, 0)
+    return full
+
+
+def sides_of(boxes):
+    y = lax.axis_index("ep") % 2
+    return [lax.dynamic_index_in_dim(boxes, i, 0, keepdims=False) for i in (y, 1 - y)]
+
+
+def join_sides(own, other):
+    y = lax.axis_index("ep") % 2
+    full = jnp.zeros((2,) + own.shape, own.dtype)
+    full = lax.dynamic_update_index_in_dim(full, own, y, 0)
+    return lax.dynamic_update_index_in_dim(full, other, 1 - y, 0)
+
+
+FIRST_HALF = ((0, 0), (2, 0), (0, 1), (2, 1))
+LAST_HALF = ((1, 0), (1, 1), (3, 0), (3, 1))
+NT = (((1,), (1,)), ((), ()))
+TN = (((0,), (0,)), ((), ()))
+
+
+def dot_f32(left, right, dims=None):
+    if dims is None:
+        return jnp.dot(left, right, preferred_element_type=jnp.float32)
+    return lax.dot_general(left, right, dims, preferred_element_type=jnp.float32)
+
+
+def store_halves(own_ref, other_ref, block, plane, result):
+    half = result.shape[0] // 2
+    count = own_ref.shape[1] // (2 * half)
+    for i in range(4):
+        (part_a, place_a), (part_b, place_b) = FIRST_HALF[i], LAST_HALF[i]
+        first = pl.ds((place_a * count + plane) * half, half)
+        last = pl.ds((place_b * count + plane) * half, half)
+        for side, ref in enumerate((own_ref, other_ref)):
+
+            @pl.when(block == side * 4 + i)
+            def _(ref=ref, first=first, last=last, part_a=part_a, part_b=part_b):
+                ref[part_a, first, :] = result[:half]
+                ref[part_b, last, :] = result[half:]
+
+
+def expert_kernel(sizes, *refs):
+    experts, slots, blocks, rows, routed = sizes
+    x_parts, g_ref = refs[:8], refs[8]
+    base_ref, order_ref, router_ref, gate_ref, up_ref, down_ref = refs[9:15]
+    own_ref, other_ref, xr_out, gr_out, dgu_ref, wh_ref, rg_ref, picks = refs[15:23]
+    xs, gs, xr, gr, wgu, wd, back, probs, weight, d_weight, table = refs[23:34]
+    x_sem, g_sem, w_sem, out_sem = refs[34:38]
+    width = xs.shape[1]
+    units = wd.shape[1]
+    total = experts * slots
+    depth = blocks * slots
+    for b in range(blocks):
+        source = pl.ds(pl.multiple_of(order_ref[b] * rows, rows), rows)
+        pltpu.make_async_copy(x_parts[b], xs.at[pl.ds(b * rows, rows)], x_sem.at[b]).start()
+        pltpu.make_async_copy(g_ref.at[source], gs.at[pl.ds(b * rows, rows)], g_sem.at[b]).start()
+    for e in range(experts):
+        pltpu.make_async_copy(gate_ref.at[e], wgu.at[e, :, pl.ds(0, units)], w_sem.at[0, e]).start()
+        pltpu.make_async_copy(up_ref.at[e], wgu.at[e, :, pl.ds(units, units)], w_sem.at[1, e]).start()
+        pltpu.make_async_copy(down_ref.at[e], wd.at[e], w_sem.at[2, e]).start()
+    rg_ref[...] = jnp.zeros_like(rg_ref)
+
+    def block_rows(b):
+        return pl.ds(pl.multiple_of(b * rows, rows), rows)
+
+    def slot_rows(b):
+        return pl.ds(pl.multiple_of(b * slots, slots), slots)
+
+    def expand(values):
+        return jnp.concatenate([jnp.broadcast_to(values[e], (slots, rows)) for e in range(experts)], axis=0)
+
+    place = jnp.concatenate(
+        [lax.broadcasted_iota(jnp.int32, (slots, rows), 0)] * experts, axis=0
+    ).astype(jnp.float32)
+
+    def gather_x(b, carry):
+        pltpu.make_async_copy(xs.at[block_rows(b)], xs.at[block_rows(b)], x_sem.at[b]).wait()
+        pltpu.make_async_copy(gs.at[block_rows(b)], gs.at[block_rows(b)], g_sem.at[b]).wait()
+        x_block = xs[block_rows(b), :]
+        logits = dot_f32(router_ref[...], x_block, NT)
+        lane = lax.broadcasted_iota(jnp.int32, logits.shape, 0)
+        logits = jnp.where(lane < routed, logits, -1e30)
+        expo = jnp.exp(logits - jnp.max(logits, axis=0, keepdims=True))
+        prob = expo / jnp.sum(expo, axis=0, keepdims=True)
+        probs[b] = prob
+        table[...] = gs[block_rows(b), width:].astype(jnp.float32).T
+        hit = expand([table[pl.ds(base_ref[0] + e, 1), :] for e in range(experts)]) == place
+        prob_rows = expand([prob[e : e + 1, :] for e in range(experts)])
+        chosen = jnp.sum(jnp.where(hit, prob_rows, 0.0), axis=1, keepdims=True)
+        chosen = jnp.broadcast_to(chosen, (total, rows))
+        one = hit.astype(jnp.float32).astype(jnp.bfloat16)
+        picks[b] = one
+        taken = dot_f32(one, x_block).astype(jnp.bfloat16)
+        for e in range(experts):
+            xr[e, slot_rows(b), :] = taken[e * slots : (e + 1) * slots]
+            weight[e, slot_rows(b), :] = chosen[e * slots : (e + 1) * slots]
+        back[b, pl.ds(total, router_ref.shape[0]), :] = router_ref[...]
+        return carry
+
+    def gather_g(b, carry):
+        taken = dot_f32(picks[b], gs[block_rows(b), :width]).astype(jnp.bfloat16)
+        for e in range(experts):
+            gr[e, slot_rows(b), :] = taken[e * slots : (e + 1) * slots]
+        return carry
+
+    lax.fori_loop(0, blocks, gather_x, 0)
+    pltpu.make_async_copy(xr, xr_out, out_sem.at[0]).start()
+    lax.fori_loop(0, blocks, gather_g, 0)
+    pltpu.make_async_copy(gr, gr_out, out_sem.at[1]).start()
+
+    def one_expert(e, carry):
+        low, high = pl.ds(0, units), pl.ds(units, units)
+        pltpu.make_async_copy(wgu.at[e, :, low], wgu.at[e, :, low], w_sem.at[0, e]).wait()
+        pltpu.make_async_copy(wgu.at[e, :, high], wgu.at[e, :, high], w_sem.at[1, e]).wait()
+        pltpu.make_async_copy(wd.at[e], wd.at[e], w_sem.at[2, e]).wait()
+        both = dot_f32(xr[e], wgu[e])
+        gate, up = both[:, :units], both[:, units:]
+        back_hidden = dot_f32(gr[e], wd[e], NT)
+        sig = 1.0 / (1.0 + jnp.exp(-gate))
+        silu = gate * sig
+        hidden = silu * up
+        product = hidden.astype(jnp.bfloat16).astype(jnp.float32) * back_hidden
+        d_weight[e] = jnp.broadcast_to(jnp.sum(product, axis=1, keepdims=True), (depth, rows))
+        share = weight[e]
+        d_hidden = share * back_hidden
+        d_gate = d_hidden * up * (sig * (1.0 + gate * (1.0 - sig)))
+        d_up = d_hidden * silu
+        d_both = jnp.concatenate([d_gate, d_up], axis=1).astype(jnp.bfloat16)
+        dgu_ref[e] = d_both
+        wh_ref[e] = (share * hidden).astype(jnp.bfloat16)
+        d_rows = dot_f32(d_both, wgu[e], NT).astype(jnp.bfloat16)
+        for b in range(blocks):
+            back[b, slot_rows(e), :] = d_rows[b * slots : (b + 1) * slots]
+        return carry
+
+    lax.fori_loop(0, experts, one_expert, 0)
+
+    def scatter(b, carry):
+        one = picks[b]
+        d_slot = jnp.concatenate([d_weight[e, slot_rows(b), :] for e in range(experts)], axis=0)
+        spread = one.astype(jnp.float32) * d_slot
+        d_prob = jnp.concatenate(
+            [jnp.sum(spread[e * slots : (e + 1) * slots], axis=0, keepdims=True) for e in range(experts)]
+            + [jnp.zeros((router_ref.shape[0] - experts, rows), jnp.float32)],
+            axis=0,
+        )
+        prob = probs[b]
+        centre = jnp.sum(prob * d_prob, axis=0, keepdims=True)
+        d_logits = (prob * (d_prob - centre)).astype(jnp.bfloat16)
+        rg_ref[...] += dot_f32(d_logits, xs[block_rows(b), :])
+        result = dot_f32(jnp.concatenate([one, d_logits], axis=0), back[b], TN).astype(jnp.bfloat16)
+        store_halves(own_ref, other_ref, b, 0, result)
+        return carry
+
+    lax.fori_loop(0, blocks, scatter, 0)
+    pltpu.make_async_copy(xr, xr_out, out_sem.at[0]).wait()
+    pltpu.make_async_copy(gr, gr_out, out_sem.at[1]).wait()
+
+
+def expert_call(x_parts, g_all, base, order, router_rows, gate_weight, up_weight, down_weight, routed, slots):
+    blocks = len(x_parts)
+    rows, width = x_parts[0].shape
+    experts, _, units = gate_weight.shape
+    depth = blocks * slots
+    padded = router_rows.shape[0]
+    extra = g_all.shape[1] - width
+    low, full = jnp.bfloat16, jnp.float32
+    any_spec = pl.BlockSpec(memory_space=pl.ANY)
+    vmem_spec = pl.BlockSpec(memory_space=pltpu.VMEM)
+    smem_spec = pl.BlockSpec(memory_space=pltpu.SMEM)
+    return pl.pallas_call(
+        lambda *refs: expert_kernel((experts, slots, blocks, rows, routed), *refs),
+        out_shape=(
+            jax.ShapeDtypeStruct((4, rows, width), low),
+            jax.ShapeDtypeStruct((4, rows, width), low),
+            jax.ShapeDtypeStruct((experts, depth, width), low),
+            jax.ShapeDtypeStruct((experts, depth, width), low),
+            jax.ShapeDtypeStruct((experts, depth, 2 * units), low),
+            jax.ShapeDtypeStruct((experts, depth, units), low),
+            jax.ShapeDtypeStruct((padded, width), full),
+            jax.ShapeDtypeStruct((blocks, experts * slots, rows), low),
+        ),
+        in_specs=[any_spec] * 9 + [smem_spec, smem_spec, vmem_spec] + [any_spec] * 3,
+        out_specs=(vmem_spec, vmem_spec, any_spec, any_spec) + (vmem_spec,) * 4,
+        scratch_shapes=[
+            pltpu.VMEM((blocks * rows, width), low),
+            pltpu.VMEM((blocks * rows, width + extra), low),
+            pltpu.VMEM((experts, depth, width), low),
+            pltpu.VMEM((experts, depth, width), low),
+            pltpu.VMEM((experts, width, 2 * units), low),
+            pltpu.VMEM((experts, units, width), low),
+            pltpu.VMEM((blocks, experts * slots + padded, width), low),
+            pltpu.VMEM((blocks, padded, rows), full),
+            pltpu.VMEM((experts, depth, rows), full),
+            pltpu.VMEM((experts, depth, rows), full),
+            pltpu.VMEM((extra, rows), full),
+            pltpu.SemaphoreType.DMA((blocks,)),
+            pltpu.SemaphoreType.DMA((blocks,)),
+            pltpu.SemaphoreType.DMA((3, experts)),
+            pltpu.SemaphoreType.DMA((2,)),
+        ],
+        compiler_params=pltpu.CompilerParams(vmem_limit_bytes=50 * 2**20),
+        cost_estimate=pl.CostEstimate(
+            flops=2 * experts * depth * width * units * 40, bytes_accessed=60 * 2**20, transcendentals=0
+        ),
+        name="expert_chunk",
+    )(*x_parts, g_all, base, order, router_rows, gate_weight, up_weight, down_weight)
+
+
+def output_kernel(sizes, *refs):
+    experts, slots, blocks, planes = sizes
+    weighted, picks = refs[:planes], refs[planes : 2 * planes]
+    down_ref, own_ref, other_ref, rows_ref = refs[2 * planes :]
+    for plane in range(planes):
+
+        def one_expert(e, carry, plane=plane):
+            result = dot_f32(weighted[plane][e], down_ref[e]).astype(jnp.bfloat16)
+            for b in range(blocks):
+                rows_ref[b, pl.ds(pl.multiple_of(e * slots, slots), slots), :] = result[b * slots : (b + 1) * slots]
+            return carry
+
+        lax.fori_loop(0, experts, one_expert, 0)
+
+        def scatter(b, carry, plane=plane):
+            result = dot_f32(picks[plane][b], rows_ref[b], TN).astype(jnp.bfloat16)
+            store_halves(own_ref, other_ref, b, plane, result)
+            return carry
+
+        lax.fori_loop(0, blocks, scatter, 0)
+
+
+def output_call(weighted, picks, down_weight):
+    planes = len(weighted)
+    experts, depth, units = weighted[0].shape
+    width = down_weight.shape[2]
+    blocks, total, rows = picks[0].shape
+    boxes = jax.ShapeDtypeStruct((4, planes * rows, width), jnp.bfloat16)
+    vmem_spec = pl.BlockSpec(memory_space=pltpu.VMEM)
+    return pl.pallas_call(
+        lambda *refs: output_kernel((experts, total // experts, blocks, planes), *refs),
+        in_specs=[vmem_spec] * (2 * planes + 1),
+        out_specs=(vmem_spec,) * 2,
+        out_shape=(boxes, boxes),
+        scratch_shapes=[pltpu.VMEM((blocks, total, width), jnp.bfloat16)],
+        compiler_params=pltpu.CompilerParams(vmem_limit_bytes=40 * 2**20),
+        cost_estimate=pl.CostEstimate(
+            flops=2 * planes * experts * depth * width * units * 12,
+            bytes_accessed=planes * 18 * 2**20,
+            transcendentals=0,
+        ),
+        name="expert_output",
+    )(*weighted, *picks, down_weight)
+
+
+def weight_kernel(count, *refs):
+    xr, gr, dgu, wh = (refs[i * count : (i + 1) * count] for i in range(4))
+    gate_ref, up_ref, down_ref = refs[4 * count :]
+    units = gate_ref.shape[2]
+    both = sum(dot_f32(x[0], d[0], TN) for x, d in zip(xr, dgu))
+    gate_ref[0] = both[:, :units]
+    up_ref[0] = both[:, units:]
+    down_ref[0] = sum(dot_f32(h[0], g[0], TN) for h, g in zip(wh, gr))
+
+
+def weight_call(xr, gr, dgu, wh):
+    count = len(xr)
+    experts, depth, width = xr[0].shape
+    units = wh[0].shape[2]
+    spec = lambda array: pl.BlockSpec((1,) + array.shape[1:], lambda e: (e, 0, 0))
+    operands = [*xr, *gr, *dgu, *wh]
+    up_like = jax.ShapeDtypeStruct((experts, width, units), jnp.float32)
+    down_like = jax.ShapeDtypeStruct((experts, units, width), jnp.float32)
+    return pl.pallas_call(
+        lambda *refs: weight_kernel(count, *refs),
+        grid=(experts,),
+        out_shape=(up_like, up_like, down_like),
+        in_specs=[spec(a) for a in operands],
+        out_specs=(spec(up_like), spec(up_like), spec(down_like)),
+        compiler_params=pltpu.CompilerParams(vmem_limit_bytes=50 * 2**20),
+        cost_estimate=pl.CostEstimate(
+            flops=2 * experts * depth * count * width * units * 3,
+            bytes_accessed=60 * 2**20,
+            transcendentals=0,
+        ),
+        name="expert_weights",
+    )(*operands)
+
+
+def swap_halves(values, half):
+    lane = lax.broadcasted_iota(jnp.int32, values.shape, 1)
+    size = values.shape[1]
+    return jnp.where(
+        lane % (2 * half) < half, pltpu.roll(values, size - half, 1), pltpu.roll(values, half, 1)
+    )
+
+
+def attention_back_kernel(sizes, *refs):
+    group_factor, head_size = sizes
+    parts, me_ref = refs[:4], refs[4]
+    att_ref, q_ref, k_ref, v_ref, normed_ref, wo_ref, wq_ref, wk_ref, wv_ref = refs[5:14]
+    cos_ref, sin_ref, column_ref, row_ref, live_ref = refs[14:19]
+    weights_ref, out_ref, stay_ref, leave_ref = refs[19:23]
+    branch, back, d_q, d_k, d_v, d_all, sem = refs[23:30]
+    rows = parts[0].shape[0]
+    seq_len = branch.shape[0]
+    factor = 1.0 / math.sqrt(head_size)
+    me = me_ref[0]
+
+    def place(flip):
+        return pl.ds(pl.multiple_of((me ^ flip) * rows, rows), rows)
+
+    for flip, part in enumerate(parts):
+        pltpu.make_async_copy(part, branch.at[place(flip)], sem.at[flip]).start()
+    for flip, part in enumerate(parts):
+        pltpu.make_async_copy(part, branch.at[place(flip)], sem.at[flip]).wait()
+    back[...] = dot_f32(branch[...], wo_ref[...], NT).astype(jnp.bfloat16)
+    out_ref[...] = dot_f32(att_ref[...], branch[...], TN).astype(jnp.bfloat16)
+    d_k[...] = jnp.zeros_like(d_k)
+    d_v[...] = jnp.zeros_like(d_v)
+    step = seq_len // 2
+    for start in (0, step):
+        keys = start + step
+        shape = (step, keys)
+        query_place = start + lax.broadcasted_iota(jnp.int32, shape, 0)
+        key_place = lax.broadcasted_iota(jnp.int32, shape, 1)
+        same = column_ref[start : start + step, :] == row_ref[:, :keys]
+        usable = (live_ref[:, :keys] > 0) | (key_place == query_place)
+        allowed = same & (key_place <= query_place) & usable
+        for head in range(q_ref.shape[1] // head_size):
+            group = head // group_factor
+            mine = slice(head * head_size, (head + 1) * head_size)
+            shared = slice(group * head_size, (group + 1) * head_size)
+            query = q_ref[start : start + step, mine]
+            key, value = k_ref[:keys, shared], v_ref[:keys, shared]
+            d_out = back[start : start + step, mine]
+            scores = jnp.where(allowed, dot_f32(query, key, NT) * factor, -1e30)
+            expo = jnp.exp(scores - jnp.max(scores, axis=1, keepdims=True))
+            probs = expo * (1.0 / jnp.sum(expo, axis=1, keepdims=True))
+            d_probs = dot_f32(d_out, value, NT)
+            centre = jnp.sum(probs * d_probs, axis=1, keepdims=True)
+            d_scores = (probs * (d_probs - centre)).astype(jnp.bfloat16)
+            d_q[start : start + step, mine] = dot_f32(d_scores, key) * factor
+            d_k[:keys, shared] += dot_f32(d_scores, query, TN) * factor
+            d_v[:keys, shared] += dot_f32(probs.astype(jnp.bfloat16), d_out, TN)
+    pair = 2 * head_size
+    q_width = q_ref.shape[1]
+    kv_width = k_ref.shape[1]
+    for source, count, offset in ((d_q, q_width // pair, 0), (d_k, kv_width // pair, q_width)):
+        for i in range(count):
+            turned = source[:, i * pair : (i + 1) * pair]
+            flat = turned * cos_ref[...] + swap_halves(turned, head_size // 2) * sin_ref[...]
+            d_all[:, offset + i * pair : offset + (i + 1) * pair] = flat.astype(jnp.bfloat16)
+    d_all[:, q_width + kv_width :] = d_v[...].astype(jnp.bfloat16)
+    width = normed_ref.shape[1]
+    for i in range(4):
+        features = slice(i * width // 4, (i + 1) * width // 4)
+        weights_ref[features, :] = dot_f32(normed_ref[:, features], d_all[...], TN).astype(jnp.bfloat16)
+    for flip in range(4):
+        values = d_all[place(flip), :]
+        total = dot_f32(values[:, :q_width], wq_ref[...], NT)
+        total += dot_f32(values[:, q_width : q_width + kv_width], wk_ref[...], NT)
+        total += dot_f32(values[:, q_width + kv_width :], wv_ref[...], NT)
+        if flip % 2:
+            leave_ref[flip // 2] = total.astype(jnp.bfloat16)
+        else:
+            stay_ref[flip // 2] = total
+
+
+def attention_back_call(parts, attended, query, key, value, normed, wo, wq, wk, wv, cos, sin, segments, live, factor):
+    rows, width = parts[0].shape
+    seq_len, q_width = query.shape
+    kv_width = key.shape[1]
+    me = lax.axis_index("tp").astype(jnp.int32)[None]
+    low, full = jnp.bfloat16, jnp.float32
+    any_spec = pl.BlockSpec(memory_space=pl.ANY)
+    vmem_spec = pl.BlockSpec(memory_space=pltpu.VMEM)
+    cos_pair = jnp.tile(cos, (1, 4))
+    sin_pair = jnp.tile(jnp.concatenate([sin, -sin], axis=1), (1, 2))
+    return pl.pallas_call(
+        lambda *refs: attention_back_kernel((factor, HEAD_SIZE_DIM), *refs),
+        out_shape=(
+            jax.ShapeDtypeStruct((width, q_width + 2 * kv_width), low),
+            jax.ShapeDtypeStruct((q_width, width), low),
+            jax.ShapeDtypeStruct((2, rows, width), full),
+            jax.ShapeDtypeStruct((2, rows, width), low),
+        ),
+        in_specs=[any_spec] * 4 + [pl.BlockSpec(memory_space=pltpu.SMEM)] + [vmem_spec] * 14,
+        out_specs=(vmem_spec,) * 4,
+        scratch_shapes=[
+            pltpu.VMEM((seq_len, width), low),
+            pltpu.VMEM((seq_len, q_width), low),
+            pltpu.VMEM((seq_len, q_width), full),
+            pltpu.VMEM((seq_len, kv_width), full),
+            pltpu.VMEM((seq_len, kv_width), full),
+            pltpu.VMEM((seq_len, q_width + 2 * kv_width), low),
+            pltpu.SemaphoreType.DMA((4,)),
+        ],
+        compiler_params=pltpu.CompilerParams(vmem_limit_bytes=48 * 2**20),
+        cost_estimate=pl.CostEstimate(
+            flops=2 * seq_len * width * (2 * q_width + 4 * kv_width) * 2 * 6,
+            bytes_accessed=60 * 2**20,
+            transcendentals=0,
+        ),
+        name="attention_back",
+    )(
+        *parts, me, attended, query, key, value, normed, wo, wq, wk, wv, cos_pair, sin_pair,
+        segments.reshape(-1, 1), segments.reshape(1, -1), live.reshape(1, -1),
+    )
+
+
+def local_gathered(
+    tokens,
+    norm_gain,
+    query_matrix,
+    key_matrix,
+    value_matrix,
+    out_weight,
+    moe_gain,
+    router_weight,
+    gate_weight,
+    up_weight,
+    down_weight,
+    cotangent,
+    expert_ids,
+    segments,
+    valid_mask,
+):
+    quarter = tokens.shape[0]
+    width = tokens.shape[1]
+    groups = lax.axis_size("tp")
+    owners = lax.axis_size("ep")
+    my_part = lax.axis_index("tp")
+    seq_len = quarter * groups
+    head_size = HEAD_SIZE_DIM
+    kv_heads = key_matrix.shape[1] // head_size
+    q_heads = query_matrix.shape[1] // head_size
+    group_factor = q_heads // kv_heads
+    local_experts = gate_weight.shape[0]
+    experts_all = router_weight.shape[1]
+    chosen_count = expert_ids.shape[1]
+    slots = max(8, 3 * quarter * chosen_count // (2 * experts_all) // 8 * 8)
+    factor = 1.0 / math.sqrt(head_size)
+    segment_row = segments[0]
+    live_row = valid_mask[0]
+    x_float = tokens.astype(jnp.float32)
+    planes = owners // 2
+    owner = lax.axis_index("ep")
+    my_valid = lax.dynamic_slice_in_dim(live_row, my_part * quarter, quarter, 0)
+    padded = -(-experts_all // 16) * 16
+    named = jnp.any(expert_ids[:, :, None] == jnp.arange(padded)[None, None, :], axis=1) & (my_valid[:, None] > 0)
+    before = (jnp.arange(quarter)[None, :] < jnp.arange(quarter)[:, None]).astype(jnp.bfloat16)
+    earlier = jnp.dot(before, named.astype(jnp.bfloat16), preferred_element_type=jnp.float32)
+    slot = jnp.where(named, earlier, -1.0).astype(jnp.bfloat16)
+    slot = jnp.pad(slot, ((0, 0), (0, -padded % 128)), constant_values=-1.0)
+    sent = jnp.concatenate([cotangent, slot], axis=1)
+    g_all = lax.all_gather(sent, ("ep", "tp"), axis=0, tiled=True)
+    router_rows = jnp.roll(router_weight.T, -owner * local_experts, axis=0)
+    router_rows = jnp.pad(router_rows, ((0, padded - experts_all), (0, 0)))
+    base = (owner * local_experts).astype(jnp.int32)[None]
+    step = jnp.arange(planes)[:, None]
+    flip_y = jnp.array([0, 0, 1, 1, 0, 0, 1, 1])[None, :]
+    flip_tp = jnp.array([0, 2, 0, 2, 1, 3, 1, 3])[None, :]
+    order = (((owner // 2 - step) % planes) * 2 + (owner % 2 ^ flip_y)) * 4 + (my_part ^ flip_tp)
+    order = order.astype(jnp.int32)
+    tokens_all = gather_tp(tokens)
+    normed_all = rms_norm(tokens_all.astype(jnp.float32), norm_gain).astype(jnp.bfloat16)
+    query_unrotated = jnp.dot(normed_all, query_matrix, preferred_element_type=jnp.float32).reshape(
+        seq_len, kv_heads, group_factor, head_size
+    )
+    key_unrotated = jnp.dot(normed_all, key_matrix, preferred_element_type=jnp.float32).reshape(
+        seq_len, kv_heads, head_size
+    )
+    value_vectors = (
+        jnp.dot(normed_all, value_matrix, preferred_element_type=jnp.float32)
+        .astype(jnp.bfloat16)
+        .reshape(seq_len, kv_heads, head_size)
+    )
+    cos_table, sin_table = angle_tables(seq_len, head_size)
+    cos_query = cos_table[:, None, None, :]
+    sin_query = sin_table[:, None, None, :]
+    cos_key = cos_table[:, None, :]
+    sin_key = sin_table[:, None, :]
+    query_val = rotate(query_unrotated, cos_query, sin_query).astype(jnp.bfloat16)
+    key_val = rotate(key_unrotated, cos_key, sin_key).astype(jnp.bfloat16)
+    height = min(512, seq_len)
+    offset = 0
+    allowed = block_mask(segment_row, live_row, offset, height)
+    scores = block_scores(query_val, key_val, allowed, factor)
+    peak = jnp.max(scores, axis=-1, keepdims=True)
+    expo = jnp.exp(scores - peak)
+    denom = jnp.sum(expo, axis=-1, keepdims=True)
+    weights = (expo / denom).astype(jnp.bfloat16)
+    mixed = jnp.einsum("grqk,kgd->qgrd", weights, value_vectors, preferred_element_type=jnp.float32)
+    outputs = mixed.reshape(height, q_heads * head_size)
+    log_sums = [peak + jnp.log(denom)]
+    attended = outputs.astype(jnp.bfloat16)
+    branch, _ = scatter_tp(
+        jnp.dot(attended, out_weight, preferred_element_type=jnp.float32), jnp.float32
+    )
+    middle = x_float + branch
+    moe_in = rms_norm(middle, moe_gain).astype(jnp.bfloat16)
+    column, x_chunks = moe_in, []
+    for i in range(planes):
+        column = shift_z(column, 1) if i else column
+        across, along = swap_x(column), swap_y(column)
+        diagonal = swap_x(along) if i % 2 else swap_y(across)
+        parts = (column, across, along, diagonal)
+        x_chunks.append(parts + tuple(swap_core(part) for part in parts))
+    kept, boxes, sends, halves = [], [], [], []
+
+    def second(i):
+        first, first_sent, last, last_sent = reduce_second(boxes[i], swap_x(sends[i][0]), swap_y(sends[i][1]))
+        halves.append((first, swap_y(first_sent), last, swap_x(last_sent)))
+        return first_sent, last_sent
+
+    for i in range(planes):
+        ready = [part for chunk in x_chunks for part in chunk[1:3]] if i == 0 else []
+        if i >= 2:
+            sends.append(reduce_sends(boxes[i - 2]))
+            ready += [*sends[i - 2]]
+        if i >= 3:
+            ready += second(i - 3)
+        own, other, *rest = expert_call(
+            x_chunks[i], g_all, base, order[i], after(router_rows, *ready),
+            gate_weight, up_weight, down_weight, experts_all, slots,
+        )
+        kept.append(rest)
+        boxes.append(reduce_first(own, other))
+    xr, gr, dgu, wh, router_parts, picks = zip(*kept)
+    pairs = planes
+    grad_parts = []
+    for i in range(planes):
+        if i >= len(sends):
+            sends.append(reduce_sends(boxes[i]))
+        if i == planes - 1:
+            own, other = output_call((after(wh[0], *sends[i]),) + wh[1:], picks, down_weight)
+        if i >= len(halves):
+            sent_on = second(i)
+        if i == planes - 1:
+            out_boxes = [reduce_first(own, after(other, *sent_on))]
+        grad_parts += reduce_home(*halves[i], (i,))
+    grad_moe_in = sum(part.astype(jnp.float32) for part in grad_parts)
+    router_part = jnp.roll(sum(router_parts)[:experts_all], owner * local_experts, axis=0)
+    grad_out = cotangent.astype(jnp.float32)
+    _, norm_two_back = jax.vjp(rms_norm, middle, moe_gain)
+    grad_mid_norm, moe_gain_grad = norm_two_back(grad_moe_in)
+    grad_middle = grad_out + grad_mid_norm
+    branch_parts = gather_pieces(grad_middle.astype(jnp.bfloat16))
+    out_sends = [reduce_sends(box) for box in out_boxes]
+    branch_parts, out_sends = lax.optimization_barrier((branch_parts, out_sends))
+    out_from = [(swap_x(to_x), swap_y(to_y)) for to_x, to_y in out_sends]
+    flat = lambda array: array.reshape(seq_len, -1)
+    weights, out_grad, stay, leave = attention_back_call(
+        branch_parts, attended, flat(query_val), flat(key_val), flat(value_vectors), normed_all,
+        out_weight, query_matrix, key_matrix, value_matrix, cos_table, sin_table, segment_row, live_row, group_factor,
+    )
+    out_grad = lax.psum(out_grad, "ep")
+    weights, leave, out_from = lax.optimization_barrier((weights, leave, out_from))
+    cut = weights.shape[0] * 2 // 3
+    columns = weights.shape[1]
+    upper_own, upper_leave = sides_of(weights[:cut].reshape(2, planes, -1, columns))
+    lower_parts = planes_of(weights[cut:].reshape(planes, 2, -1, columns))
+    upper_came = swap_y(upper_leave)
+    lower_came = send_planes(lower_parts)
+    both = stay + swap_core(leave).astype(jnp.float32)
+    across_came = swap_x(both[1].astype(jnp.bfloat16))
+    out_second = [reduce_second(box, *came) for box, came in zip(out_boxes, out_from)]
+    gate_grad, up_grad, down_grad = weight_call(xr, gr, (after(dgu[0], leave),) + dgu[1:], wh)
+    upper_parts = planes_of(add_low(upper_own, upper_came))
+    lower_own, lower_leave = sides_of(add_all(lower_parts[0], lower_came).astype(jnp.bfloat16))
+    upper_parts, lower_leave, across_came, out_second, down_grad = lax.optimization_barrier(
+        (upper_parts, lower_leave, across_came, out_second, down_grad)
+    )
+    upper_came = send_planes(upper_parts)
+    lower_came = swap_y(lower_leave)
+    out_third = [(first, swap_y(first_sent), last, swap_x(last_sent)) for first, first_sent, last, last_sent in out_second]
+    grad_normed = both[0] + across_came.astype(jnp.float32)
+    _, norm_one_back = jax.vjp(rms_norm, x_float, norm_gain)
+    grad_x_norm, norm_gain_grad = norm_one_back(grad_normed)
+    input_grad = grad_middle + grad_x_norm
+    small = jnp.concatenate([router_part, moe_gain_grad[None], norm_gain_grad[None]], axis=0)
+    upper_sum = add_all(upper_parts[0], upper_came).astype(jnp.bfloat16)
+    lower_sum = add_low(lower_own, lower_came)
+    upper_sum, lower_sum, out_third, small = lax.optimization_barrier((upper_sum, lower_sum, out_third, small))
+    out_parts = []
+    for i, third in enumerate(out_third):
+        out_parts += reduce_home(*third, tuple(range(i * pairs, (i + 1) * pairs)))
+    upper_came = spread_planes(upper_sum)
+    lower_came = swap_y(lower_sum)
+    small = small + swap_core(small)
+    small = small + swap_x(small)
+    upper_half, lower_half = join_planes(upper_came), join_sides(lower_sum, lower_came)
+    upper_half, lower_half, small, out_parts = lax.optimization_barrier((upper_half, lower_half, small, out_parts))
+    upper_came = swap_y(upper_half)
+    lower_came = spread_planes(lower_half)
+    output = (middle + sum(part.astype(jnp.float32) for part in out_parts)).astype(jnp.bfloat16)
+    small = small + swap_y(small)
+    small = small + shift_z(small, 2)
+    small = small + lax.ppermute(small, "ep", [(i, i ^ 2) for i in range(owners)])
+    out_grad = after(out_grad, small).astype(jnp.float32)
+    upper = join_sides(upper_half, upper_came).reshape(cut, columns)
+    lower = join_planes(lower_came).reshape(-1, columns)
+    weights = jnp.concatenate([upper, lower], axis=0).astype(jnp.float32)
+    q_width, kv_width = query_matrix.shape[1], key_matrix.shape[1]
+    query_grad, key_grad, value_grad = jnp.split(weights, (q_width, q_width + kv_width), axis=1)
+    router_grad, moe_gain_grad, norm_gain_grad = small[:experts_all].T, small[experts_all], small[experts_all + 1]
+    return (
+        output,
+        input_grad,
+        norm_gain_grad,
+        query_grad,
+        key_grad,
+        value_grad,
+        out_grad,
+        moe_gain_grad,
+        router_grad,
+        gate_grad,
+        up_grad,
+        down_grad,
+    )
+
+
+def local(*operands):
+    tokens, router_weight, gate_weight, expert_ids = operands[0], operands[7], operands[8], operands[12]
+    quarter, experts_all = tokens.shape[0], router_weight.shape[1]
+    slots = max(8, 3 * quarter * expert_ids.shape[1] // (2 * experts_all) // 8 * 8)
+    gathers = lax.axis_size("tp") == 4 and lax.axis_size("ep") == 8 and gate_weight.shape[0] * slots >= quarter
+    return (local_gathered if gathers else local_routed)(*operands)
+
+
 def solution(mesh):
     in_specs = (
         P(("ep", "tp"), None),

time: 1270 us -> 604 us (0.48)
  waiting for transfers between devices: 713 us -> 249 us
  blocking collectives: 224 us -> 0 us
  Pallas kernels: 0 us -> 149 us
  matrix products: 159 us -> 11.8 us
  starting transfers between devices: 12.6 us -> 92.7 us
  local copies, waits for them, and re-layouts: 105 us -> 29.6 us
  other arithmetic: 34.4 us -> 47.6 us
    psum x2 -> x1, waiting for transfers between devices: 292 us -> 0.01 us  [local_gathered(): out_grad = lax.psum(out_grad, 'ep')]
    ppermute x0 -> x93, waiting for transfers between devices: none -> 249 us  [the longest x22 108 us: shift_z(): lax.ppermute(value, 'ep', [(i, (i + 2 * step) % owners) for i in range(ow...]
    reduce_scatter x4 -> x0, waiting for transfers between devices: 215 us -> none  [the longest x1 117 us: local(): lax.psum_scatter(summed.reshape(1 * lax.axis_size('tp'), owners, local_ex...]
    all_to_all x2 -> x0, blocking collectives: 185 us -> none  [dispatch_rows(): return lax.all_to_all(boxes, 'ep', split_axis=1, concat_axis=1, tiled=True)]
    dot_general x32 -> x6, matrix products: 159 us -> 6.82 us  [the longest x1 3.55 us: local_gathered(): jnp.einsum('grqk,kgd->qgrd', weights, value_vectors, preferred_element_ty...]
    pallas_call x0 -> x15, Pallas kernels: none -> 149 us  [the longest x4 74.1 us: expert_call(): pl.pallas_call(lambda *refs: expert_kernel((experts, slots, blocks, rows,...]
    all_gather x4 -> x1, waiting for transfers between devices: 146 us -> 0.01 us  [local_gathered(): g_all = lax.all_gather(sent, ('ep', 'tp'), axis=0, tiled=True)]
    ppermute x0 -> x93, starting transfers between devices: none -> 92.7 us  [the longest x22 41.9 us: shift_z(): lax.ppermute(value, 'ep', [(i, (i + 2 * step) % owners) for i in range(ow...]
  transfers between devices with their start and end apart: 12 -> 95, of which waited for: 9 -> 35; matrix products, arithmetic and copies ran while one was open for 12% -> 11% of each run, Pallas kernels for 0% -> 25%
where the time goes in v3:
time: 604 us; the launch traced here: 596 us
  waiting for transfers between devices  249 us (41%)
  Pallas kernels  149 us (25%)
  starting transfers between devices  92.7 us (15%)
  other arithmetic  47.6 us (8%)
  local copies, waits for them, and re-layouts  29.6 us (5%)
  between operations  15.9 us (3%)
  matrix products  11.8 us (2%)
    ppermute x22, waiting for transfers between devices, shift_z(): lax.ppermute(value, 'ep', [(i, (i + 2 * step) % owners) for i in range(ow...  108 us
    ppermute x21, waiting for transfers between devices, swap_x(): return lax.ppermute(value, 'tp', [(i, i ^ 2) for i in range(4)])  83.8 us
    pallas_call x4, Pallas kernels, expert_call(): pl.pallas_call(lambda *refs: expert_kernel((experts, slots, blocks, rows,...  74.1 us
    ppermute x22, starting transfers between devices, shift_z(): lax.ppermute(value, 'ep', [(i, (i + 2 * step) % owners) for i in range(ow...  41.9 us
    ppermute x21, waiting for transfers between devices, swap_y(): return lax.ppermute(value, 'ep', [(i, i ^ 1) for i in range(owners)])  39.2 us
    ppermute x21, starting transfers between devices, swap_x(): return lax.ppermute(value, 'tp', [(i, i ^ 2) for i in range(4)])  23.5 us
    ppermute x21, starting transfers between devices, swap_y(): return lax.ppermute(value, 'ep', [(i, i ^ 1) for i in range(owners)])  21.8 us
    pallas_call x1, Pallas kernels, output_call(): pl.pallas_call(lambda *refs: output_kernel((experts, total // experts, bl...  21 us
  transfers between devices with their start and end apart: 95, of which 35 were waited for; matrix products, arithmetic and copies ran while one was open for 11% of the time, Pallas kernels for 25%

profile of v3, /device:TPU:0, one launch (start us, length us, event | category | flops | bytes accessed | tf_op | source)
XLA Modules:
  0.0 595.8 jit_solution(9491093247958227756)
XLA Ops:
  16.2 7.7 %collective-permute-done.1 = bf16[128,1536]{1,0:T(8,128)(2,1)S(1)} collective-permute-done((bf16[128,1536]{1,0:T(8,128)(2,1)}, bf16[128,1536]{1,0:T(8,128)(2,1)S(1)}, u32[]{:S(2)}, u32[]{:S(2)}) %collective-permute-start.1) | collective-permute-done | bytes 393248 | tf_op jit(solution)/shard_map/ppermute | solution.py:352
  51.5 13.3 %collective-permute-done.4 = bf16[128,1536]{1,0:T(8,128)(2,1)S(1)} collective-permute-done((bf16[128,1536]{1,0:T(8,128)(2,1)S(1)}, bf16[128,1536]{1,0:T(8,128)(2,1)S(1)}, u32[]{:S(2)}, u32[]{:S(2)}) %collective-permute-start.4) | collective-permute-done | bytes 393248 | tf_op jit(solution)/shard_map/ppermute | solution.py:352
  68.4 15.0 %collective-permute-done.12.refs_0_ = bf16[128,1536]{1,0:T(8,128)(2,1)} collective-permute-done((bf16[128,1536]{1,0:T(8,128)(2,1)S(1)}, bf16[128,1536]{1,0:T(8,128)(2,1)}, u32[]{:S(2)}, u32[]{:S(2)}) %collective-permute-start.12) | collective-permute-done | bytes 393248 | tf_op jit(solution)/shard_map/ppermute | solution.py:362
  89.4 18.5 %collective-permute-done.15.refs_0_ = bf16[128,1536]{1,0:T(8,128)(2,1)S(1)} collective-permute-done((bf16[128,1536]{1,0:T(8,128)(2,1)}, bf16[128,1536]{1,0:T(8,128)(2,1)S(1)}, u32[]{:S(2)}, u32[]{:S(2)}) %collective-permute-start.15) | collective-permute-done | bytes 393248 | tf_op jit(solution)/shard_map/ppermute | solution.py:362
  120.1 9.1 %collective-permute-done.18.refs_0_ = bf16[128,1536]{1,0:T(8,128)(2,1)S(1)} collective-permute-done((bf16[128,1536]{1,0:T(8,128)(2,1)S(1)}, bf16[128,1536]{1,0:T(8,128)(2,1)S(1)}, u32[]{:S(2)}, u32[]{:S(2)}) %collective-permute-start.18) | collective-permute-done | bytes 393248 | tf_op jit(solution)/shard_map/ppermute | solution.py:362
  132.6 7.8 %collective-permute-done.17.refs_2_ = bf16[128,1536]{1,0:T(8,128)(2,1)S(1)} collective-permute-done((bf16[128,1536]{1,0:T(8,128)(2,1)S(1)}, bf16[128,1536]{1,0:T(8,128)(2,1)S(1)}, u32[]{:S(2)}, u32[]{:S(2)}) %collective-permute-start.17) | collective-permute-done | bytes 393248 | tf_op jit(solution)/shard_map/ppermute | solution.py:357
  155.3 18.5 %expert_chunk.4 = (bf16[4,128,1536]{2,1,0:T(8,128)(2,1)}, bf16[4,128,1536]{2,1,0:T(8,128)(2,1)}, bf16[5,256,1536]{2,1,0:T(8,128)(2,1)}, bf16[5,256,1536]{2,1,0:T...) custom-call(bf16[128,1536]{1,0:T(8,128)(2,1)S(1)} %multiply_convert_, ...), custom_call_target="tpu_custom_call" | custom-call | flops 20132659200 | bytes 62914560 | tf_op jit(solution)/shard_map/expert_chunk/pallas_call | solution.py:649
  175.1 18.9 %expert_chunk.5 = (bf16[4,128,1536]{2,1,0:T(8,128)(2,1)}, bf16[4,128,1536]{2,1,0:T(8,128)(2,1)}, bf16[5,256,1536]{2,1,0:T(8,128)(2,1)}, bf16[5,256,1536]{2,1,0:T...) custom-call(bf16[128,1536]{1,0:T(8,128)(2,1)} %collective-permute-do, ...), custom_call_target="tpu_custom_call" | custom-call | flops 20132659200 | bytes 62914560 | tf_op jit(solution)/shard_map/expert_chunk/pallas_call | solution.py:649
  201.2 7.2 %collective-permute-done.48.refs_3_ = bf16[128,1536]{1,0:T(8,128)(2,1)S(1)} collective-permute-done((bf16[128,1536]{1,0:T(8,128)(2,1)}, bf16[128,1536]{1,0:T(8,128)(2,1)S(1)}, u32[]{:S(2)}, u32[]{:S(2)}) %collective-permute-start.48) | collective-permute-done | bytes 393248 | tf_op jit(solution)/shard_map/ppermute | solution.py:352
  219.8 18.2 %expert_chunk.7 = (bf16[4,128,1536]{2,1,0:T(8,128)(2,1)}, bf16[4,128,1536]{2,1,0:T(8,128)(2,1)}, bf16[5,256,1536]{2,1,0:T(8,128)(2,1)}, bf16[5,256,1536]{2,1,0:T...) custom-call(bf16[128,1536]{1,0:T(8,128)(2,1)S(1)} %collective-permut, ...), custom_call_target="tpu_custom_call" | custom-call | flops 20132659200 | bytes 62914560 | tf_op jit(solution)/shard_map/expert_chunk/pallas_call | solution.py:649
  239.9 18.4 %expert_chunk.6 = (bf16[4,128,1536]{2,1,0:T(8,128)(2,1)}, bf16[4,128,1536]{2,1,0:T(8,128)(2,1)}, bf16[5,256,1536]{2,1,0:T(8,128)(2,1)}, bf16[5,256,1536]{2,1,0:T...) custom-call(bf16[128,1536]{1,0:T(8,128)(2,1)S(1)} %collective-permut, ...), custom_call_target="tpu_custom_call" | custom-call | flops 20132659200 | bytes 62914560 | tf_op jit(solution)/shard_map/expert_chunk/pallas_call | solution.py:649
  260.9 21.0 %expert_output.1 = (bf16[4,512,1536]{2,1,0:T(8,128)(2,1)S(1)}, bf16[4,512,1536]{2,1,0:T(8,128)(2,1)}) custom-call(bf16[5,256,128]{2,1,0:T(8,128)(2,1)S(1)} %get-tuple-element.107.refs_0_.refs_12_, bf16[5,256,128]{2,1,0:T(8,128)(2,1)S(1)} %get-tuple-element.108.refs_1_.refs_13_, bf16[5,256,128]{2,1,0:T(8,128)(2,1)S(1)} %get-tuple-element.109.refs_2_.refs_14_, ...), custom_call_target="tpu_custom_call" | custom-call | flops 24159191040 | bytes 75497472 | tf_op jit(solution)/shard_map/expert_output/pallas_call | solution.py:717
  290.7 6.6 %collective-permute-done.42 = bf16[4,128,1536]{2,1,0:T(8,128)(2,1)S(1)} collective-permute-done((bf16[4,128,1536]{2,1,0:T(8,128)(2,1)S(1)}, bf16[4,128,1536]{2,1,0:T(8,128)(2,1)S(1)}, u32[]{:S(2)}, u32[]{:S(2)}) %collective-permute-start.42) | collective-permute-done | bytes 1572896 | tf_op jit(solution)/shard_map/ppermute | solution.py:348
  344.6 14.3 %collective-permute-done.47 = bf16[128,1536]{1,0:T(8,128)(2,1)} collective-permute-done((bf16[128,1536]{1,0:T(8,128)(2,1)}, bf16[128,1536]{1,0:T(8,128)(2,1)}, u32[]{:S(2)}, u32[]{:S(2)}) %collective-permute-start.47) | collective-permute-done | bytes 393248 | tf_op jit(solution)/shard_map/ppermute | solution.py:362
  366.1 7.3 %collective-permute-done.60.refs_2_ = bf16[128,1536]{1,0:T(8,128)(2,1)S(1)} collective-permute-done((bf16[128,1536]{1,0:T(8,128)(2,1)S(1)}, bf16[128,1536]{1,0:T(8,128)(2,1)S(1)}, u32[]{:S(2)}, u32[]{:S(2)}) %collective-permute-start.60) | collective-permute-done | bytes 393248 | tf_op jit(solution)/shard_map/ppermute | solution.py:352
  379.2 19.2 %attention_back.1 = (bf16[1536,640]{1,0:T(8,128)(2,1)}, bf16[384,1536]{1,0:T(8,128)(2,1)}, f32[2,128,1536]{2,1,0:T(8,128)}, bf16[2,128,1536]{2,1,0:T(8,128)(2,1)S(1)}) custom-call(bf16[128,1536]{1,0:T(8,128)(2,1)S(1)} %get-tuple-element.118.refs_0_, bf16[128,1536]{1,0:T(8,128)(2,1)S(1)} %collective-permute-done.59.refs_1_, ...), custom_call_target="tpu_custom_call" | custom-call | flops 24159191040 | bytes 62914560 | tf_op jit(solution)/shard_map/attention_back/pallas_call | solution.py:857
  398.5 16.7 %collective-permute-done.63 = bf16[512,1536]{1,0:T(8,128)(2,1)} collective-permute-done((bf16[512,1536]{1,0:T(8,128)(2,1)}, bf16[512,1536]{1,0:T(8,128)(2,1)}, u32[]{:S(2)}, u32[]{:S(2)}) %collective-permute-start.63) | collective-permute-done | bytes 1572896 | tf_op jit(solution)/shard_map/ppermute | solution.py:352
  436.5 17.8 %expert_weights.1 = (f32[5,1536,128]{2,1,0:T(8,128)}, f32[5,1536,128]{2,1,0:T(8,128)}, f32[5,128,1536]{2,1,0:T(8,128)}) custom-call(bf16[5,256,1536]{2,1,0:T(8,128)(2,1)} %get-tuple-element.131.refs_0_, bf16[5,256,1536]{2,1,0:T(8,128)(2,1)} %get-tuple-element.132.refs_1_, bf16[5,256,1536]{2,1,0:T(8,128)(2,1)} %get-tuple-element.133.refs_2_, ...), custom_call_target="tpu_custom_call" | custom-call | flops 6039797760 | bytes 62914560 | tf_op jit(solution)/shard_map/expert_weights/pallas_call | solution.py:751
  456.7 9.6 %collective-permute-done.70 = bf16[128,1536]{1,0:T(8,128)(2,1)S(1)} collective-permute-done((bf16[128,1536]{1,0:T(8,128)(2,1)S(1)}, bf16[128,1536]{1,0:T(8,128)(2,1)S(1)}, u32[]{:S(2)}, u32[]{:S(2)}) %collective-permute-start.70) | collective-permute-done | bytes 393248 | tf_op jit(solution)/shard_map/ppermute | solution.py:352
  474.2 16.3 %collective-permute-done.72 = bf16[128,640]{1,0:T(8,128)(2,1)S(1)} collective-permute-done((bf16[128,640]{1,0:T(8,128)(2,1)S(1)}, bf16[128,640]{1,0:T(8,128)(2,1)S(1)}, u32[]{:S(2)}, u32[]{:S(2)}) %collective-permute-start.72) | collective-permute-done | bytes 163872 | tf_op jit(solution)/shard_map/ppermute | solution.py:362
  513.3 7.1 %collective-permute-done.82 = f32[42,1536]{1,0:T(8,128)S(1)} collective-permute-done((f32[42,1536]{1,0:T(8,128)S(1)}, f32[42,1536]{1,0:T(8,128)S(1)}, u32[]{:S(2)}, u32[]{:S(2)}) %collective-permute-start.82) | collective-permute-done | bytes 258080 | tf_op jit(solution)/shard_map/ppermute | solution.py:352
  521.0 23.6 %collective-permute-done.84 = bf16[128,1536]{1,0:T(8,128)(2,1)S(1)} collective-permute-done((bf16[128,1536]{1,0:T(8,128)(2,1)S(1)}, bf16[128,1536]{1,0:T(8,128)(2,1)S(1)}, u32[]{:S(2)}, u32[]{:S(2)}) %collective-permute-start.84) | collective-permute-done | bytes 393248 | tf_op jit(solution)/shard_map/ppermute | solution.py:362
  553.6 6.4 %collective-permute-done.86 = f32[42,1536]{1,0:T(8,128)S(1)} collective-permute-done((f32[42,1536]{1,0:T(8,128)S(1)}, f32[42,1536]{1,0:T(8,128)S(1)}, u32[]{:S(2)}, u32[]{:S(2)}) %collective-permute-start.86) | collective-permute-done | bytes 258080 | tf_op jit(solution)/shard_map/ppermute | solution.py:357
  564.7 10.7 %collective-permute-done.87 = f32[42,1536]{1,0:T(8,128)S(1)} collective-permute-done((f32[42,1536]{1,0:T(8,128)S(1)}, f32[42,1536]{1,0:T(8,128)S(1)}, u32[]{:S(2)}, u32[]{:S(2)}) %collective-permute-start.87) | collective-permute-done | bytes 258080 | tf_op jit(solution)/shard_map/ppermute | solution.py:362
  (480 shorter events, 250.5 us)
Async XLA Ops:
  7.2 145.2 %all-gather.2.cloned.1.call-start = ((), (), s32[]{:S(2)}) async-start(), calls=%async_computation | async-start | bytes 14057472 | tf_op jit(solution)/shard_map/all_gather | solution.py:934
  10.8 574.7 %all-reduce.4.cloned.1.call-start = ((), (), s32[]{:S(2)}) async-start(), calls=%async_computation.1 | async-start | bytes 2359296 | tf_op jit(solution)/shard_map/psum | solution.py:1035
  83.4 24.5 %collective-permute-start.15 = (bf16[128,1536]{1,0:T(8,128)(2,1)}, bf16[128,1536]{1,0:T(8,128)(2,1)S(1)}, u32[]{:S(2)}, u32[]{:S(2)}) collective-permute-start(bf16[128,1536]{1,0:T(8,128)(2,1)} %collective-permute-done.12.refs_0_), channel_id=1, source_target_pairs={{0,8},{4,12},{8,16},{12,20},{16,24},{20,28},{24,0},{28,4},{1,9},{5... | collective-permute-start | bytes 1179656 | tf_op jit(solution)/shard_map/ppermute | solution.py:362
  86.4 26.4 %collective-permute-start.5 = (bf16[128,1536]{1,0:T(8,128)(2,1)S(1)}, bf16[128,1536]{1,0:T(8,128)(2,1)}, u32[]{:S(2)}, u32[]{:S(2)}) collective-permute-start(bf16[128,1536]{1,0:T(8,128)(2,1)S(1)} %multiply_convert_fusion.refs_0_), channel_id=1, source_target_pairs={{0,2},{1,3},{2,0},{3,1},{4,6},{5,7},{6,4},{7,5},{8,10},{9,11},{10,... | collective-permute-start | bytes 1179656 | tf_op jit(solution)/shard_map/ppermute | solution.py:352
  86.4 26.9 %collective-permute-start.6 = (bf16[128,1536]{1,0:T(8,128)(2,1)S(1)}, bf16[128,1536]{1,0:T(8,128)(2,1)}, u32[]{:S(2)}, u32[]{:S(2)}) collective-permute-start(bf16[128,1536]{1,0:T(8,128)(2,1)S(1)} %multiply_convert_fusion.refs_0_), channel_id=1, source_target_pairs={{0,4},{4,0},{8,12},{12,8},{16,20},{20,16},{24,28},{28,24},{1,5},{5... | collective-permute-start | bytes 1179656 | tf_op jit(solution)/shard_map/ppermute | solution.py:357
  87.6 31.0 %collective-permute-start.13 = (bf16[128,1536]{1,0:T(8,128)(2,1)}, bf16[128,1536]{1,0:T(8,128)(2,1)}, u32[]{:S(2)}, u32[]{:S(2)}) collective-permute-start(bf16[128,1536]{1,0:T(8,128)(2,1)} %collective-permute-done.12.refs_0_), channel_id=1, source_target_pairs={{0,2},{1,3},{2,0},{3,1},{4,6},{5,7},{6,4},{7,5},{8,10},{9,11},{10,... | collective-permute-start | bytes 1179656 | tf_op jit(solution)/shard_map/ppermute | solution.py:352
  145.9 29.2 %collective-permute-start.27 = (bf16[128,1536]{1,0:T(8,128)(2,1)}, bf16[128,1536]{1,0:T(8,128)(2,1)}, u32[]{:S(2)}, u32[]{:S(2)}) collective-permute-start(bf16[128,1536]{1,0:T(8,128)(2,1)} %collective-permute-done.12.refs_0_), channel_id=1, source_target_pairs={{0,1},{1,0},{2,3},{3,2},{4,5},{5,4},{6,7},{7,6},{8,9},{9,8},{10,11... | collective-permute-start | bytes 1179656 | tf_op jit(solution)/shard_map/ppermute | solution.py:348
  147.1 28.0 %collective-permute-start.28 = (bf16[128,1536]{1,0:T(8,128)(2,1)}, bf16[128,1536]{1,0:T(8,128)(2,1)}, u32[]{:S(2)}, u32[]{:S(2)}) collective-permute-start(bf16[128,1536]{1,0:T(8,128)(2,1)} %collective-permute-done.13.refs_1_), channel_id=1, source_target_pairs={{0,1},{1,0},{2,3},{3,2},{4,5},{5,4},{6,7},{7,6},{8,9},{9,8},{10,11... | collective-permute-start | bytes 1179656 | tf_op jit(solution)/shard_map/ppermute | solution.py:348
  147.9 27.2 %collective-permute-start.29 = (bf16[128,1536]{1,0:T(8,128)(2,1)}, bf16[128,1536]{1,0:T(8,128)(2,1)}, u32[]{:S(2)}, u32[]{:S(2)}) collective-permute-start(bf16[128,1536]{1,0:T(8,128)(2,1)} %collective-permute-done.14.refs_2_), channel_id=1, source_target_pairs={{0,1},{1,0},{2,3},{3,2},{4,5},{5,4},{6,7},{7,6},{8,9},{9,8},{10,11... | collective-permute-start | bytes 1179656 | tf_op jit(solution)/shard_map/ppermute | solution.py:348
  260.0 24.5 %collective-permute-start.56 = (bf16[128,1536]{1,0:T(8,128)(2,1)S(1)}, bf16[128,1536]{1,0:T(8,128)(2,1)S(1)}, u32[]{:S(2)}, u32[]{:S(2)}) collective-permute-start(bf16[128,1536]{1,0:T(8,128)(2,1)S(1)} %get-tuple-element.222), channel_id=1, source_target_pairs={{0,4},{4,0},{8,12},{12,8},{16,20},{20,16},{24,28},{28,24},{1,5},{5... | collective-permute-start | bytes 1179656 | tf_op jit(solution)/shard_map/ppermute | solution.py:357
  260.6 23.9 %collective-permute-start.54 = (bf16[128,1536]{1,0:T(8,128)(2,1)S(1)}, bf16[128,1536]{1,0:T(8,128)(2,1)S(1)}, u32[]{:S(2)}, u32[]{:S(2)}) collective-permute-start(bf16[128,1536]{1,0:T(8,128)(2,1)S(1)} %get-tuple-element.223), channel_id=1, source_target_pairs={{0,2},{1,3},{2,0},{3,1},{4,6},{5,7},{6,4},{7,5},{8,10},{9,11},{10,... | collective-permute-start | bytes 1179656 | tf_op jit(solution)/shard_map/ppermute | solution.py:352
  286.9 86.4 %collective-permute-start.62 = (bf16[4,512,1536]{2,1,0:T(8,128)(2,1)}, bf16[4,512,1536]{2,1,0:T(8,128)(2,1)}, u32[]{:S(2)}, u32[]{:S(2)}) collective-permute-start(bf16[4,512,1536]{2,1,0:T(8,128)(2,1)} %get-tuple-element.117), channel_id=1, source_target_pairs={{0,1},{1,0},{2,3},{3,2},{4,5},{5,4},{6,7},{7,6},{8,9},{9,8},{10,11... | collective-permute-start | bytes 18874376 | tf_op jit(solution)/shard_map/ppermute | solution.py:348
  327.6 31.3 %collective-permute-start.47 = (bf16[128,1536]{1,0:T(8,128)(2,1)}, bf16[128,1536]{1,0:T(8,128)(2,1)}, u32[]{:S(2)}, u32[]{:S(2)}) collective-permute-start(bf16[128,1536]{1,0:T(8,128)(2,1)} %join_halves.10), channel_id=1, source_target_pairs={{0,16},{4,20},{8,24},{12,28},{16,0},{20,4},{24,8},{28,12},{1,17},{... | collective-permute-start | bytes 1179656 | tf_op jit(solution)/shard_map/ppermute | solution.py:362
  331.2 27.7 %collective-permute-start.58 = (bf16[128,1536]{1,0:T(8,128)(2,1)}, bf16[128,1536]{1,0:T(8,128)(2,1)}, u32[]{:S(2)}, u32[]{:S(2)}) collective-permute-start(bf16[128,1536]{1,0:T(8,128)(2,1)} %join_halves.11), channel_id=1, source_target_pairs={{0,8},{4,12},{8,16},{12,20},{16,24},{20,28},{24,0},{28,4},{1,9},{5... | collective-permute-start | bytes 1179656 | tf_op jit(solution)/shard_map/ppermute | solution.py:362
  377.9 37.2 %collective-permute-start.63 = (bf16[512,1536]{1,0:T(8,128)(2,1)}, bf16[512,1536]{1,0:T(8,128)(2,1)}, u32[]{:S(2)}, u32[]{:S(2)}) collective-permute-start(bf16[512,1536]{1,0:T(8,128)(2,1)} %get-tuple-element.124), channel_id=1, source_target_pairs={{0,2},{1,3},{2,0},{3,1},{4,6},{5,7},{6,4},{7,5},{8,10},{9,11},{10,... | collective-permute-start | bytes 4718600 | tf_op jit(solution)/shard_map/ppermute | solution.py:352
  378.3 41.1 %collective-permute-start.64 = (bf16[512,1536]{1,0:T(8,128)(2,1)}, bf16[512,1536]{1,0:T(8,128)(2,1)}, u32[]{:S(2)}, u32[]{:S(2)}) collective-permute-start(bf16[512,1536]{1,0:T(8,128)(2,1)} %get-tuple-element.125), channel_id=1, source_target_pairs={{0,4},{4,0},{8,12},{12,8},{16,20},{20,16},{24,28},{28,24},{1,5},{5... | collective-permute-start | bytes 4718600 | tf_op jit(solution)/shard_map/ppermute | solution.py:357
  422.1 34.3 %collective-permute-start.65 = (bf16[4,128,640]{2,1,0:T(8,128)(2,1)S(1)}, bf16[4,128,640]{2,1,0:T(8,128)(2,1)S(1)}, u32[]{:S(2)}, u32[]{:S(2)}) collective-permute-start(bf16[4,128,640]{2,1,0:T(8,128)(2,1)S(1)} %dynamic-slice_bitcast_fusion.1), channel_id=1, source_target_pairs={{0,4},{4,0},{8,12},{12,8},{16,20},{20,16},{24,28},{28,24},{1,5},{5... | collective-permute-start | bytes 1966088 | tf_op jit(solution)/shard_map/ppermute | solution.py:357
  423.3 30.9 %collective-permute-start.68 = (bf16[2,64,640]{2,1,0:T(8,128)(2,1)S(1)}, bf16[2,64,640]{2,1,0:T(8,128)(2,1)S(1)}, u32[]{:S(2)}, u32[]{:S(2)}) collective-permute-start(bf16[2,64,640]{2,1,0:T(8,128)(2,1)S(1)} %get-tuple-element.233), channel_id=1, source_target_pairs={{0,24},{4,28},{8,0},{12,4},{16,8},{20,12},{24,16},{28,20},{1,25},{... | collective-permute-start | bytes 491528 | tf_op jit(solution)/shard_map/ppermute | solution.py:362
  423.4 30.9 %collective-permute-start.67 = (bf16[2,64,640]{2,1,0:T(8,128)(2,1)S(1)}, bf16[2,64,640]{2,1,0:T(8,128)(2,1)S(1)}, u32[]{:S(2)}, u32[]{:S(2)}) collective-permute-start(bf16[2,64,640]{2,1,0:T(8,128)(2,1)S(1)} %get-tuple-element.234), channel_id=1, source_target_pairs={{0,16},{4,20},{8,24},{12,28},{16,0},{20,4},{24,8},{28,12},{1,17},{... | collective-permute-start | bytes 491528 | tf_op jit(solution)/shard_map/ppermute | solution.py:362
  429.1 25.2 %collective-permute-start.66 = (bf16[2,64,640]{2,1,0:T(8,128)(2,1)S(1)}, bf16[2,64,640]{2,1,0:T(8,128)(2,1)S(1)}, u32[]{:S(2)}, u32[]{:S(2)}) collective-permute-start(bf16[2,64,640]{2,1,0:T(8,128)(2,1)S(1)} %get-tuple-element.232), channel_id=1, source_target_pairs={{0,8},{4,12},{8,16},{12,20},{16,24},{20,28},{24,0},{28,4},{1,9},{5... | collective-permute-start | bytes 491528 | tf_op jit(solution)/shard_map/ppermute | solution.py:362
  468.7 24.4 %collective-permute-start.75 = (bf16[256,1536]{1,0:T(8,128)(2,1)S(1)}, bf16[256,1536]{1,0:T(8,128)(2,1)S(1)}, u32[]{:S(2)}, u32[]{:S(2)}) collective-permute-start(bf16[256,1536]{1,0:T(8,128)(2,1)S(1)} %get-tuple-element.151), channel_id=1, source_target_pairs={{0,4},{4,0},{8,12},{12,8},{16,20},{20,16},{24,28},{28,24},{1,5},{5... | collective-permute-start | bytes 2359304 | tf_op jit(solution)/shard_map/ppermute | solution.py:357
  509.3 35.3 %collective-permute-start.84 = (bf16[128,1536]{1,0:T(8,128)(2,1)S(1)}, bf16[128,1536]{1,0:T(8,128)(2,1)S(1)}, u32[]{:S(2)}, u32[]{:S(2)}) collective-permute-start(bf16[128,1536]{1,0:T(8,128)(2,1)S(1)} %copy-done.66), channel_id=1, source_target_pairs={{0,16},{4,20},{8,24},{12,28},{16,0},{20,4},{24,8},{28,12},{1,17},{... | collective-permute-start | bytes 1179656 | tf_op jit(solution)/shard_map/ppermute | solution.py:362
  510.8 33.9 %collective-permute-start.85 = (bf16[128,1536]{1,0:T(8,128)(2,1)}, bf16[128,1536]{1,0:T(8,128)(2,1)S(1)}, u32[]{:S(2)}, u32[]{:S(2)}) collective-permute-start(bf16[128,1536]{1,0:T(8,128)(2,1)} %join_halves.15), channel_id=1, source_target_pairs={{0,8},{4,12},{8,16},{12,20},{16,24},{20,28},{24,0},{28,4},{1,9},{5... | collective-permute-start | bytes 1179656 | tf_op jit(solution)/shard_map/ppermute | solution.py:362
  551.1 24.4 %collective-permute-start.89 = (bf16[4,128,640]{2,1,0:T(8,128)(2,1)S(1)}, bf16[4,128,640]{2,1,0:T(8,128)(2,1)S(1)}, u32[]{:S(2)}, u32[]{:S(2)}) collective-permute-start(bf16[4,128,640]{2,1,0:T(8,128)(2,1)S(1)} %bitcast_dynamic-update-slice_fusion.6), channel_id=1, source_target_pairs={{0,4},{4,0},{8,12},{12,8},{16,20},{20,16},{24,28},{28,24},{1,5},{5... | collective-permute-start | bytes 1966088 | tf_op jit(solution)/shard_map/ppermute | solution.py:357
  (163 other events, 2188.7 us)
Sparse Core Ops, SparseCore 0:
  11.4 125.0 all-gather.1
  398.6 97.2 all-reduce.3

commit v4 on v3

--- a/solution.py
+++ b/solution.py
@@ -423,23 +423,17 @@
     out_ref[half:] = add_low(last_ref[...], from_x_ref[...])
 
 
-def reduce_home(first, from_y, last, from_x, steps):
-    count = len(steps)
-    half, width = first.shape[0] // count, first.shape[1]
-    total = []
-    for i in range(count):
-        half_spec = pl.BlockSpec((half, width), lambda j, i=i: (i, 0))
-        total.append(
-            pl.pallas_call(
-                join_kernel,
-                grid=(1,),
-                in_specs=[half_spec] * 4,
-                out_specs=pl.BlockSpec((2 * half, width), lambda j: (0, 0)),
-                out_shape=jax.ShapeDtypeStruct((2 * half, width), first.dtype),
-                name="join_halves",
-            )(first, from_y, last, from_x)
-        )
-    return [shift_z(total[i], -step) if step else total[i] for i, step in enumerate(steps)]
+def reduce_home(first, from_y, last, from_x):
+    half, width = first.shape
+    half_spec = pl.BlockSpec((half, width), lambda j: (0, 0))
+    return pl.pallas_call(
+        join_kernel,
+        grid=(1,),
+        in_specs=[half_spec] * 4,
+        out_specs=pl.BlockSpec((2 * half, width), lambda j: (0, 0)),
+        out_shape=jax.ShapeDtypeStruct((2 * half, width), first.dtype),
+        name="join_halves",
+    )(first, from_y, last, from_x)
 
 
 def butterfly_sum(value):
@@ -502,40 +496,30 @@
     return lax.dot_general(left, right, dims, preferred_element_type=jnp.float32)
 
 
-def store_halves(own_ref, other_ref, block, plane, result):
-    half = result.shape[0] // 2
-    count = own_ref.shape[1] // (2 * half)
-    for i in range(4):
-        (part_a, place_a), (part_b, place_b) = FIRST_HALF[i], LAST_HALF[i]
-        first = pl.ds((place_a * count + plane) * half, half)
-        last = pl.ds((place_b * count + plane) * half, half)
-        for side, ref in enumerate((own_ref, other_ref)):
-
-            @pl.when(block == side * 4 + i)
-            def _(ref=ref, first=first, last=last, part_a=part_a, part_b=part_b):
-                ref[part_a, first, :] = result[:half]
-                ref[part_b, last, :] = result[half:]
+def choose(index, values):
+    out = values[0]
+    for i in range(1, len(values)):
+        out = jnp.where(index == i, values[i], out)
+    return out
 
 
 def expert_kernel(sizes, *refs):
     experts, slots, blocks, rows, routed = sizes
     x_parts, g_ref = refs[:8], refs[8]
     base_ref, order_ref, router_ref, gate_ref, up_ref, down_ref = refs[9:15]
-    own_ref, other_ref, xr_out, gr_out, dgu_ref, wh_ref, rg_ref, picks = refs[15:23]
-    xs, gs, xr, gr, wgu, wd, back, probs, weight, d_weight, table = refs[23:34]
-    x_sem, g_sem, w_sem, out_sem = refs[34:38]
+    own_ref, other_ref, xr_out, gr_out, dgu_ref, wh_ref, rg_ref = refs[15:22]
+    xs, gs, xr, gr, wgu, wd, back, picks, probs, weight, d_weight, table, leaving, tables = refs[22:36]
+    x_sem, g_sem, w_sem, out_sem, leave_sem, t_sem = refs[36:42]
     width = xs.shape[1]
     units = wd.shape[1]
     total = experts * slots
     depth = blocks * slots
+    def source_rows(b):
+        return pl.ds(pl.multiple_of(order_ref[b] * rows, rows), rows)
+
     for b in range(blocks):
-        source = pl.ds(pl.multiple_of(order_ref[b] * rows, rows), rows)
         pltpu.make_async_copy(x_parts[b], xs.at[pl.ds(b * rows, rows)], x_sem.at[b]).start()
-        pltpu.make_async_copy(g_ref.at[source], gs.at[pl.ds(b * rows, rows)], g_sem.at[b]).start()
-    for e in range(experts):
-        pltpu.make_async_copy(gate_ref.at[e], wgu.at[e, :, pl.ds(0, units)], w_sem.at[0, e]).start()
-        pltpu.make_async_copy(up_ref.at[e], wgu.at[e, :, pl.ds(units, units)], w_sem.at[1, e]).start()
-        pltpu.make_async_copy(down_ref.at[e], wd.at[e], w_sem.at[2, e]).start()
+        pltpu.make_async_copy(g_ref.at[source_rows(b), pl.ds(width, tables.shape[2])], tables.at[b], t_sem.at[b]).start()
     rg_ref[...] = jnp.zeros_like(rg_ref)
 
     def block_rows(b):
@@ -553,7 +537,15 @@
 
     def gather_x(b, carry):
         pltpu.make_async_copy(xs.at[block_rows(b)], xs.at[block_rows(b)], x_sem.at[b]).wait()
-        pltpu.make_async_copy(gs.at[block_rows(b)], gs.at[block_rows(b)], g_sem.at[b]).wait()
+        pltpu.make_async_copy(tables.at[b], tables.at[b], t_sem.at[b]).wait()
+        pltpu.make_async_copy(g_ref.at[source_rows(b), pl.ds(0, width)], gs.at[block_rows(b)], g_sem.at[b]).start()
+
+        @pl.when(b < experts)
+        def _():
+            pltpu.make_async_copy(gate_ref.at[b], wgu.at[b, :, pl.ds(0, units)], w_sem.at[0, b]).start()
+            pltpu.make_async_copy(up_ref.at[b], wgu.at[b, :, pl.ds(units, units)], w_sem.at[1, b]).start()
+            pltpu.make_async_copy(down_ref.at[b], wd.at[b], w_sem.at[2, b]).start()
+
         x_block = xs[block_rows(b), :]
         logits = dot_f32(router_ref[...], x_block, NT)
         lane = lax.broadcasted_iota(jnp.int32, logits.shape, 0)
@@ -561,7 +553,7 @@
         expo = jnp.exp(logits - jnp.max(logits, axis=0, keepdims=True))
         prob = expo / jnp.sum(expo, axis=0, keepdims=True)
         probs[b] = prob
-        table[...] = gs[block_rows(b), width:].astype(jnp.float32).T
+        table[...] = tables[b].astype(jnp.float32).T
         hit = expand([table[pl.ds(base_ref[0] + e, 1), :] for e in range(experts)]) == place
         prob_rows = expand([prob[e : e + 1, :] for e in range(experts)])
         chosen = jnp.sum(jnp.where(hit, prob_rows, 0.0), axis=1, keepdims=True)
@@ -572,11 +564,13 @@
         for e in range(experts):
             xr[e, slot_rows(b), :] = taken[e * slots : (e + 1) * slots]
             weight[e, slot_rows(b), :] = chosen[e * slots : (e + 1) * slots]
-        back[b, pl.ds(total, router_ref.shape[0]), :] = router_ref[...]
+        back[b, pl.ds(total, router_ref.shape[0]), :width] = router_ref[...]
+        back[b, pl.ds(total, router_ref.shape[0]), width:] = jnp.zeros_like(router_ref)
         return carry
 
     def gather_g(b, carry):
-        taken = dot_f32(picks[b], gs[block_rows(b), :width]).astype(jnp.bfloat16)
+        pltpu.make_async_copy(gs.at[block_rows(b)], gs.at[block_rows(b)], g_sem.at[b]).wait()
+        taken = dot_f32(picks[b], gs[block_rows(b), :]).astype(jnp.bfloat16)
         for e in range(experts):
             gr[e, slot_rows(b), :] = taken[e * slots : (e + 1) * slots]
         return carry
@@ -605,13 +599,22 @@
         d_up = d_hidden * silu
         d_both = jnp.concatenate([d_gate, d_up], axis=1).astype(jnp.bfloat16)
         dgu_ref[e] = d_both
-        wh_ref[e] = (share * hidden).astype(jnp.bfloat16)
+        weighted = (share * hidden).astype(jnp.bfloat16)
+        wh_ref[e] = weighted
         d_rows = dot_f32(d_both, wgu[e], NT).astype(jnp.bfloat16)
         for b in range(blocks):
-            back[b, slot_rows(e), :] = d_rows[b * slots : (b + 1) * slots]
+            back[b, slot_rows(e), :width] = d_rows[b * slots : (b + 1) * slots]
+        out_rows = dot_f32(weighted, wd[e]).astype(jnp.bfloat16)
+        for b in range(blocks):
+            back[b, slot_rows(e), width:] = out_rows[b * slots : (b + 1) * slots]
         return carry
 
     lax.fori_loop(0, experts, one_expert, 0)
+
+    half = rows // 2
+
+    def left(turn):
+        pltpu.make_async_copy(leaving.at[turn], leaving.at[turn], leave_sem.at[turn]).wait()
 
     def scatter(b, carry):
         one = picks[b]
@@ -626,11 +629,30 @@
         centre = jnp.sum(prob * d_prob, axis=0, keepdims=True)
         d_logits = (prob * (d_prob - centre)).astype(jnp.bfloat16)
         rg_ref[...] += dot_f32(d_logits, xs[block_rows(b), :])
-        result = dot_f32(jnp.concatenate([one, d_logits], axis=0), back[b], TN).astype(jnp.bfloat16)
-        store_halves(own_ref, other_ref, b, 0, result)
+        turn = b % 2
+
+        @pl.when(b >= 2)
+        def _():
+            left(turn)
+
+        leaving[turn] = dot_f32(jnp.concatenate([one, d_logits], axis=0), back[b], TN).astype(jnp.bfloat16)
+        for i, table_of in enumerate((FIRST_HALF, LAST_HALF)):
+            part = choose(b % 4, [place[0] for place in table_of])
+            row = choose(b % 4, [place[1] for place in table_of]) * half
+            target = (part, pl.ds(pl.multiple_of(row, half), half))
+            for ref, mine in ((own_ref, b < 4), (other_ref, b >= 4)):
+
+                @pl.when(mine)
+                def _(ref=ref, target=target, i=i):
+                    pltpu.make_async_copy(
+                        leaving.at[turn, pl.ds(i * half, half)], ref.at[target], leave_sem.at[turn]
+                    ).start()
+
         return carry
 
     lax.fori_loop(0, blocks, scatter, 0)
+    left(0)
+    left(1)
     pltpu.make_async_copy(xr, xr_out, out_sem.at[0]).wait()
     pltpu.make_async_copy(gr, gr_out, out_sem.at[1]).wait()
 
@@ -649,85 +671,44 @@
     return pl.pallas_call(
         lambda *refs: expert_kernel((experts, slots, blocks, rows, routed), *refs),
         out_shape=(
-            jax.ShapeDtypeStruct((4, rows, width), low),
-            jax.ShapeDtypeStruct((4, rows, width), low),
+            jax.ShapeDtypeStruct((4, rows, 2 * width), low),
+            jax.ShapeDtypeStruct((4, rows, 2 * width), low),
             jax.ShapeDtypeStruct((experts, depth, width), low),
             jax.ShapeDtypeStruct((experts, depth, width), low),
             jax.ShapeDtypeStruct((experts, depth, 2 * units), low),
             jax.ShapeDtypeStruct((experts, depth, units), low),
             jax.ShapeDtypeStruct((padded, width), full),
-            jax.ShapeDtypeStruct((blocks, experts * slots, rows), low),
         ),
         in_specs=[any_spec] * 9 + [smem_spec, smem_spec, vmem_spec] + [any_spec] * 3,
-        out_specs=(vmem_spec, vmem_spec, any_spec, any_spec) + (vmem_spec,) * 4,
+        out_specs=(any_spec,) * 4 + (vmem_spec,) * 3,
         scratch_shapes=[
             pltpu.VMEM((blocks * rows, width), low),
-            pltpu.VMEM((blocks * rows, width + extra), low),
+            pltpu.VMEM((blocks * rows, width), low),
             pltpu.VMEM((experts, depth, width), low),
             pltpu.VMEM((experts, depth, width), low),
             pltpu.VMEM((experts, width, 2 * units), low),
             pltpu.VMEM((experts, units, width), low),
-            pltpu.VMEM((blocks, experts * slots + padded, width), low),
+            pltpu.VMEM((blocks, experts * slots + padded, 2 * width), low),
+            pltpu.VMEM((blocks, experts * slots, rows), low),
             pltpu.VMEM((blocks, padded, rows), full),
             pltpu.VMEM((experts, depth, rows), full),
             pltpu.VMEM((experts, depth, rows), full),
             pltpu.VMEM((extra, rows), full),
+            pltpu.VMEM((2, rows, 2 * width), low),
+            pltpu.VMEM((blocks, rows, extra), low),
             pltpu.SemaphoreType.DMA((blocks,)),
             pltpu.SemaphoreType.DMA((blocks,)),
             pltpu.SemaphoreType.DMA((3, experts)),
             pltpu.SemaphoreType.DMA((2,)),
+            pltpu.SemaphoreType.DMA((2,)),
+            pltpu.SemaphoreType.DMA((blocks,)),
         ],
-        compiler_params=pltpu.CompilerParams(vmem_limit_bytes=50 * 2**20),
+        compiler_params=pltpu.CompilerParams(vmem_limit_bytes=58 * 2**20),
         cost_estimate=pl.CostEstimate(
             flops=2 * experts * depth * width * units * 40, bytes_accessed=60 * 2**20, transcendentals=0
         ),
         name="expert_chunk",
     )(*x_parts, g_all, base, order, router_rows, gate_weight, up_weight, down_weight)
-
-
-def output_kernel(sizes, *refs):
-    experts, slots, blocks, planes = sizes
-    weighted, picks = refs[:planes], refs[planes : 2 * planes]
-    down_ref, own_ref, other_ref, rows_ref = refs[2 * planes :]
-    for plane in range(planes):
-
-        def one_expert(e, carry, plane=plane):
-            result = dot_f32(weighted[plane][e], down_ref[e]).astype(jnp.bfloat16)
-            for b in range(blocks):
-                rows_ref[b, pl.ds(pl.multiple_of(e * slots, slots), slots), :] = result[b * slots : (b + 1) * slots]
-            return carry
-
-        lax.fori_loop(0, experts, one_expert, 0)
-
-        def scatter(b, carry, plane=plane):
-            result = dot_f32(picks[plane][b], rows_ref[b], TN).astype(jnp.bfloat16)
-            store_halves(own_ref, other_ref, b, plane, result)
-            return carry
-
-        lax.fori_loop(0, blocks, scatter, 0)
-
-
-def output_call(weighted, picks, down_weight):
-    planes = len(weighted)
-    experts, depth, units = weighted[0].shape
-    width = down_weight.shape[2]
-    blocks, total, rows = picks[0].shape
-    boxes = jax.ShapeDtypeStruct((4, planes * rows, width), jnp.bfloat16)
-    vmem_spec = pl.BlockSpec(memory_space=pltpu.VMEM)
-    return pl.pallas_call(
-        lambda *refs: output_kernel((experts, total // experts, blocks, planes), *refs),
-        in_specs=[vmem_spec] * (2 * planes + 1),
-        out_specs=(vmem_spec,) * 2,
-        out_shape=(boxes, boxes),
-        scratch_shapes=[pltpu.VMEM((blocks, total, width), jnp.bfloat16)],
-        compiler_params=pltpu.CompilerParams(vmem_limit_bytes=40 * 2**20),
-        cost_estimate=pl.CostEstimate(
-            flops=2 * planes * experts * depth * width * units * 12,
-            bytes_accessed=planes * 18 * 2**20,
-            transcendentals=0,
-        ),
-        name="expert_output",
-    )(*weighted, *picks, down_weight)
 
 
 def weight_kernel(count, *refs):
@@ -772,27 +753,59 @@
     )
 
 
+def branch_back_kernel(*refs):
+    parts, me_ref, att_ref, wo_ref, back_ref, out_ref, branch, sem = refs[:4], *refs[4:]
+    rows = parts[0].shape[0]
+    for flip, part in enumerate(parts):
+        target = pl.ds(pl.multiple_of((me_ref[0] ^ flip) * rows, rows), rows)
+        pltpu.make_async_copy(part, branch.at[target], sem.at[flip]).start()
+    for flip, part in enumerate(parts):
+        target = pl.ds(pl.multiple_of((me_ref[0] ^ flip) * rows, rows), rows)
+        pltpu.make_async_copy(part, branch.at[target], sem.at[flip]).wait()
+    out_part = dot_f32(att_ref[...], branch[...], TN).astype(jnp.bfloat16)
+    _, planes, size, _ = out_ref.shape
+    for i in range(2 * planes):
+        out_ref[me_ref[1] ^ (i // planes), i % planes] = out_part[i * size : (i + 1) * size]
+    back_ref[...] = dot_f32(branch[...], wo_ref[...], NT).astype(jnp.bfloat16)
+
+
+def branch_back_call(parts, attended, wo):
+    rows, width = parts[0].shape
+    seq_len, q_width = attended.shape
+    planes = lax.axis_size("ep") // 2
+    me = jnp.stack([lax.axis_index("tp"), lax.axis_index("ep") % 2]).astype(jnp.int32)
+    vmem_spec = pl.BlockSpec(memory_space=pltpu.VMEM)
+    return pl.pallas_call(
+        branch_back_kernel,
+        out_shape=(
+            jax.ShapeDtypeStruct((seq_len, q_width), jnp.bfloat16),
+            jax.ShapeDtypeStruct((2, planes, q_width // planes // 2, width), jnp.bfloat16),
+        ),
+        in_specs=[pl.BlockSpec(memory_space=pl.ANY)] * 4 + [pl.BlockSpec(memory_space=pltpu.SMEM)] + [vmem_spec] * 2,
+        out_specs=(vmem_spec,) * 2,
+        scratch_shapes=[pltpu.VMEM((seq_len, width), jnp.bfloat16), pltpu.SemaphoreType.DMA((4,))],
+        compiler_params=pltpu.CompilerParams(vmem_limit_bytes=24 * 2**20),
+        cost_estimate=pl.CostEstimate(
+            flops=4 * seq_len * width * q_width, bytes_accessed=8 * 2**20, transcendentals=0
+        ),
+        name="branch_back",
+    )(*parts, me, attended, wo)
+
+
 def attention_back_kernel(sizes, *refs):
     group_factor, head_size = sizes
-    parts, me_ref = refs[:4], refs[4]
-    att_ref, q_ref, k_ref, v_ref, normed_ref, wo_ref, wq_ref, wk_ref, wv_ref = refs[5:14]
-    cos_ref, sin_ref, column_ref, row_ref, live_ref = refs[14:19]
-    weights_ref, out_ref, stay_ref, leave_ref = refs[19:23]
-    branch, back, d_q, d_k, d_v, d_all, sem = refs[23:30]
-    rows = parts[0].shape[0]
-    seq_len = branch.shape[0]
+    me_ref, back, q_ref, k_ref, v_ref, normed_ref, wq_ref, wk_ref, wv_ref = refs[:9]
+    cos_ref, sin_ref, column_ref, row_ref, live_ref = refs[9:14]
+    upper_ref, lower_ref, stay_ref, leave_ref = refs[14:18]
+    d_q, d_k, d_v, d_all = refs[18:22]
+    seq_len = q_ref.shape[0]
+    rows = stay_ref.shape[1]
     factor = 1.0 / math.sqrt(head_size)
     me = me_ref[0]
 
     def place(flip):
         return pl.ds(pl.multiple_of((me ^ flip) * rows, rows), rows)
 
-    for flip, part in enumerate(parts):
-        pltpu.make_async_copy(part, branch.at[place(flip)], sem.at[flip]).start()
-    for flip, part in enumerate(parts):
-        pltpu.make_async_copy(part, branch.at[place(flip)], sem.at[flip]).wait()
-    back[...] = dot_f32(branch[...], wo_ref[...], NT).astype(jnp.bfloat16)
-    out_ref[...] = dot_f32(att_ref[...], branch[...], TN).astype(jnp.bfloat16)
     d_k[...] = jnp.zeros_like(d_k)
     d_v[...] = jnp.zeros_like(d_v)
     step = seq_len // 2
@@ -829,10 +842,15 @@
             flat = turned * cos_ref[...] + swap_halves(turned, head_size // 2) * sin_ref[...]
             d_all[:, offset + i * pair : offset + (i + 1) * pair] = flat.astype(jnp.bfloat16)
     d_all[:, q_width + kv_width :] = d_v[...].astype(jnp.bfloat16)
-    width = normed_ref.shape[1]
-    for i in range(4):
-        features = slice(i * width // 4, (i + 1) * width // 4)
-        weights_ref[features, :] = dot_f32(normed_ref[:, features], d_all[...], TN).astype(jnp.bfloat16)
+    plane, side = me_ref[1], me_ref[2]
+    planes, size = lower_ref.shape[0], lower_ref.shape[1]
+    for i in range(3 * planes):
+        features = slice(i * size, (i + 1) * size)
+        part = dot_f32(normed_ref[:, features], d_all[...], TN).astype(jnp.bfloat16)
+        if i < 2 * planes:
+            upper_ref[side ^ (i // planes), i % planes] = part
+        else:
+            lower_ref[(i + planes - plane) % planes] = part
     for flip in range(4):
         values = d_all[place(flip), :]
         total = dot_f32(values[:, :q_width], wq_ref[...], NT)
@@ -844,34 +862,33 @@
             stay_ref[flip // 2] = total
 
 
-def attention_back_call(parts, attended, query, key, value, normed, wo, wq, wk, wv, cos, sin, segments, live, factor):
-    rows, width = parts[0].shape
+def attention_back_call(back, query, key, value, normed, wq, wk, wv, cos, sin, segments, live, factor):
     seq_len, q_width = query.shape
-    kv_width = key.shape[1]
-    me = lax.axis_index("tp").astype(jnp.int32)[None]
+    width, kv_width = wk.shape
+    rows = seq_len // 4
+    owner = lax.axis_index("ep")
+    planes = lax.axis_size("ep") // 2
+    size = width // (3 * planes)
+    me = jnp.stack([lax.axis_index("tp"), owner // 2, owner % 2]).astype(jnp.int32)
     low, full = jnp.bfloat16, jnp.float32
-    any_spec = pl.BlockSpec(memory_space=pl.ANY)
     vmem_spec = pl.BlockSpec(memory_space=pltpu.VMEM)
     cos_pair = jnp.tile(cos, (1, 4))
     sin_pair = jnp.tile(jnp.concatenate([sin, -sin], axis=1), (1, 2))
     return pl.pallas_call(
         lambda *refs: attention_back_kernel((factor, HEAD_SIZE_DIM), *refs),
         out_shape=(
-            jax.ShapeDtypeStruct((width, q_width + 2 * kv_width), low),
-            jax.ShapeDtypeStruct((q_width, width), low),
+            jax.ShapeDtypeStruct((2, planes, size, q_width + 2 * kv_width), low),
+            jax.ShapeDtypeStruct((planes, size, q_width + 2 * kv_width), low),
             jax.ShapeDtypeStruct((2, rows, width), full),
             jax.ShapeDtypeStruct((2, rows, width), low),
         ),
-        in_specs=[any_spec] * 4 + [pl.BlockSpec(memory_space=pltpu.SMEM)] + [vmem_spec] * 14,
+        in_specs=[pl.BlockSpec(memory_space=pltpu.SMEM)] + [vmem_spec] * 13,
         out_specs=(vmem_spec,) * 4,
         scratch_shapes=[
-            pltpu.VMEM((seq_len, width), low),
-            pltpu.VMEM((seq_len, q_width), low),
             pltpu.VMEM((seq_len, q_width), full),
             pltpu.VMEM((seq_len, kv_width), full),
             pltpu.VMEM((seq_len, kv_width), full),
             pltpu.VMEM((seq_len, q_width + 2 * kv_width), low),
-            pltpu.SemaphoreType.DMA((4,)),
         ],
         compiler_params=pltpu.CompilerParams(vmem_limit_bytes=48 * 2**20),
         cost_estimate=pl.CostEstimate(
@@ -881,7 +898,7 @@
         ),
         name="attention_back",
     )(
-        *parts, me, attended, query, key, value, normed, wo, wq, wk, wv, cos_pair, sin_pair,
+        me, back, query, key, value, normed, wq, wk, wv, cos_pair, sin_pair,
         segments.reshape(-1, 1), segments.reshape(1, -1), live.reshape(1, -1),
     )
 
@@ -977,106 +994,162 @@
     )
     middle = x_float + branch
     moe_in = rms_norm(middle, moe_gain).astype(jnp.bfloat16)
-    column, x_chunks = moe_in, []
-    for i in range(planes):
-        column = shift_z(column, 1) if i else column
-        across, along = swap_x(column), swap_y(column)
-        diagonal = swap_x(along) if i % 2 else swap_y(across)
-        parts = (column, across, along, diagonal)
-        x_chunks.append(parts + tuple(swap_core(part) for part in parts))
-    kept, boxes, sends, halves = [], [], [], []
-
-    def second(i):
-        first, first_sent, last, last_sent = reduce_second(boxes[i], swap_x(sends[i][0]), swap_y(sends[i][1]))
-        halves.append((first, swap_y(first_sent), last, swap_x(last_sent)))
-        return first_sent, last_sent
-
-    for i in range(planes):
-        ready = [part for chunk in x_chunks for part in chunk[1:3]] if i == 0 else []
-        if i >= 2:
-            sends.append(reduce_sends(boxes[i - 2]))
-            ready += [*sends[i - 2]]
-        if i >= 3:
-            ready += second(i - 3)
-        own, other, *rest = expert_call(
-            x_chunks[i], g_all, base, order[i], after(router_rows, *ready),
-            gate_weight, up_weight, down_weight, experts_all, slots,
-        )
-        kept.append(rest)
-        boxes.append(reduce_first(own, other))
-    xr, gr, dgu, wh, router_parts, picks = zip(*kept)
-    pairs = planes
-    grad_parts = []
-    for i in range(planes):
-        if i >= len(sends):
-            sends.append(reduce_sends(boxes[i]))
-        if i == planes - 1:
-            own, other = output_call((after(wh[0], *sends[i]),) + wh[1:], picks, down_weight)
-        if i >= len(halves):
-            sent_on = second(i)
-        if i == planes - 1:
-            out_boxes = [reduce_first(own, after(other, *sent_on))]
-        grad_parts += reduce_home(*halves[i], (i,))
-    grad_moe_in = sum(part.astype(jnp.float32) for part in grad_parts)
+    barrier = lax.optimization_barrier
+    columns, cross, diagonal, swapped, far = [moe_in], {}, {}, {}, {}
+
+    def send_cross(step):
+        cross[step] = (swap_x(columns[step]), swap_y(columns[step]))
+
+    def send_diagonal(step):
+        diagonal[step] = swap_x(cross[step][1]) if step % 2 else swap_y(cross[step][0])
+
+    def send_swapped(step):
+        swapped[step] = tuple(swap_core(part) for part in (columns[step], *cross[step]))
+
+    send_cross(0)
+    columns.append(shift_z(columns[0], 1))
+    columns[1], cross = barrier((columns[1], cross))
+    send_cross(1)
+    columns.append(shift_z(columns[1], 1))
+    columns[2], cross = barrier((columns[2], cross))
+    send_diagonal(1)
+    send_swapped(1)
+    send_cross(2)
+    columns.append(shift_z(columns[2], 1))
+    columns[3], cross, diagonal, swapped = barrier((columns[3], cross, diagonal, swapped))
+    far[1] = swap_core(diagonal[1])
+    turns = [*range(1, planes), 0]
+    kept, grad_parts = [], []
+    own, other, arrived, from_x, from_y, halves, second, home = {}, {}, {}, {}, {}, {}, {}, {}
+    for stage in range(planes + 4):
+        ready, sends, joined = [], None, None
+        a, b, c = stage - 2, stage - 3, stage - 4
+        if a in arrived:
+            sends = reduce_sends((own[a], arrived[a]))
+            ready += sends
+        if b in from_x:
+            halves[b] = reduce_second((own[b], arrived[b]), from_x[b], from_y[b])
+            ready += halves[b]
+        if c in second:
+            joined = reduce_home(halves[c][0], second[c][0], halves[c][2], second[c][1])
+            ready += [joined]
+            if turns[c] == 0:
+                grad_parts.append(joined)
+                joined = None
+        came = {}
+        if stage < planes:
+            step = turns[stage]
+            x_parts = (columns[step], *cross[step], diagonal[step], *swapped[step], far[step])
+            if stage == 0:
+                send_diagonal(2)
+                send_cross(3)
+                send_swapped(2)
+                came["gather"] = (diagonal[2], cross[3], swapped[2])
+            if stage == 1:
+                send_diagonal(3)
+                send_diagonal(0)
+                send_swapped(3)
+                came["gather"] = (diagonal[3], diagonal[0], swapped[3])
+            if stage == 2:
+                send_swapped(0)
+                came["gather"] = (swapped[0],)
+            own[stage], other[stage], *rest = expert_call(
+                x_parts, g_all, base, order[step], after(router_rows, *ready),
+                gate_weight, up_weight, down_weight, experts_all, slots,
+            )
+            kept.append(rest)
+            came["kernel"] = (own[stage], other[stage])
+        if stage == planes:
+            xr, gr, dgu, wh, router_parts = zip(*kept)
+            came["weights"] = weight_call(xr, gr, (after(dgu[0], *ready),) + dgu[1:], wh)
+        if stage - 1 in other:
+            came["core"] = swap_core(other[stage - 1])
+        if sends:
+            came["cross"] = (swap_x(sends[0]), swap_y(sends[1]))
+        if b in halves:
+            came["second"] = (swap_y(halves[b][1]), swap_x(halves[b][3]))
+        if joined is not None:
+            came["home"] = shift_z(joined, -turns[c])
+        came = barrier(came)
+        if stage == 0:
+            diagonal[2], cross[3], swapped[2] = came["gather"]
+            far[2] = swap_core(diagonal[2])
+        if stage == 1:
+            diagonal[3], diagonal[0], swapped[3] = came["gather"]
+            far[3], far[0] = swap_core(diagonal[3]), swap_core(diagonal[0])
+        if stage == 2:
+            (swapped[0],) = came["gather"]
+        if "kernel" in came:
+            own[stage], other[stage] = came["kernel"]
+        if "weights" in came:
+            gate_grad, up_grad, down_grad = came["weights"]
+        if "core" in came:
+            arrived[stage - 1] = came["core"]
+        if "cross" in came:
+            from_x[a], from_y[a] = came["cross"]
+        if "second" in came:
+            second[b] = came["second"]
+        if "home" in came:
+            grad_parts.append(came["home"])
+    grad_moe_in = sum(part[:, :width].astype(jnp.float32) for part in grad_parts)
+    expert_sum = sum(part[:, width:].astype(jnp.float32) for part in grad_parts)
+    output = (middle + expert_sum).astype(jnp.bfloat16)
     router_part = jnp.roll(sum(router_parts)[:experts_all], owner * local_experts, axis=0)
     grad_out = cotangent.astype(jnp.float32)
     _, norm_two_back = jax.vjp(rms_norm, middle, moe_gain)
     grad_mid_norm, moe_gain_grad = norm_two_back(grad_moe_in)
     grad_middle = grad_out + grad_mid_norm
     branch_parts = gather_pieces(grad_middle.astype(jnp.bfloat16))
-    out_sends = [reduce_sends(box) for box in out_boxes]
-    branch_parts, out_sends = lax.optimization_barrier((branch_parts, out_sends))
-    out_from = [(swap_x(to_x), swap_y(to_y)) for to_x, to_y in out_sends]
     flat = lambda array: array.reshape(seq_len, -1)
-    weights, out_grad, stay, leave = attention_back_call(
-        branch_parts, attended, flat(query_val), flat(key_val), flat(value_vectors), normed_all,
-        out_weight, query_matrix, key_matrix, value_matrix, cos_table, sin_table, segment_row, live_row, group_factor,
-    )
-    out_grad = lax.psum(out_grad, "ep")
-    weights, leave, out_from = lax.optimization_barrier((weights, leave, out_from))
-    cut = weights.shape[0] * 2 // 3
-    columns = weights.shape[1]
-    upper_own, upper_leave = sides_of(weights[:cut].reshape(2, planes, -1, columns))
-    lower_parts = planes_of(weights[cut:].reshape(planes, 2, -1, columns))
-    upper_came = swap_y(upper_leave)
-    lower_came = send_planes(lower_parts)
+    back, out_grad = branch_back_call(branch_parts, attended, out_weight)
+    out_came = swap_y(out_grad[1])
+    upper, lower, stay, leave = attention_back_call(
+        back, flat(query_val), flat(key_val), flat(value_vectors), normed_all,
+        query_matrix, key_matrix, value_matrix, cos_table, sin_table, segment_row, live_row, group_factor,
+    )
+    upper, lower, stay, leave, out_came = barrier((upper, lower, stay, leave, out_came))
+    out_parts = planes_of(add_low(out_grad[0], out_came))
+    out_came = send_planes(out_parts)
+    small = jnp.concatenate([router_part, moe_gain_grad[None]], axis=0)
+    upper_came = swap_y(upper[1])
+    lower_came = send_planes(lower)
     both = stay + swap_core(leave).astype(jnp.float32)
     across_came = swap_x(both[1].astype(jnp.bfloat16))
-    out_second = [reduce_second(box, *came) for box, came in zip(out_boxes, out_from)]
-    gate_grad, up_grad, down_grad = weight_call(xr, gr, (after(dgu[0], leave),) + dgu[1:], wh)
-    upper_parts = planes_of(add_low(upper_own, upper_came))
-    lower_own, lower_leave = sides_of(add_all(lower_parts[0], lower_came).astype(jnp.bfloat16))
-    upper_parts, lower_leave, across_came, out_second, down_grad = lax.optimization_barrier(
-        (upper_parts, lower_leave, across_came, out_second, down_grad)
-    )
-    upper_came = send_planes(upper_parts)
-    lower_came = swap_y(lower_leave)
-    out_third = [(first, swap_y(first_sent), last, swap_x(last_sent)) for first, first_sent, last, last_sent in out_second]
+    small = small + swap_core(small)
+    upper_came, lower_came, across_came, small, out_came = barrier((upper_came, lower_came, across_came, small, out_came))
+    out_sum = add_all(out_parts[0], out_came).astype(jnp.bfloat16)
+    out_came = spread_planes(out_sum)
+    upper_parts = planes_of(add_low(upper[0], upper_came))
+    lower_parts = add_all(lower[0], lower_came).astype(jnp.bfloat16).reshape(2, -1, lower.shape[-1])
+    lower_own, lower_leave = sides_of(lower_parts)
     grad_normed = both[0] + across_came.astype(jnp.float32)
     _, norm_one_back = jax.vjp(rms_norm, x_float, norm_gain)
     grad_x_norm, norm_gain_grad = norm_one_back(grad_normed)
     input_grad = grad_middle + grad_x_norm
-    small = jnp.concatenate([router_part, moe_gain_grad[None], norm_gain_grad[None]], axis=0)
+    gain_part = norm_gain_grad[None]
+    gain_part = gain_part + swap_core(gain_part)
+    small = jnp.concatenate([small, gain_part], axis=0)
+    small = small + swap_x(small)
+    small = small + swap_y(small)
+    upper_came = send_planes(upper_parts)
+    lower_came = swap_y(lower_leave)
+    upper_came, lower_came, small, out_came = barrier((upper_came, lower_came, small, out_came))
+    out_half = join_planes(out_came)
+    out_came = swap_y(out_half)
     upper_sum = add_all(upper_parts[0], upper_came).astype(jnp.bfloat16)
     lower_sum = add_low(lower_own, lower_came)
-    upper_sum, lower_sum, out_third, small = lax.optimization_barrier((upper_sum, lower_sum, out_third, small))
-    out_parts = []
-    for i, third in enumerate(out_third):
-        out_parts += reduce_home(*third, tuple(range(i * pairs, (i + 1) * pairs)))
     upper_came = spread_planes(upper_sum)
     lower_came = swap_y(lower_sum)
-    small = small + swap_core(small)
-    small = small + swap_x(small)
+    small_came = spread_planes(small)
+    upper_came, lower_came, small_came, out_came = barrier((upper_came, lower_came, small_came, out_came))
     upper_half, lower_half = join_planes(upper_came), join_sides(lower_sum, lower_came)
-    upper_half, lower_half, small, out_parts = lax.optimization_barrier((upper_half, lower_half, small, out_parts))
+    small = sum(small_came)
     upper_came = swap_y(upper_half)
     lower_came = spread_planes(lower_half)
-    output = (middle + sum(part.astype(jnp.float32) for part in out_parts)).astype(jnp.bfloat16)
-    small = small + swap_y(small)
-    small = small + shift_z(small, 2)
-    small = small + lax.ppermute(small, "ep", [(i, i ^ 2) for i in range(owners)])
-    out_grad = after(out_grad, small).astype(jnp.float32)
-    upper = join_sides(upper_half, upper_came).reshape(cut, columns)
+    upper_came, lower_came = barrier((upper_came, lower_came))
+    out_grad = join_sides(out_half, out_came).reshape(-1, width).astype(jnp.float32)
+    columns = upper_half.shape[-1]
+    upper = join_sides(upper_half, upper_came).reshape(-1, columns)
     lower = join_planes(lower_came).reshape(-1, columns)
     weights = jnp.concatenate([upper, lower], axis=0).astype(jnp.float32)
     q_width, kv_width = query_matrix.shape[1], key_matrix.shape[1]

time: 604 us -> 551 us (0.912)
  waiting for transfers between devices: 249 us -> 206 us
  Pallas kernels: 149 us -> 130 us
  starting transfers between devices: 92.7 us -> 105 us
  local copies, waits for them, and re-layouts: 29.6 us -> 18 us
    ppermute x21 -> x19, waiting for transfers between devices: 83.8 us -> 38.1 us  [swap_x(): return lax.ppermute(value, 'tp', [(i, i ^ 2) for i in range(4)])]
    ppermute x21, waiting for transfers between devices: 39.2 us -> 70.9 us  [swap_y(): return lax.ppermute(value, 'ep', [(i, i ^ 1) for i in range(owners)])]
    ppermute x22 -> x27, waiting for transfers between devices: 108 us -> 88.2 us  [shift_z(): lax.ppermute(value, 'ep', [(i, (i + 2 * step) % owners) for i in range(ow...]
    pallas_call x1, Pallas kernels: 21 us -> 3.19 us  [branch_back_call(): pl.pallas_call(branch_back_kernel, out_shape=(jax.ShapeDtypeStruct((seq_l...]
    pallas_call x4, Pallas kernels: 74.1 us -> 84.3 us  [expert_call(): pl.pallas_call(lambda *refs: expert_kernel((experts, slots, blocks, rows,...]
    unnamed x184 -> x138, local copies, waits for them, and re-layouts: 15.7 us -> 5.63 us
    ppermute x22 -> x27, starting transfers between devices: 41.9 us -> 50.2 us  [shift_z(): lax.ppermute(value, 'ep', [(i, (i + 2 * step) % owners) for i in range(ow...]
    pallas_call x8 -> x4, Pallas kernels: 16.7 us -> 9.64 us  [reduce_home(): pl.pallas_call(join_kernel, grid=(1,), in_specs=[half_spec] * 4, out_spec...]
  transfers between devices with their start and end apart: 95 -> 96, of which waited for: 35 -> 35; matrix products, arithmetic and copies ran while one was open for 11% -> 13% of each run, Pallas kernels for 25% -> 23%
where the time goes in v4:
time: 551 us; the launch traced here: 543 us
  waiting for transfers between devices  206 us (37%)
  Pallas kernels  130 us (24%)
  starting transfers between devices  105 us (19%)
  other arithmetic  52.9 us (10%)
  local copies, waits for them, and re-layouts  18 us (3%)
  between operations  15.9 us (3%)
  matrix products  14.5 us (3%)
    ppermute x27, waiting for transfers between devices, shift_z(): lax.ppermute(value, 'ep', [(i, (i + 2 * step) % owners) for i in range(ow...  88.2 us
    pallas_call x4, Pallas kernels, expert_call(): pl.pallas_call(lambda *refs: expert_kernel((experts, slots, blocks, rows,...  84.3 us
    ppermute x21, waiting for transfers between devices, swap_y(): return lax.ppermute(value, 'ep', [(i, i ^ 1) for i in range(owners)])  70.9 us
    ppermute x27, starting transfers between devices, shift_z(): lax.ppermute(value, 'ep', [(i, (i + 2 * step) % owners) for i in range(ow...  50.2 us
    ppermute x19, waiting for transfers between devices, swap_x(): return lax.ppermute(value, 'tp', [(i, i ^ 2) for i in range(4)])  38.1 us
    ppermute x21, starting transfers between devices, swap_y(): return lax.ppermute(value, 'ep', [(i, i ^ 1) for i in range(owners)])  24.8 us
    ppermute x19, starting transfers between devices, swap_x(): return lax.ppermute(value, 'tp', [(i, i ^ 2) for i in range(4)])  24.2 us
    pallas_call x1, Pallas kernels, weight_call(): pl.pallas_call(lambda *refs: weight_kernel(count, *refs), grid=(experts,)...  17.6 us
  transfers between devices with their start and end apart: 96, of which 35 were waited for; matrix products, arithmetic and copies ran while one was open for 13% of the time, Pallas kernels for 23%

profile of v4, /device:TPU:0, one launch (start us, length us, event | category | flops | bytes accessed | tf_op | source)
XLA Modules:
  0.0 542.6 jit_solution(4509162472259314394)
XLA Ops:
  16.8 7.0 %collective-permute-done.1 = bf16[128,1536]{1,0:T(8,128)(2,1)S(1)} collective-permute-done((bf16[128,1536]{1,0:T(8,128)(2,1)}, bf16[128,1536]{1,0:T(8,128)(2,1)S(1)}, u32[]{:S(2)}, u32[]{:S(2)}) %collective-permute-start.1) | collective-permute-done | bytes 393248 | tf_op jit(solution)/shard_map/ppermute | solution.py:352
  32.8 6.1 %fusion.84 = (f32[2,3,512]{2,1,0:T(4,128)S(1)}, f32[2,3,512,512]{2,3,1,0:T(8,128)}) fusion(pred[512,512]{0,1:T(8,128)(4,1)} %fusion.16, bf16[512,2,32]{0,2,1:T(8,128)(2,1)} %get-tuple-element.361, bf16[512,2,32]{0,2,1:T(8,128)(2,1)S(1)} %get-tuple-element.360, bf16[512,2,3,32]{0,3,2,1:T(8,128)(2,1)S(1)} %get-tuple-element.349, ...), kind=kOutput, calls=%fused_computation.220 | convolution fusion | flops 208667136 | bytes 7090176 | tf_op jit(solution)/shard_map/sub | solution.py:985
  55.4 9.6 %collective-permute-done.4 = bf16[128,1536]{1,0:T(8,128)(2,1)S(1)} collective-permute-done((bf16[128,1536]{1,0:T(8,128)(2,1)}, bf16[128,1536]{1,0:T(8,128)(2,1)S(1)}, u32[]{:S(2)}, u32[]{:S(2)}) %collective-permute-start.4) | collective-permute-done | bytes 393248 | tf_op jit(solution)/shard_map/ppermute | solution.py:352
  72.8 15.7 %collective-permute-done.5.refs_0_ = bf16[128,1536]{1,0:T(8,128)(2,1)} collective-permute-done((bf16[128,1536]{1,0:T(8,128)(2,1)S(1)}, bf16[128,1536]{1,0:T(8,128)(2,1)}, u32[]{:S(2)}, u32[]{:S(2)}) %collective-permute-start.5) | collective-permute-done | bytes 393248 | tf_op jit(solution)/shard_map/ppermute | solution.py:362
  98.8 11.9 %collective-permute-done.10.refs_2_ = bf16[128,1536]{1,0:T(8,128)(2,1)} collective-permute-done((bf16[128,1536]{1,0:T(8,128)(2,1)}, bf16[128,1536]{1,0:T(8,128)(2,1)}, u32[]{:S(2)}, u32[]{:S(2)}) %collective-permute-start.10) | collective-permute-done | bytes 393248 | tf_op jit(solution)/shard_map/ppermute | solution.py:357
  118.0 17.3 %collective-permute-done.11.refs_0_ = bf16[128,1536]{1,0:T(8,128)(2,1)} collective-permute-done((bf16[128,1536]{1,0:T(8,128)(2,1)}, bf16[128,1536]{1,0:T(8,128)(2,1)}, u32[]{:S(2)}, u32[]{:S(2)}) %collective-permute-start.11) | collective-permute-done | bytes 393248 | tf_op jit(solution)/shard_map/ppermute | solution.py:362
  142.6 21.2 %expert_chunk.4 = (bf16[4,128,3072]{2,1,0:T(8,128)(2,1)}, bf16[4,128,3072]{2,1,0:T(8,128)(2,1)}, bf16[5,256,1536]{2,1,0:T(8,128)(2,1)}, bf16[5,256,1536]{2,1,0:T...) custom-call(bf16[128,1536]{1,0:T(8,128)(2,1)} %collective-permute-done.5.refs_0_, ...), custom_call_target="tpu_custom_call" | custom-call | flops 20132659200 | bytes 62914560 | tf_op jit(solution)/shard_map/expert_chunk/pallas_call | solution.py:671
  166.8 8.8 %collective-permute-done.27.refs_3_ = bf16[128,1536]{1,0:T(8,128)(2,1)} collective-permute-done((bf16[128,1536]{1,0:T(8,128)(2,1)S(1)}, bf16[128,1536]{1,0:T(8,128)(2,1)}, u32[]{:S(2)}, u32[]{:S(2)}) %collective-permute-start.27) | collective-permute-done | bytes 393248 | tf_op jit(solution)/shard_map/ppermute | solution.py:357
  176.3 21.0 %expert_chunk.5 = (bf16[4,128,3072]{2,1,0:T(8,128)(2,1)}, bf16[4,128,3072]{2,1,0:T(8,128)(2,1)}, bf16[5,256,1536]{2,1,0:T(8,128)(2,1)}, bf16[5,256,1536]{2,1,0:T...) custom-call(bf16[128,1536]{1,0:T(8,128)(2,1)} %collective-permute-done.8.refs_0_, ...), custom_call_target="tpu_custom_call" | custom-call | flops 20132659200 | bytes 62914560 | tf_op jit(solution)/shard_map/expert_chunk/pallas_call | solution.py:671
  207.1 21.0 %expert_chunk.6 = (bf16[4,128,3072]{2,1,0:T(8,128)(2,1)}, bf16[4,128,3072]{2,1,0:T(8,128)(2,1)}, bf16[5,256,1536]{2,1,0:T(8,128)(2,1)}, bf16[5,256,1536]{2,1,0:T...) custom-call(bf16[128,1536]{1,0:T(8,128)(2,1)} %collective-permute-done.11.refs_0_, ...), custom_call_target="tpu_custom_call" | custom-call | flops 20132659200 | bytes 62914560 | tf_op jit(solution)/shard_map/expert_chunk/pallas_call | solution.py:671
  239.7 21.1 %expert_chunk.7 = (bf16[4,128,3072]{2,1,0:T(8,128)(2,1)}, bf16[4,128,3072]{2,1,0:T(8,128)(2,1)}, bf16[5,256,1536]{2,1,0:T(8,128)(2,1)}, bf16[5,256,1536]{2,1,0:T...) custom-call(bf16[128,1536]{1,0:T(8,128)(2,1)} %copy-done.39, ...), custom_call_target="tpu_custom_call" | custom-call | flops 20132659200 | bytes 62914560 | tf_op jit(solution)/shard_map/expert_chunk/pallas_call | solution.py:671
  278.1 17.6 %expert_weights.1 = (f32[5,1536,128]{2,1,0:T(8,128)}, f32[5,1536,128]{2,1,0:T(8,128)}, f32[5,128,1536]{2,1,0:T(8,128)}) custom-call(bf16[5,256,1536]{2,1,0:T(8,128)(2,1)} %get-tuple-element.216.refs_0_, bf16[5,256,1536]{2,1,0:T(8,128)(2,1)} %get-tuple-element.217.refs_1_, bf16[5,256,1536]{2,1,0:T(8,128)(2,1)} %get-tuple-element.218.refs_2_, ...), custom_call_target="tpu_custom_call" | custom-call | flops 6039797760 | bytes 62914560 | tf_op jit(solution)/shard_map/expert_weights/pallas_call | solution.py:732
  317.2 19.3 %collective-permute-done.54.from_y_ref = bf16[64,3072]{1,0:T(8,128)(2,1)} collective-permute-done((bf16[64,3072]{1,0:T(8,128)(2,1)}, bf16[64,3072]{1,0:T(8,128)(2,1)}, u32[]{:S(2)}, u32[]{:S(2)}) %collective-permute-start.54) | collective-permute-done | bytes 393248 | tf_op jit(solution)/shard_map/ppermute | solution.py:357
  358.9 5.6 %collective-permute-done.56 = bf16[128,3072]{1,0:T(8,128)(2,1)} collective-permute-done((bf16[128,3072]{1,0:T(8,128)(2,1)}, bf16[128,3072]{1,0:T(8,128)(2,1)}, u32[]{:S(2)}, u32[]{:S(2)}) %collective-permute-start.56) | collective-permute-done | bytes 786464 | tf_op jit(solution)/shard_map/ppermute | solution.py:362
  372.0 8.9 %collective-permute-done.60.refs_2_ = bf16[128,1536]{1,0:T(8,128)(2,1)S(1)} collective-permute-done((bf16[128,1536]{1,0:T(8,128)(2,1)S(1)}, bf16[128,1536]{1,0:T(8,128)(2,1)S(1)}, u32[]{:S(2)}, u32[]{:S(2)}) %collective-permute-start.60) | collective-permute-done | bytes 393248 | tf_op jit(solution)/shard_map/ppermute | solution.py:352
  386.7 15.2 %attention_back.1 = (bf16[2,4,128,640]{3,2,1,0:T(8,128)(2,1)}, bf16[4,128,640]{2,1,0:T(8,128)(2,1)S(1)}, f32[2,128,1536]{2,1,0:T(8,128)}, bf16[2,128,1536]{2,1,0:T(8,128)(2,1)S(1)}) custom-call(s32[3]{0:T(128)S(1)} %pad_add_fusion.refs_0_, bf16[512,384]{1,0:T(8,128)(2,1)S(1)} %get-tuple-element.251.refs_1_, bf16[512,384]{1,0:T(8,128)(2,1)S(1)} %copy.59.refs_2_, ...), custom_call_target="tpu_custom_call" | custom-call | flops 24159191040 | bytes 62914560 | tf_op jit(solution)/shard_map/attention_back/pallas_call | solution.py:877
  421.1 8.9 %collective-permute-done.66 = bf16[128,640]{1,0:T(8,128)(2,1)S(1)} collective-permute-done((bf16[128,640]{1,0:T(8,128)(2,1)S(1)}, bf16[128,640]{1,0:T(8,128)(2,1)S(1)}, u32[]{:S(2)}, u32[]{:S(2)}) %collective-permute-start.66) | collective-permute-done | bytes 163872 | tf_op jit(solution)/shard_map/ppermute | solution.py:362
  430.6 7.4 %collective-permute-start.80 = (bf16[48,1536]{1,0:T(8,128)(2,1)S(1)}, bf16[48,1536]{1,0:T(8,128)(2,1)S(1)}, u32[]{:S(2)}, u32[]{:S(2)}) collective-permute-start(bf16[48,1536]{1,0:T(8,128)(2,1)S(1)} %fusion.58), channel_id=1, source_target_pairs={{0,8},{4,12},{8,16},{12,20},{16,24},{20,28},{24,0},{28,4},{1,9},{5... | collective-permute-start | bytes 442376 | tf_op jit(solution)/shard_map/ppermute | solution.py:362
  443.1 6.3 %collective-permute-done.78 = f32[42,1536]{1,0:T(8,128)S(1)} collective-permute-done((f32[42,1536]{1,0:T(8,128)S(1)}, f32[42,1536]{1,0:T(8,128)S(1)}, u32[]{:S(2)}, u32[]{:S(2)}) %collective-permute-start.78) | collective-permute-done | bytes 258080 | tf_op jit(solution)/shard_map/ppermute | solution.py:352
  474.4 10.1 %collective-permute-done.86 = bf16[64,640]{1,0:T(8,128)(2,1)S(1)} collective-permute-done((bf16[64,640]{1,0:T(8,128)(2,1)S(1)}, bf16[64,640]{1,0:T(8,128)(2,1)S(1)}, u32[]{:S(2)}, u32[]{:S(2)}) %collective-permute-start.86) | collective-permute-done | bytes 81952 | tf_op jit(solution)/shard_map/ppermute | solution.py:357
  490.0 6.3 %collective-permute-done.87 = f32[42,1536]{1,0:T(8,128)S(1)} collective-permute-done((f32[42,1536]{1,0:T(8,128)S(1)}, f32[42,1536]{1,0:T(8,128)S(1)}, u32[]{:S(2)}, u32[]{:S(2)}) %collective-permute-start.87) | collective-permute-done | bytes 258080 | tf_op jit(solution)/shard_map/ppermute | solution.py:362
  496.3 9.0 %collective-permute-done.88 = f32[42,1536]{1,0:T(8,128)S(1)} collective-permute-done((f32[42,1536]{1,0:T(8,128)S(1)}, f32[42,1536]{1,0:T(8,128)S(1)}, u32[]{:S(2)}, u32[]{:S(2)}) %collective-permute-start.88) | collective-permute-done | bytes 258080 | tf_op jit(solution)/shard_map/ppermute | solution.py:362
  505.3 6.4 %collective-permute-start.92 = (bf16[2,64,640]{2,1,0:T(8,128)(2,1)S(1)}, bf16[2,64,640]{2,1,0:T(8,128)(2,1)S(1)}, u32[]{:S(2)}, u32[]{:S(2)}) collective-permute-start(bf16[2,64,640]{2,1,0:T(8,128)(2,1)S(1)} %bitcast_dynamic-update-slice_fusion.16), channel_id=1, source_target_pairs={{0,8},{4,12},{8,16},{12,20},{16,24},{20,28},{24,0},{28,4},{1,9},{5... | collective-permute-start | bytes 491528 | tf_op jit(solution)/shard_map/ppermute | solution.py:362
  523.3 8.7 %collective-permute-done.91 = bf16[4,128,640]{2,1,0:T(8,128)(2,1)S(1)} collective-permute-done((bf16[4,128,640]{2,1,0:T(8,128)(2,1)S(1)}, bf16[4,128,640]{2,1,0:T(8,128)(2,1)S(1)}, u32[]{:S(2)}, u32[]{:S(2)}) %collective-permute-start.91) | collective-permute-done | bytes 655392 | tf_op jit(solution)/shard_map/ppermute | solution.py:357
  (439 shorter events, 236.2 us)
Async XLA Ops:
  7.2 135.2 %all-gather.2.cloned.1.call-start = ((), (), s32[]{:S(2)}) async-start(), calls=%async_computation | async-start | bytes 14057472 | tf_op jit(solution)/shard_map/all_gather | solution.py:951
  138.3 25.5 %collective-permute-start.19 = (bf16[128,1536]{1,0:T(8,128)(2,1)}, bf16[128,1536]{1,0:T(8,128)(2,1)}, u32[]{:S(2)}, u32[]{:S(2)}) collective-permute-start(bf16[128,1536]{1,0:T(8,128)(2,1)} %collective-permute-done.11.refs_0_), channel_id=1, source_target_pairs={{0,2},{1,3},{2,0},{3,1},{4,6},{5,7},{6,4},{7,5},{8,10},{9,11},{10,... | collective-permute-start | bytes 1179656 | tf_op jit(solution)/shard_map/ppermute | solution.py:352
  139.8 24.0 %collective-permute-start.20 = (bf16[128,1536]{1,0:T(8,128)(2,1)}, bf16[128,1536]{1,0:T(8,128)(2,1)}, u32[]{:S(2)}, u32[]{:S(2)}) collective-permute-start(bf16[128,1536]{1,0:T(8,128)(2,1)} %collective-permute-done.11.refs_0_), channel_id=1, source_target_pairs={{0,4},{4,0},{8,12},{12,8},{16,20},{20,16},{24,28},{28,24},{1,5},{5... | collective-permute-start | bytes 1179656 | tf_op jit(solution)/shard_map/ppermute | solution.py:357
  163.8 33.6 %collective-permute-start.25 = (bf16[4,128,3072]{2,1,0:T(8,128)(2,1)}, bf16[4,128,3072]{2,1,0:T(8,128)(2,1)}, u32[]{:S(2)}, u32[]{:S(2)}) collective-permute-start(bf16[4,128,3072]{2,1,0:T(8,128)(2,1)} %get-tuple-element.176), channel_id=1, source_target_pairs={{0,1},{1,0},{2,3},{3,2},{4,5},{5,4},{6,7},{7,6},{8,9},{9,8},{10,11... | collective-permute-start | bytes 9437192 | tf_op jit(solution)/shard_map/ppermute | solution.py:348
  165.5 31.8 %collective-permute-start.28 = (bf16[128,1536]{1,0:T(8,128)(2,1)}, bf16[128,1536]{1,0:T(8,128)(2,1)S(1)}, u32[]{:S(2)}, u32[]{:S(2)}) collective-permute-start(bf16[128,1536]{1,0:T(8,128)(2,1)} %collective-permute-done.11.refs_0_), channel_id=1, source_target_pairs={{0,1},{1,0},{2,3},{3,2},{4,5},{5,4},{6,7},{7,6},{8,9},{9,8},{10,11... | collective-permute-start | bytes 1179656 | tf_op jit(solution)/shard_map/ppermute | solution.py:348
  165.9 31.5 %collective-permute-start.26 = (bf16[128,1536]{1,0:T(8,128)(2,1)}, bf16[128,1536]{1,0:T(8,128)(2,1)S(1)}, u32[]{:S(2)}, u32[]{:S(2)}) collective-permute-start(bf16[128,1536]{1,0:T(8,128)(2,1)} %collective-permute-done.20.refs_2_), channel_id=1, source_target_pairs={{0,2},{1,3},{2,0},{3,1},{4,6},{5,7},{6,4},{7,5},{8,10},{9,11},{10,... | collective-permute-start | bytes 1179656 | tf_op jit(solution)/shard_map/ppermute | solution.py:352
  197.4 30.9 %collective-permute-start.32 = (bf16[4,128,3072]{2,1,0:T(8,128)(2,1)}, bf16[4,128,3072]{2,1,0:T(8,128)(2,1)}, u32[]{:S(2)}, u32[]{:S(2)}) collective-permute-start(bf16[4,128,3072]{2,1,0:T(8,128)(2,1)} %get-tuple-element.186), channel_id=1, source_target_pairs={{0,1},{1,0},{2,3},{3,2},{4,5},{5,4},{6,7},{7,6},{8,9},{9,8},{10,11... | collective-permute-start | bytes 9437192 | tf_op jit(solution)/shard_map/ppermute | solution.py:348
  198.1 30.1 %collective-permute-start.36 = (bf16[128,1536]{1,0:T(8,128)(2,1)S(1)}, bf16[128,1536]{1,0:T(8,128)(2,1)}, u32[]{:S(2)}, u32[]{:S(2)}) collective-permute-start(bf16[128,1536]{1,0:T(8,128)(2,1)S(1)} %copy-done.59), channel_id=1, source_target_pairs={{0,1},{1,0},{2,3},{3,2},{4,5},{5,4},{6,7},{7,6},{8,9},{9,8},{10,11... | collective-permute-start | bytes 1179656 | tf_op jit(solution)/shard_map/ppermute | solution.py:348
  198.5 29.8 %collective-permute-start.37 = (bf16[128,1536]{1,0:T(8,128)(2,1)}, bf16[128,1536]{1,0:T(8,128)(2,1)}, u32[]{:S(2)}, u32[]{:S(2)}) collective-permute-start(bf16[128,1536]{1,0:T(8,128)(2,1)} %collective-permute-done.7.refs_2_), channel_id=1, source_target_pairs={{0,1},{1,0},{2,3},{3,2},{4,5},{5,4},{6,7},{7,6},{8,9},{9,8},{10,11... | collective-permute-start | bytes 1179656 | tf_op jit(solution)/shard_map/ppermute | solution.py:348
  228.3 32.9 %collective-permute-start.39 = (bf16[4,128,3072]{2,1,0:T(8,128)(2,1)}, bf16[4,128,3072]{2,1,0:T(8,128)(2,1)}, u32[]{:S(2)}, u32[]{:S(2)}) collective-permute-start(bf16[4,128,3072]{2,1,0:T(8,128)(2,1)} %get-tuple-element.197), channel_id=1, source_target_pairs={{0,1},{1,0},{2,3},{3,2},{4,5},{5,4},{6,7},{7,6},{8,9},{9,8},{10,11... | collective-permute-start | bytes 9437192 | tf_op jit(solution)/shard_map/ppermute | solution.py:348
  232.8 28.0 %collective-permute-start.43 = (bf16[64,3072]{1,0:T(8,128)(2,1)}, bf16[64,3072]{1,0:T(8,128)(2,1)S(1)}, u32[]{:S(2)}, u32[]{:S(2)}) collective-permute-start(bf16[64,3072]{1,0:T(8,128)(2,1)} %get-tuple-element.340), channel_id=1, source_target_pairs={{0,4},{4,0},{8,12},{12,8},{16,20},{20,16},{24,28},{28,24},{1,5},{5... | collective-permute-start | bytes 1179656 | tf_op jit(solution)/shard_map/ppermute | solution.py:357
  233.5 27.2 %collective-permute-start.44 = (bf16[64,3072]{1,0:T(8,128)(2,1)}, bf16[64,3072]{1,0:T(8,128)(2,1)S(1)}, u32[]{:S(2)}, u32[]{:S(2)}) collective-permute-start(bf16[64,3072]{1,0:T(8,128)(2,1)} %get-tuple-element.325), channel_id=1, source_target_pairs={{0,2},{1,3},{2,0},{3,1},{4,6},{5,7},{6,4},{7,5},{8,10},{9,11},{10,... | collective-permute-start | bytes 1179656 | tf_op jit(solution)/shard_map/ppermute | solution.py:352
  237.4 23.8 %collective-permute-start.40 = (bf16[128,3072]{1,0:T(8,128)(2,1)}, bf16[128,3072]{1,0:T(8,128)(2,1)S(1)}, u32[]{:S(2)}, u32[]{:S(2)}) collective-permute-start(bf16[128,3072]{1,0:T(8,128)(2,1)} %get-tuple-element.342), channel_id=1, source_target_pairs={{0,2},{1,3},{2,0},{3,1},{4,6},{5,7},{6,4},{7,5},{8,10},{9,11},{10,... | collective-permute-start | bytes 2359304 | tf_op jit(solution)/shard_map/ppermute | solution.py:352
  261.2 40.4 %collective-permute-start.45 = (bf16[4,128,3072]{2,1,0:T(8,128)(2,1)}, bf16[4,128,3072]{2,1,0:T(8,128)(2,1)}, u32[]{:S(2)}, u32[]{:S(2)}) collective-permute-start(bf16[4,128,3072]{2,1,0:T(8,128)(2,1)} %get-tuple-element.209), channel_id=1, source_target_pairs={{0,1},{1,0},{2,3},{3,2},{4,5},{5,4},{6,7},{7,6},{8,9},{9,8},{10,11... | collective-permute-start | bytes 9437192 | tf_op jit(solution)/shard_map/ppermute | solution.py:348
  268.6 32.1 %collective-permute-start.48 = (bf16[128,3072]{1,0:T(8,128)(2,1)}, bf16[128,3072]{1,0:T(8,128)(2,1)S(1)}, u32[]{:S(2)}, u32[]{:S(2)}) collective-permute-start(bf16[128,3072]{1,0:T(8,128)(2,1)} %join_halves.4), channel_id=1, source_target_pairs={{0,24},{4,28},{8,0},{12,4},{16,8},{20,12},{24,16},{28,20},{1,25},{... | collective-permute-start | bytes 2359304 | tf_op jit(solution)/shard_map/ppermute | solution.py:362
  272.8 27.9 %collective-permute-start.46 = (bf16[128,3072]{1,0:T(8,128)(2,1)S(1)}, bf16[128,3072]{1,0:T(8,128)(2,1)}, u32[]{:S(2)}, u32[]{:S(2)}) collective-permute-start(bf16[128,3072]{1,0:T(8,128)(2,1)S(1)} %get-tuple-element.338), channel_id=1, source_target_pairs={{0,2},{1,3},{2,0},{3,1},{4,6},{5,7},{6,4},{7,5},{8,10},{9,11},{10,... | collective-permute-start | bytes 2359304 | tf_op jit(solution)/shard_map/ppermute | solution.py:352
  274.3 26.4 %collective-permute-start.47 = (bf16[128,3072]{1,0:T(8,128)(2,1)S(1)}, bf16[128,3072]{1,0:T(8,128)(2,1)}, u32[]{:S(2)}, u32[]{:S(2)}) collective-permute-start(bf16[128,3072]{1,0:T(8,128)(2,1)S(1)} %get-tuple-element.337), channel_id=1, source_target_pairs={{0,4},{4,0},{8,12},{12,8},{16,20},{20,16},{24,28},{28,24},{1,5},{5... | collective-permute-start | bytes 2359304 | tf_op jit(solution)/shard_map/ppermute | solution.py:357
  276.6 24.1 %collective-permute-start.50 = (bf16[64,3072]{1,0:T(8,128)(2,1)S(1)}, bf16[64,3072]{1,0:T(8,128)(2,1)S(1)}, u32[]{:S(2)}, u32[]{:S(2)}) collective-permute-start(bf16[64,3072]{1,0:T(8,128)(2,1)S(1)} %copy-done.37), channel_id=1, source_target_pairs={{0,2},{1,3},{2,0},{3,1},{4,6},{5,7},{6,4},{7,5},{8,10},{9,11},{10,... | collective-permute-start | bytes 1179656 | tf_op jit(solution)/shard_map/ppermute | solution.py:352
  304.1 36.4 %collective-permute-start.53 = (bf16[128,3072]{1,0:T(8,128)(2,1)}, bf16[128,3072]{1,0:T(8,128)(2,1)}, u32[]{:S(2)}, u32[]{:S(2)}) collective-permute-start(bf16[128,3072]{1,0:T(8,128)(2,1)} %join_halves.5), channel_id=1, source_target_pairs={{0,16},{4,20},{8,24},{12,28},{16,0},{20,4},{24,8},{28,12},{1,17},{... | collective-permute-start | bytes 2359304 | tf_op jit(solution)/shard_map/ppermute | solution.py:362
  308.2 32.2 %collective-permute-start.51 = (bf16[128,3072]{1,0:T(8,128)(2,1)}, bf16[128,3072]{1,0:T(8,128)(2,1)}, u32[]{:S(2)}, u32[]{:S(2)}) collective-permute-start(bf16[128,3072]{1,0:T(8,128)(2,1)} %get-tuple-element.334), channel_id=1, source_target_pairs={{0,2},{1,3},{2,0},{3,1},{4,6},{5,7},{6,4},{7,5},{8,10},{9,11},{10,... | collective-permute-start | bytes 2359304 | tf_op jit(solution)/shard_map/ppermute | solution.py:352
  309.5 30.9 %collective-permute-start.52 = (bf16[128,3072]{1,0:T(8,128)(2,1)}, bf16[128,3072]{1,0:T(8,128)(2,1)}, u32[]{:S(2)}, u32[]{:S(2)}) collective-permute-start(bf16[128,3072]{1,0:T(8,128)(2,1)} %get-tuple-element.333), channel_id=1, source_target_pairs={{0,4},{4,0},{8,12},{12,8},{16,20},{20,16},{24,28},{28,24},{1,5},{5... | collective-permute-start | bytes 2359304 | tf_op jit(solution)/shard_map/ppermute | solution.py:357
  381.1 26.8 %collective-permute-start.69 = (f32[41,1536]{1,0:T(8,128)S(1)}, f32[41,1536]{1,0:T(8,128)S(1)}, u32[]{:S(2)}, u32[]{:S(2)}) collective-permute-start(f32[41,1536]{1,0:T(8,128)S(1)} %pad_maximum_fusion), channel_id=1, source_target_pairs={{0,1},{1,0},{2,3},{3,2},{4,5},{5,4},{6,7},{7,6},{8,9},{9,8},{10,11... | collective-permute-start | bytes 755720 | tf_op jit(solution)/shard_map/ppermute | solution.py:348
  406.3 23.7 %collective-permute-start.64 = (bf16[4,128,640]{2,1,0:T(8,128)(2,1)S(1)}, bf16[4,128,640]{2,1,0:T(8,128)(2,1)S(1)}, u32[]{:S(2)}, u32[]{:S(2)}) collective-permute-start(bf16[4,128,640]{2,1,0:T(8,128)(2,1)S(1)} %slice_bitcast_fusion.1), channel_id=1, source_target_pairs={{0,4},{4,0},{8,12},{12,8},{16,20},{20,16},{24,28},{28,24},{1,5},{5... | collective-permute-start | bytes 1966088 | tf_op jit(solution)/shard_map/ppermute | solution.py:357
  469.2 36.1 %collective-permute-start.90 = (bf16[4,48,1536]{2,1,0:T(8,128)(2,1)S(1)}, bf16[4,48,1536]{2,1,0:T(8,128)(2,1)S(1)}, u32[]{:S(2)}, u32[]{:S(2)}) collective-permute-start(bf16[4,48,1536]{2,1,0:T(8,128)(2,1)S(1)} %bitcast_dynamic-update-slice_fusion.12), channel_id=1, source_target_pairs={{0,4},{4,0},{8,12},{12,8},{16,20},{20,16},{24,28},{28,24},{1,5},{5... | collective-permute-start | bytes 1769480 | tf_op jit(solution)/shard_map/ppermute | solution.py:357
  (141 other events, 1850.2 us)
Sparse Core Ops, SparseCore 0:
  11.4 127.2 all-gather.1

commit v5 on v4

--- a/solution.py
+++ b/solution.py
@@ -397,13 +397,8 @@
     return mine + swap_x(theirs).astype(jnp.float32), theirs
 
 
-def reduce_first(own_core, other_core):
-    return own_core, swap_core(other_core)
-
-
-def reduce_sends(boxes):
-    own_core, arrived = boxes
-    return add_low(own_core[2], arrived[2]), add_low(own_core[3], arrived[3])
+def reduce_sends(own_core, arrived):
+    return add_low(own_core[2], arrived[0]), add_low(own_core[3], arrived[1])
 
 
 def reduce_second(boxes, from_x, from_y):
@@ -507,9 +502,9 @@
     experts, slots, blocks, rows, routed = sizes
     x_parts, g_ref = refs[:8], refs[8]
     base_ref, order_ref, router_ref, gate_ref, up_ref, down_ref = refs[9:15]
-    own_ref, other_ref, xr_out, gr_out, dgu_ref, wh_ref, rg_ref = refs[15:22]
-    xs, gs, xr, gr, wgu, wd, back, picks, probs, weight, d_weight, table, leaving, tables = refs[22:36]
-    x_sem, g_sem, w_sem, out_sem, leave_sem, t_sem = refs[36:42]
+    own_ref, keep_ref, send_ref, xr_out, gr_out, dgu_ref, wh_ref, rg_ref = refs[15:23]
+    xs, gs, xr, gr, wgu, wd, back, picks, probs, weight, d_weight, table, leaving, tables = refs[23:37]
+    x_sem, g_sem, w_sem, out_sem, leave_sem, t_sem = refs[37:43]
     width = xs.shape[1]
     units = wd.shape[1]
     total = experts * slots
@@ -639,13 +634,17 @@
         for i, table_of in enumerate((FIRST_HALF, LAST_HALF)):
             part = choose(b % 4, [place[0] for place in table_of])
             row = choose(b % 4, [place[1] for place in table_of]) * half
-            target = (part, pl.ds(pl.multiple_of(row, half), half))
-            for ref, mine in ((own_ref, b < 4), (other_ref, b >= 4)):
+            place_rows = pl.ds(pl.multiple_of(row, half), half)
+            for ref, index, mine in (
+                (own_ref, part, b < 4),
+                (keep_ref, part, (b >= 4) & (part < 2)),
+                (send_ref, part - 2, (b >= 4) & (part >= 2)),
+            ):
 
                 @pl.when(mine)
-                def _(ref=ref, target=target, i=i):
+                def _(ref=ref, index=index, place_rows=place_rows, i=i):
                     pltpu.make_async_copy(
-                        leaving.at[turn, pl.ds(i * half, half)], ref.at[target], leave_sem.at[turn]
+                        leaving.at[turn, pl.ds(i * half, half)], ref.at[index, place_rows], leave_sem.at[turn]
                     ).start()
 
         return carry
@@ -672,7 +671,8 @@
         lambda *refs: expert_kernel((experts, slots, blocks, rows, routed), *refs),
         out_shape=(
             jax.ShapeDtypeStruct((4, rows, 2 * width), low),
-            jax.ShapeDtypeStruct((4, rows, 2 * width), low),
+            jax.ShapeDtypeStruct((2, rows, 2 * width), low),
+            jax.ShapeDtypeStruct((2, rows, 2 * width), low),
             jax.ShapeDtypeStruct((experts, depth, width), low),
             jax.ShapeDtypeStruct((experts, depth, width), low),
             jax.ShapeDtypeStruct((experts, depth, 2 * units), low),
@@ -680,7 +680,7 @@
             jax.ShapeDtypeStruct((padded, width), full),
         ),
         in_specs=[any_spec] * 9 + [smem_spec, smem_spec, vmem_spec] + [any_spec] * 3,
-        out_specs=(any_spec,) * 4 + (vmem_spec,) * 3,
+        out_specs=(any_spec,) * 5 + (vmem_spec,) * 3,
         scratch_shapes=[
             pltpu.VMEM((blocks * rows, width), low),
             pltpu.VMEM((blocks * rows, width), low),
@@ -796,8 +796,8 @@
     group_factor, head_size = sizes
     me_ref, back, q_ref, k_ref, v_ref, normed_ref, wq_ref, wk_ref, wv_ref = refs[:9]
     cos_ref, sin_ref, column_ref, row_ref, live_ref = refs[9:14]
-    upper_ref, lower_ref, stay_ref, leave_ref = refs[14:18]
-    d_q, d_k, d_v, d_all = refs[18:22]
+    weights_ref, stay_ref, leave_ref = refs[14:17]
+    d_q, d_k, d_v, d_all = refs[17:21]
     seq_len = q_ref.shape[0]
     rows = stay_ref.shape[1]
     factor = 1.0 / math.sqrt(head_size)
@@ -842,15 +842,10 @@
             flat = turned * cos_ref[...] + swap_halves(turned, head_size // 2) * sin_ref[...]
             d_all[:, offset + i * pair : offset + (i + 1) * pair] = flat.astype(jnp.bfloat16)
     d_all[:, q_width + kv_width :] = d_v[...].astype(jnp.bfloat16)
-    plane, side = me_ref[1], me_ref[2]
-    planes, size = lower_ref.shape[0], lower_ref.shape[1]
-    for i in range(3 * planes):
-        features = slice(i * size, (i + 1) * size)
-        part = dot_f32(normed_ref[:, features], d_all[...], TN).astype(jnp.bfloat16)
-        if i < 2 * planes:
-            upper_ref[side ^ (i // planes), i % planes] = part
-        else:
-            lower_ref[(i + planes - plane) % planes] = part
+    size = weights_ref.shape[1] // 6
+    for i in range(12):
+        part = dot_f32(normed_ref[:, i * size : (i + 1) * size], d_all[...], TN).astype(jnp.bfloat16)
+        weights_ref[me_ref[1] ^ (i // 6), i % 6 * size : (i % 6 + 1) * size] = part
     for flip in range(4):
         values = d_all[place(flip), :]
         total = dot_f32(values[:, :q_width], wq_ref[...], NT)
@@ -866,10 +861,7 @@
     seq_len, q_width = query.shape
     width, kv_width = wk.shape
     rows = seq_len // 4
-    owner = lax.axis_index("ep")
-    planes = lax.axis_size("ep") // 2
-    size = width // (3 * planes)
-    me = jnp.stack([lax.axis_index("tp"), owner // 2, owner % 2]).astype(jnp.int32)
+    me = jnp.stack([lax.axis_index("tp"), lax.axis_index("ep") % 2]).astype(jnp.int32)
     low, full = jnp.bfloat16, jnp.float32
     vmem_spec = pl.BlockSpec(memory_space=pltpu.VMEM)
     cos_pair = jnp.tile(cos, (1, 4))
@@ -877,13 +869,12 @@
     return pl.pallas_call(
         lambda *refs: attention_back_kernel((factor, HEAD_SIZE_DIM), *refs),
         out_shape=(
-            jax.ShapeDtypeStruct((2, planes, size, q_width + 2 * kv_width), low),
-            jax.ShapeDtypeStruct((planes, size, q_width + 2 * kv_width), low),
+            jax.ShapeDtypeStruct((2, width // 2, q_width + 2 * kv_width), low),
             jax.ShapeDtypeStruct((2, rows, width), full),
             jax.ShapeDtypeStruct((2, rows, width), low),
         ),
         in_specs=[pl.BlockSpec(memory_space=pltpu.SMEM)] + [vmem_spec] * 13,
-        out_specs=(vmem_spec,) * 4,
+        out_specs=(vmem_spec,) * 3,
         scratch_shapes=[
             pltpu.VMEM((seq_len, q_width), full),
             pltpu.VMEM((seq_len, kv_width), full),
@@ -1020,13 +1011,16 @@
     far[1] = swap_core(diagonal[1])
     turns = [*range(1, planes), 0]
     kept, grad_parts = [], []
-    own, other, arrived, from_x, from_y, halves, second, home = {}, {}, {}, {}, {}, {}, {}, {}
-    for stage in range(planes + 4):
+    own, keep, send, arrived, from_x, from_y, halves, second = {}, {}, {}, {}, {}, {}, {}, {}
+    for stage in range(planes + 3):
         ready, sends, joined = [], None, None
-        a, b, c = stage - 2, stage - 3, stage - 4
-        if a in arrived:
-            sends = reduce_sends((own[a], arrived[a]))
+        a, b, c = stage - 1, stage - 2, stage - 3
+        if a in send:
+            sends = reduce_sends(own[a], swap_core(send[a]))
             ready += sends
+            if stage >= 3:
+                arrived[a] = swap_core(keep[a])
+                ready += [arrived[a]]
         if b in from_x:
             halves[b] = reduce_second((own[b], arrived[b]), from_x[b], from_y[b])
             ready += halves[b]
@@ -1053,18 +1047,18 @@
             if stage == 2:
                 send_swapped(0)
                 came["gather"] = (swapped[0],)
-            own[stage], other[stage], *rest = expert_call(
+            own[stage], keep[stage], send[stage], *rest = expert_call(
                 x_parts, g_all, base, order[step], after(router_rows, *ready),
                 gate_weight, up_weight, down_weight, experts_all, slots,
             )
             kept.append(rest)
-            came["kernel"] = (own[stage], other[stage])
+            came["kernel"] = (own[stage], keep[stage], send[stage])
         if stage == planes:
             xr, gr, dgu, wh, router_parts = zip(*kept)
             came["weights"] = weight_call(xr, gr, (after(dgu[0], *ready),) + dgu[1:], wh)
-        if stage - 1 in other:
-            came["core"] = swap_core(other[stage - 1])
         if sends:
+            if stage < 3:
+                came["core"] = swap_core(keep[a])
             came["cross"] = (swap_x(sends[0]), swap_y(sends[1]))
         if b in halves:
             came["second"] = (swap_y(halves[b][1]), swap_x(halves[b][3]))
@@ -1080,11 +1074,11 @@
         if stage == 2:
             (swapped[0],) = came["gather"]
         if "kernel" in came:
-            own[stage], other[stage] = came["kernel"]
+            own[stage], keep[stage], send[stage] = came["kernel"]
         if "weights" in came:
             gate_grad, up_grad, down_grad = came["weights"]
         if "core" in came:
-            arrived[stage - 1] = came["core"]
+            arrived[a] = came["core"]
         if "cross" in came:
             from_x[a], from_y[a] = came["cross"]
         if "second" in came:
@@ -1103,55 +1097,46 @@
     flat = lambda array: array.reshape(seq_len, -1)
     back, out_grad = branch_back_call(branch_parts, attended, out_weight)
     out_came = swap_y(out_grad[1])
-    upper, lower, stay, leave = attention_back_call(
+    weights, stay, leave = attention_back_call(
         back, flat(query_val), flat(key_val), flat(value_vectors), normed_all,
         query_matrix, key_matrix, value_matrix, cos_table, sin_table, segment_row, live_row, group_factor,
     )
-    upper, lower, stay, leave, out_came = barrier((upper, lower, stay, leave, out_came))
+    weights, stay, leave, out_came = barrier((weights, stay, leave, out_came))
+    weights = weights.reshape(2, planes, -1, weights.shape[-1])
+    weights_came = swap_y(weights[1])
     out_parts = planes_of(add_low(out_grad[0], out_came))
     out_came = send_planes(out_parts)
-    small = jnp.concatenate([router_part, moe_gain_grad[None]], axis=0)
-    upper_came = swap_y(upper[1])
-    lower_came = send_planes(lower)
     both = stay + swap_core(leave).astype(jnp.float32)
+    out_came, both = barrier((out_came, both))
     across_came = swap_x(both[1].astype(jnp.bfloat16))
-    small = small + swap_core(small)
-    upper_came, lower_came, across_came, small, out_came = barrier((upper_came, lower_came, across_came, small, out_came))
     out_sum = add_all(out_parts[0], out_came).astype(jnp.bfloat16)
     out_came = spread_planes(out_sum)
-    upper_parts = planes_of(add_low(upper[0], upper_came))
-    lower_parts = add_all(lower[0], lower_came).astype(jnp.bfloat16).reshape(2, -1, lower.shape[-1])
-    lower_own, lower_leave = sides_of(lower_parts)
+    weights_came, across_came, out_came = barrier((weights_came, across_came, out_came))
+    weights_parts = planes_of(add_low(weights[0], weights_came))
+    weights_came = send_planes(weights_parts)
+    out_half = join_planes(out_came)
+    out_came = swap_y(out_half)
     grad_normed = both[0] + across_came.astype(jnp.float32)
     _, norm_one_back = jax.vjp(rms_norm, x_float, norm_gain)
     grad_x_norm, norm_gain_grad = norm_one_back(grad_normed)
     input_grad = grad_middle + grad_x_norm
-    gain_part = norm_gain_grad[None]
-    gain_part = gain_part + swap_core(gain_part)
-    small = jnp.concatenate([small, gain_part], axis=0)
-    small = small + swap_x(small)
-    small = small + swap_y(small)
-    upper_came = send_planes(upper_parts)
-    lower_came = swap_y(lower_leave)
-    upper_came, lower_came, small, out_came = barrier((upper_came, lower_came, small, out_came))
-    out_half = join_planes(out_came)
-    out_came = swap_y(out_half)
-    upper_sum = add_all(upper_parts[0], upper_came).astype(jnp.bfloat16)
-    lower_sum = add_low(lower_own, lower_came)
-    upper_came = spread_planes(upper_sum)
-    lower_came = swap_y(lower_sum)
-    small_came = spread_planes(small)
-    upper_came, lower_came, small_came, out_came = barrier((upper_came, lower_came, small_came, out_came))
-    upper_half, lower_half = join_planes(upper_came), join_sides(lower_sum, lower_came)
-    small = sum(small_came)
-    upper_came = swap_y(upper_half)
-    lower_came = spread_planes(lower_half)
-    upper_came, lower_came = barrier((upper_came, lower_came))
+    small = jnp.concatenate([router_part, moe_gain_grad[None], norm_gain_grad[None]], axis=0)
+    small = small + swap_core(small)
+    small_came = swap_x(small)
+    weights_came, small_came, out_came = barrier((weights_came, small_came, out_came))
+    small = small + small_came
+    small_came = swap_y(small)
+    weights_sum = add_all(weights_parts[0], weights_came).astype(jnp.bfloat16)
+    weights_came = spread_planes(weights_sum)
+    weights_came, small_came = barrier((weights_came, small_came))
+    small = small + small_came
+    weights_half = join_planes(weights_came)
+    weights_came = swap_y(weights_half)
+    small_came = send_planes([small] * planes)
+    weights_came, small_came = barrier((weights_came, small_came))
+    small = add_all(small, small_came)
     out_grad = join_sides(out_half, out_came).reshape(-1, width).astype(jnp.float32)
-    columns = upper_half.shape[-1]
-    upper = join_sides(upper_half, upper_came).reshape(-1, columns)
-    lower = join_planes(lower_came).reshape(-1, columns)
-    weights = jnp.concatenate([upper, lower], axis=0).astype(jnp.float32)
+    weights = join_sides(weights_half, weights_came).reshape(width, -1).astype(jnp.float32)
     q_width, kv_width = query_matrix.shape[1], key_matrix.shape[1]
     query_grad, key_grad, value_grad = jnp.split(weights, (q_width, q_width + kv_width), axis=1)
     router_grad, moe_gain_grad, norm_gain_grad = small[:experts_all].T, small[experts_all], small[experts_all + 1]

time: 551 us -> 498 us (0.904)
  the two profiles are of different devices: /device:TPU:0 before, /device:TPU:8 now
where the time goes in v5:
time: 498 us; the launch traced here: 490 us
  waiting for transfers between devices  175 us (35%)
  Pallas kernels  130 us (26%)
  starting transfers between devices  79.3 us (16%)
  other arithmetic  51.4 us (10%)
  local copies, waits for them, and re-layouts  23.7 us (5%)
  between operations  15.9 us (3%)
  matrix products  14.5 us (3%)
    ppermute x21, waiting for transfers between devices, shift_z(): lax.ppermute(value, 'ep', [(i, (i + 2 * step) % owners) for i in range(ow...  110 us
    pallas_call x4, Pallas kernels, expert_call(): pl.pallas_call(lambda *refs: expert_kernel((experts, slots, blocks, rows,...  84.2 us
    ppermute x19, waiting for transfers between devices, swap_y(): return lax.ppermute(value, 'ep', [(i, i ^ 1) for i in range(owners)])  33.7 us
    ppermute x21, starting transfers between devices, shift_z(): lax.ppermute(value, 'ep', [(i, (i + 2 * step) % owners) for i in range(ow...  32 us
    ppermute x19, waiting for transfers between devices, swap_x(): return lax.ppermute(value, 'tp', [(i, i ^ 2) for i in range(4)])  25.1 us
    ppermute x19, starting transfers between devices, swap_y(): return lax.ppermute(value, 'ep', [(i, i ^ 1) for i in range(owners)])  21.9 us
    ppermute x19, starting transfers between devices, swap_x(): return lax.ppermute(value, 'tp', [(i, i ^ 2) for i in range(4)])  20.4 us
    pallas_call x1, Pallas kernels, weight_call(): pl.pallas_call(lambda *refs: weight_kernel(count, *refs), grid=(experts,)...  17.6 us
  transfers between devices with their start and end apart: 91, of which 34 were waited for; matrix products, arithmetic and copies ran while one was open for 14% of the time, Pallas kernels for 25%

profile of v5, /device:TPU:8, one launch (start us, length us, event | category | flops | bytes accessed | tf_op | source)
XLA Modules:
  0.0 489.6 jit_solution(11828067755703516203)
XLA Ops:
  15.4 7.3 %collective-permute-done.1 = bf16[128,1536]{1,0:T(8,128)(2,1)S(1)} collective-permute-done((bf16[128,1536]{1,0:T(8,128)(2,1)}, bf16[128,1536]{1,0:T(8,128)(2,1)S(1)}, u32[]{:S(2)}, u32[]{:S(2)}) %collective-permute-start.1) | collective-permute-done | bytes 393248 | tf_op jit(solution)/shard_map/ppermute | solution.py:352
  31.6 6.1 %fusion.83 = (f32[2,3,512]{2,1,0:T(4,128)S(1)}, f32[2,3,512,512]{2,3,1,0:T(8,128)}) fusion(pred[512,512]{0,1:T(8,128)(4,1)} %fusion.16, bf16[512,2,32]{0,2,1:T(8,128)(2,1)} %get-tuple-element.352, bf16[512,2,32]{0,2,1:T(8,128)(2,1)S(1)} %get-tuple-element.351, bf16[512,2,3,32]{0,3,2,1:T(8,128)(2,1)S(1)} %get-tuple-element.346, ...), kind=kOutput, calls=%fused_computation.203 | convolution fusion | flops 208667136 | bytes 7090176 | tf_op jit(solution)/shard_map/sub | solution.py:976
  53.2 10.1 %collective-permute-done.4 = bf16[128,1536]{1,0:T(8,128)(2,1)} collective-permute-done((bf16[128,1536]{1,0:T(8,128)(2,1)S(1)}, bf16[128,1536]{1,0:T(8,128)(2,1)}, u32[]{:S(2)}, u32[]{:S(2)}) %collective-permute-start.4) | collective-permute-done | bytes 393248 | tf_op jit(solution)/shard_map/ppermute | solution.py:352
  70.6 22.0 %collective-permute-done.5.refs_0_ = bf16[128,1536]{1,0:T(8,128)(2,1)} collective-permute-done((bf16[128,1536]{1,0:T(8,128)(2,1)}, bf16[128,1536]{1,0:T(8,128)(2,1)}, u32[]{:S(2)}, u32[]{:S(2)}) %collective-permute-start.5) | collective-permute-done | bytes 393248 | tf_op jit(solution)/shard_map/ppermute | solution.py:362
  98.5 13.0 %collective-permute-done.10.refs_2_ = bf16[128,1536]{1,0:T(8,128)(2,1)S(1)} collective-permute-done((bf16[128,1536]{1,0:T(8,128)(2,1)}, bf16[128,1536]{1,0:T(8,128)(2,1)S(1)}, u32[]{:S(2)}, u32[]{:S(2)}) %collective-permute-start.10) | collective-permute-done | bytes 393248 | tf_op jit(solution)/shard_map/ppermute | solution.py:357
  117.4 15.0 %collective-permute-done.11.refs_0_ = bf16[128,1536]{1,0:T(8,128)(2,1)S(1)} collective-permute-done((bf16[128,1536]{1,0:T(8,128)(2,1)}, bf16[128,1536]{1,0:T(8,128)(2,1)S(1)}, u32[]{:S(2)}, u32[]{:S(2)}) %collective-permute-start.11) | collective-permute-done | bytes 393248 | tf_op jit(solution)/shard_map/ppermute | solution.py:362
  139.0 21.0 %expert_chunk.4 = (bf16[4,128,3072]{2,1,0:T(8,128)(2,1)}, bf16[2,128,3072]{2,1,0:T(8,128)(2,1)}, bf16[2,128,3072]{2,1,0:T(8,128)(2,1)}, bf16[5,256,1536]{2,1,0:T...) custom-call(bf16[128,1536]{1,0:T(8,128)(2,1)} %collective-permute-do, ...), custom_call_target="tpu_custom_call" | custom-call | flops 20132659200 | bytes 62914560 | tf_op jit(solution)/shard_map/expert_chunk/pallas_call | solution.py:670
  167.6 4.3 collective-permute-done.30.refs_3_
  176.6 21.1 %expert_chunk.5 = (bf16[4,128,3072]{2,1,0:T(8,128)(2,1)}, bf16[2,128,3072]{2,1,0:T(8,128)(2,1)}, bf16[2,128,3072]{2,1,0:T(8,128)(2,1)}, bf16[5,256,1536]{2,1,0:T...) custom-call(bf16[128,1536]{1,0:T(8,128)(2,1)} %collective-permute-do, ...), custom_call_target="tpu_custom_call" | custom-call | flops 20132659200 | bytes 62914560 | tf_op jit(solution)/shard_map/expert_chunk/pallas_call | solution.py:670
  207.7 21.1 %expert_chunk.6 = (bf16[4,128,3072]{2,1,0:T(8,128)(2,1)}, bf16[2,128,3072]{2,1,0:T(8,128)(2,1)}, bf16[2,128,3072]{2,1,0:T(8,128)(2,1)}, bf16[5,256,1536]{2,1,0:T...) custom-call(bf16[128,1536]{1,0:T(8,128)(2,1)} %copy-done.58, ...), custom_call_target="tpu_custom_call" | custom-call | flops 20132659200 | bytes 62914560 | tf_op jit(solution)/shard_map/expert_chunk/pallas_call | solution.py:670
  247.7 21.1 %expert_chunk.7 = (bf16[4,128,3072]{2,1,0:T(8,128)(2,1)}, bf16[2,128,3072]{2,1,0:T(8,128)(2,1)}, bf16[2,128,3072]{2,1,0:T(8,128)(2,1)}, bf16[5,256,1536]{2,1,0:T...) custom-call(bf16[128,1536]{1,0:T(8,128)(2,1)} %multiply_convert_fusi, ...), custom_call_target="tpu_custom_call" | custom-call | flops 20132659200 | bytes 62914560 | tf_op jit(solution)/shard_map/expert_chunk/pallas_call | solution.py:670
  284.6 17.6 %expert_weights.1 = (f32[5,1536,128]{2,1,0:T(8,128)}, f32[5,1536,128]{2,1,0:T(8,128)}, f32[5,128,1536]{2,1,0:T(8,128)}) custom-call(bf16[5,256,1536]{2,1,0:T(8,128)(2,1)} %get-tuple-element.225.refs_0_, bf16[5,256,1536]{2,1,0:T(8,128)(2,1)} %get-tuple-element.226.refs_1_, bf16[5,256,1536]{2,1,0:T(8,128)(2,1)} %get-tuple-element.227.refs_2_, ...), custom_call_target="tpu_custom_call" | custom-call | flops 6039797760 | bytes 62914560 | tf_op jit(solution)/shard_map/expert_weights/pallas_call | solution.py:732
  313.1 4.1 fusion.33
  320.7 7.5 %collective-permute-done.61.from_y_ref = bf16[64,3072]{1,0:T(8,128)(2,1)} collective-permute-done((bf16[64,3072]{1,0:T(8,128)(2,1)}, bf16[64,3072]{1,0:T(8,128)(2,1)}, u32[]{:S(2)}, u32[]{:S(2)}) %collective-permute-start.61) | collective-permute-done | bytes 393248 | tf_op jit(solution)/shard_map/ppermute | solution.py:357
  335.4 3.9 multiply_reduce_fusion
  358.0 14.7 %attention_back.1 = (bf16[2,768,640]{2,1,0:T(8,128)(2,1)}, f32[2,128,1536]{2,1,0:T(8,128)S(1)}, bf16[2,128,1536]{2,1,0:T(8,128)(2,1)S(1)}) custom-call(s32[2]{0:T(128)S(1)} %pad_add_fusion.refs_4_.refs_0_, bf16[512,384]{1,0:T(8,128)(2,1)S(1)} %get-tuple-element.255.refs_1_, bf16[512,384]{1,0:T(8,128)(2,1)S(1)} %copy.59.refs_2_, ...), custom_call_target="tpu_custom_call" | custom-call | flops 24159191040 | bytes 62914560 | tf_op jit(solution)/shard_map/attention_back/pallas_call | solution.py:869
  373.2 5.6 %collective-permute-start.68 = (bf16[48,1536]{1,0:T(8,128)(2,1)S(1)}, bf16[48,1536]{1,0:T(8,128)(2,1)S(1)}, u32[]{:S(2)}, u32[]{:S(2)}) collective-permute-start(bf16[48,1536]{1,0:T(8,128)(2,1)S(1)} %get-tuple-element.348), channel_id=1, source_target_pairs={{0,16},{4,20},{8,24},{12,28},{16,0},{20,4},{24,8},{28,12},{1,17},{... | collective-permute-start | bytes 442376 | tf_op jit(solution)/shard_map/ppermute | solution.py:362
  381.2 7.5 %collective-permute-done.68 = bf16[48,1536]{1,0:T(8,128)(2,1)S(1)} collective-permute-done((bf16[48,1536]{1,0:T(8,128)(2,1)S(1)}, bf16[48,1536]{1,0:T(8,128)(2,1)S(1)}, u32[]{:S(2)}, u32[]{:S(2)}) %collective-permute-start.68) | collective-permute-done | bytes 147488 | tf_op jit(solution)/shard_map/ppermute | solution.py:362
  394.7 4.4 collective-permute-done.73
  399.1 5.7 %collective-permute-done.74 = bf16[48,1536]{1,0:T(8,128)(2,1)S(1)} collective-permute-done((bf16[48,1536]{1,0:T(8,128)(2,1)S(1)}, bf16[48,1536]{1,0:T(8,128)(2,1)S(1)}, u32[]{:S(2)}, u32[]{:S(2)}) %collective-permute-start.74) | collective-permute-done | bytes 147488 | tf_op jit(solution)/shard_map/ppermute | solution.py:362
  416.5 12.3 %collective-permute-done.78 = bf16[192,640]{1,0:T(8,128)(2,1)S(1)} collective-permute-done((bf16[192,640]{1,0:T(8,128)(2,1)S(1)}, bf16[192,640]{1,0:T(8,128)(2,1)S(1)}, u32[]{:S(2)}, u32[]{:S(2)}) %collective-permute-start.78) | collective-permute-done | bytes 245792 | tf_op jit(solution)/shard_map/ppermute | solution.py:362
  439.3 12.7 %collective-permute-done.83 = bf16[192,640]{1,0:T(8,128)(2,1)S(1)} collective-permute-done((bf16[192,640]{1,0:T(8,128)(2,1)S(1)}, bf16[192,640]{1,0:T(8,128)(2,1)S(1)}, u32[]{:S(2)}, u32[]{:S(2)}) %collective-permute-start.83) | collective-permute-done | bytes 245792 | tf_op jit(solution)/shard_map/ppermute | solution.py:362
  463.5 6.0 %collective-permute-done.88 = bf16[42,1536]{1,0:T(8,128)(2,1)S(1)} collective-permute-done((bf16[42,1536]{1,0:T(8,128)(2,1)S(1)}, bf16[42,1536]{1,0:T(8,128)(2,1)S(1)}, u32[]{:S(2)}, u32[]{:S(2)}) %collective-permute-start.88) | collective-permute-done | bytes 129056 | tf_op jit(solution)/shard_map/ppermute | solution.py:362
  471.3 6.3 %collective-permute-done.86 = bf16[4,192,640]{2,1,0:T(8,128)(2,1)S(1)} collective-permute-done((bf16[4,192,640]{2,1,0:T(8,128)(2,1)S(1)}, bf16[4,192,640]{2,1,0:T(8,128)(2,1)S(1)}, u32[]{:S(2)}, u32[]{:S(2)}) %collective-permute-start.86) | collective-permute-done | bytes 983072 | tf_op jit(solution)/shard_map/ppermute | solution.py:357
  (417 shorter events, 203.6 us)
Async XLA Ops:
  7.2 131.5 %all-gather.2.cloned.1.call-start = ((), (), s32[]{:S(2)}) async-start(), calls=%async_computation | async-start | bytes 14057472 | tf_op jit(solution)/shard_map/all_gather | solution.py:942
  66.4 26.2 %collective-permute-start.5 = (bf16[128,1536]{1,0:T(8,128)(2,1)}, bf16[128,1536]{1,0:T(8,128)(2,1)}, u32[]{:S(2)}, u32[]{:S(2)}) collective-permute-start(bf16[128,1536]{1,0:T(8,128)(2,1)} %multiply_convert_fusion.refs_0_), channel_id=1, source_target_pairs={{0,8},{4,12},{8,16},{12,20},{16,24},{20,28},{24,0},{28,4},{1,9},{5... | collective-permute-start | bytes 1179656 | tf_op jit(solution)/shard_map/ppermute | solution.py:362
  67.9 24.7 %collective-permute-start.6 = (bf16[128,1536]{1,0:T(8,128)(2,1)}, bf16[128,1536]{1,0:T(8,128)(2,1)}, u32[]{:S(2)}, u32[]{:S(2)}) collective-permute-start(bf16[128,1536]{1,0:T(8,128)(2,1)} %multiply_convert_fusion.refs_0_), channel_id=1, source_target_pairs={{0,2},{1,3},{2,0},{3,1},{4,6},{5,7},{6,4},{7,5},{8,10},{9,11},{10,... | collective-permute-start | bytes 1179656 | tf_op jit(solution)/shard_map/ppermute | solution.py:352
  136.2 23.9 %collective-permute-start.19 = (bf16[128,1536]{1,0:T(8,128)(2,1)}, bf16[128,1536]{1,0:T(8,128)(2,1)}, u32[]{:S(2)}, u32[]{:S(2)}) collective-permute-start(bf16[128,1536]{1,0:T(8,128)(2,1)} %copy-done.58), channel_id=1, source_target_pairs={{0,2},{1,3},{2,0},{3,1},{4,6},{5,7},{6,4},{7,5},{8,10},{9,11},{10,... | collective-permute-start | bytes 1179656 | tf_op jit(solution)/shard_map/ppermute | solution.py:352
  136.2 23.9 %collective-permute-start.20 = (bf16[128,1536]{1,0:T(8,128)(2,1)}, bf16[128,1536]{1,0:T(8,128)(2,1)}, u32[]{:S(2)}, u32[]{:S(2)}) collective-permute-start(bf16[128,1536]{1,0:T(8,128)(2,1)} %copy-done.58), channel_id=1, source_target_pairs={{0,4},{4,0},{8,12},{12,8},{16,20},{20,16},{24,28},{28,24},{1,5},{5... | collective-permute-start | bytes 1179656 | tf_op jit(solution)/shard_map/ppermute | solution.py:357
  164.0 33.7 %collective-permute-start.33 = (bf16[128,1536]{1,0:T(8,128)(2,1)}, bf16[128,1536]{1,0:T(8,128)(2,1)}, u32[]{:S(2)}, u32[]{:S(2)}) collective-permute-start(bf16[128,1536]{1,0:T(8,128)(2,1)} %collective-permute-done.20.refs_2_), channel_id=1, source_target_pairs={{0,1},{1,0},{2,3},{3,2},{4,5},{5,4},{6,7},{7,6},{8,9},{9,8},{10,11... | collective-permute-start | bytes 1179656 | tf_op jit(solution)/shard_map/ppermute | solution.py:348
  172.0 25.7 %collective-permute-start.25 = (bf16[2,128,3072]{2,1,0:T(8,128)(2,1)}, bf16[2,128,3072]{2,1,0:T(8,128)(2,1)S(1)}, u32[]{:S(2)}, u32[]{:S(2)}) collective-permute-start(bf16[2,128,3072]{2,1,0:T(8,128)(2,1)} %get-tuple-element.173), channel_id=1, source_target_pairs={{0,1},{1,0},{2,3},{3,2},{4,5},{5,4},{6,7},{7,6},{8,9},{9,8},{10,11... | collective-permute-start | bytes 4718600 | tf_op jit(solution)/shard_map/ppermute | solution.py:348
  172.0 25.7 %collective-permute-start.32 = (bf16[128,1536]{1,0:T(8,128)(2,1)}, bf16[128,1536]{1,0:T(8,128)(2,1)}, u32[]{:S(2)}, u32[]{:S(2)}) collective-permute-start(bf16[128,1536]{1,0:T(8,128)(2,1)} %collective-permute-done.19.refs_1_), channel_id=1, source_target_pairs={{0,1},{1,0},{2,3},{3,2},{4,5},{5,4},{6,7},{7,6},{8,9},{9,8},{10,11... | collective-permute-start | bytes 1179656 | tf_op jit(solution)/shard_map/ppermute | solution.py:348
  172.5 25.2 %collective-permute-start.27 = (bf16[128,3072]{1,0:T(8,128)(2,1)}, bf16[128,3072]{1,0:T(8,128)(2,1)S(1)}, u32[]{:S(2)}, u32[]{:S(2)}) collective-permute-start(bf16[128,3072]{1,0:T(8,128)(2,1)} %get-tuple-element.336), channel_id=1, source_target_pairs={{0,2},{1,3},{2,0},{3,1},{4,6},{5,7},{6,4},{7,5},{8,10},{9,11},{10,... | collective-permute-start | bytes 2359304 | tf_op jit(solution)/shard_map/ppermute | solution.py:352
  202.0 26.7 %collective-permute-start.43 = (bf16[64,3072]{1,0:T(8,128)(2,1)}, bf16[64,3072]{1,0:T(8,128)(2,1)S(1)}, u32[]{:S(2)}, u32[]{:S(2)}) collective-permute-start(bf16[64,3072]{1,0:T(8,128)(2,1)} %get-tuple-element.332), channel_id=1, source_target_pairs={{0,4},{4,0},{8,12},{12,8},{16,20},{20,16},{24,28},{28,24},{1,5},{5... | collective-permute-start | bytes 1179656 | tf_op jit(solution)/shard_map/ppermute | solution.py:357
  204.2 24.6 %collective-permute-start.44 = (bf16[64,3072]{1,0:T(8,128)(2,1)}, bf16[64,3072]{1,0:T(8,128)(2,1)}, u32[]{:S(2)}, u32[]{:S(2)}) collective-permute-start(bf16[64,3072]{1,0:T(8,128)(2,1)} %get-tuple-element.317), channel_id=1, source_target_pairs={{0,2},{1,3},{2,0},{3,1},{4,6},{5,7},{6,4},{7,5},{8,10},{9,11},{10,... | collective-permute-start | bytes 1179656 | tf_op jit(solution)/shard_map/ppermute | solution.py:352
  204.8 23.9 %collective-permute-start.35 = (bf16[2,128,3072]{2,1,0:T(8,128)(2,1)}, bf16[2,128,3072]{2,1,0:T(8,128)(2,1)S(1)}, u32[]{:S(2)}, u32[]{:S(2)}) collective-permute-start(bf16[2,128,3072]{2,1,0:T(8,128)(2,1)} %get-tuple-element.187), channel_id=1, source_target_pairs={{0,1},{1,0},{2,3},{3,2},{4,5},{5,4},{6,7},{7,6},{8,9},{9,8},{10,11... | collective-permute-start | bytes 4718600 | tf_op jit(solution)/shard_map/ppermute | solution.py:348
  204.9 27.6 %collective-permute-start.37 = (bf16[128,3072]{1,0:T(8,128)(2,1)}, bf16[128,3072]{1,0:T(8,128)(2,1)S(1)}, u32[]{:S(2)}, u32[]{:S(2)}) collective-permute-start(bf16[128,3072]{1,0:T(8,128)(2,1)} %get-tuple-element.334), channel_id=1, source_target_pairs={{0,2},{1,3},{2,0},{3,1},{4,6},{5,7},{6,4},{7,5},{8,10},{9,11},{10,... | collective-permute-start | bytes 2359304 | tf_op jit(solution)/shard_map/ppermute | solution.py:352
  206.3 26.1 %collective-permute-start.38 = (bf16[128,3072]{1,0:T(8,128)(2,1)S(1)}, bf16[128,3072]{1,0:T(8,128)(2,1)}, u32[]{:S(2)}, u32[]{:S(2)}) collective-permute-start(bf16[128,3072]{1,0:T(8,128)(2,1)S(1)} %get-tuple-element.333), channel_id=1, source_target_pairs={{0,4},{4,0},{8,12},{12,8},{16,20},{20,16},{24,28},{28,24},{1,5},{5... | collective-permute-start | bytes 2359304 | tf_op jit(solution)/shard_map/ppermute | solution.py:357
  236.3 32.6 %collective-permute-start.51 = (bf16[64,3072]{1,0:T(8,128)(2,1)}, bf16[64,3072]{1,0:T(8,128)(2,1)S(1)}, u32[]{:S(2)}, u32[]{:S(2)}) collective-permute-start(bf16[64,3072]{1,0:T(8,128)(2,1)} %get-tuple-element.328), channel_id=1, source_target_pairs={{0,4},{4,0},{8,12},{12,8},{16,20},{20,16},{24,28},{28,24},{1,5},{5... | collective-permute-start | bytes 1179656 | tf_op jit(solution)/shard_map/ppermute | solution.py:357
  237.6 31.2 %collective-permute-start.52 = (bf16[64,3072]{1,0:T(8,128)(2,1)}, bf16[64,3072]{1,0:T(8,128)(2,1)}, u32[]{:S(2)}, u32[]{:S(2)}) collective-permute-start(bf16[64,3072]{1,0:T(8,128)(2,1)} %get-tuple-element.313), channel_id=1, source_target_pairs={{0,2},{1,3},{2,0},{3,1},{4,6},{5,7},{6,4},{7,5},{8,10},{9,11},{10,... | collective-permute-start | bytes 1179656 | tf_op jit(solution)/shard_map/ppermute | solution.py:352
  240.4 28.5 %collective-permute-start.48 = (bf16[128,3072]{1,0:T(8,128)(2,1)}, bf16[128,3072]{1,0:T(8,128)(2,1)S(1)}, u32[]{:S(2)}, u32[]{:S(2)}) collective-permute-start(bf16[128,3072]{1,0:T(8,128)(2,1)} %join_halves.4), channel_id=1, source_target_pairs={{0,24},{4,28},{8,0},{12,4},{16,8},{20,12},{24,16},{28,20},{1,25},{... | collective-permute-start | bytes 2359304 | tf_op jit(solution)/shard_map/ppermute | solution.py:362
  245.2 23.7 %collective-permute-start.46 = (bf16[128,3072]{1,0:T(8,128)(2,1)S(1)}, bf16[128,3072]{1,0:T(8,128)(2,1)S(1)}, u32[]{:S(2)}, u32[]{:S(2)}) collective-permute-start(bf16[128,3072]{1,0:T(8,128)(2,1)S(1)} %get-tuple-element.330), channel_id=1, source_target_pairs={{0,2},{1,3},{2,0},{3,1},{4,6},{5,7},{6,4},{7,5},{8,10},{9,11},{10,... | collective-permute-start | bytes 2359304 | tf_op jit(solution)/shard_map/ppermute | solution.py:352
  272.7 35.6 %collective-permute-start.56 = (bf16[128,3072]{1,0:T(8,128)(2,1)}, bf16[128,3072]{1,0:T(8,128)(2,1)S(1)}, u32[]{:S(2)}, u32[]{:S(2)}) collective-permute-start(bf16[128,3072]{1,0:T(8,128)(2,1)} %join_halves.5), channel_id=1, source_target_pairs={{0,16},{4,20},{8,24},{12,28},{16,0},{20,4},{24,8},{28,12},{1,17},{... | collective-permute-start | bytes 2359304 | tf_op jit(solution)/shard_map/ppermute | solution.py:362
  276.6 31.7 %collective-permute-start.54 = (bf16[128,3072]{1,0:T(8,128)(2,1)S(1)}, bf16[128,3072]{1,0:T(8,128)(2,1)}, u32[]{:S(2)}, u32[]{:S(2)}) collective-permute-start(bf16[128,3072]{1,0:T(8,128)(2,1)S(1)} %get-tuple-element.326), channel_id=1, source_target_pairs={{0,2},{1,3},{2,0},{3,1},{4,6},{5,7},{6,4},{7,5},{8,10},{9,11},{10,... | collective-permute-start | bytes 2359304 | tf_op jit(solution)/shard_map/ppermute | solution.py:352
  277.3 31.0 %collective-permute-start.55 = (bf16[128,3072]{1,0:T(8,128)(2,1)S(1)}, bf16[128,3072]{1,0:T(8,128)(2,1)}, u32[]{:S(2)}, u32[]{:S(2)}) collective-permute-start(bf16[128,3072]{1,0:T(8,128)(2,1)S(1)} %get-tuple-element.325), channel_id=1, source_target_pairs={{0,4},{4,0},{8,12},{12,8},{16,20},{20,16},{24,28},{28,24},{1,5},{5... | collective-permute-start | bytes 2359304 | tf_op jit(solution)/shard_map/ppermute | solution.py:357
  379.0 27.0 %collective-permute-start.71 = (bf16[4,192,640]{2,1,0:T(8,128)(2,1)S(1)}, bf16[4,192,640]{2,1,0:T(8,128)(2,1)S(1)}, u32[]{:S(2)}, u32[]{:S(2)}) collective-permute-start(bf16[4,192,640]{2,1,0:T(8,128)(2,1)S(1)} %bitcast.240), channel_id=1, source_target_pairs={{0,4},{4,0},{8,12},{12,8},{16,20},{20,16},{24,28},{28,24},{1,5},{5... | collective-permute-start | bytes 2949128 | tf_op jit(solution)/shard_map/ppermute | solution.py:357
  406.1 24.2 %collective-permute-start.81 = (bf16[4,48,1536]{2,1,0:T(8,128)(2,1)S(1)}, bf16[4,48,1536]{2,1,0:T(8,128)(2,1)S(1)}, u32[]{:S(2)}, u32[]{:S(2)}) collective-permute-start(bf16[4,48,1536]{2,1,0:T(8,128)(2,1)S(1)} %bitcast_dynamic-update-slice_fusion.8), channel_id=1, source_target_pairs={{0,4},{4,0},{8,12},{12,8},{16,20},{20,16},{24,28},{28,24},{1,5},{5... | collective-permute-start | bytes 1769480 | tf_op jit(solution)/shard_map/ppermute | solution.py:357
  453.8 23.7 %collective-permute-start.86 = (bf16[4,192,640]{2,1,0:T(8,128)(2,1)S(1)}, bf16[4,192,640]{2,1,0:T(8,128)(2,1)S(1)}, u32[]{:S(2)}, u32[]{:S(2)}) collective-permute-start(bf16[4,192,640]{2,1,0:T(8,128)(2,1)S(1)} %bitcast_dynamic-update-slice_fusion.4), channel_id=1, source_target_pairs={{0,4},{4,0},{8,12},{12,8},{16,20},{20,16},{24,28},{28,24},{1,5},{5... | collective-permute-start | bytes 2949128 | tf_op jit(solution)/shard_map/ppermute | solution.py:357
  (137 other events, 1721.3 us)
Sparse Core Ops, SparseCore 0:
  11.4 124.1 all-gather.1

commit v6 on v5

--- a/solution.py
+++ b/solution.py
@@ -412,21 +412,22 @@
     return parts
 
 
-def join_kernel(first_ref, from_y_ref, last_ref, from_x_ref, out_ref):
-    half = first_ref.shape[0]
-    out_ref[:half] = add_low(first_ref[...], from_y_ref[...])
-    out_ref[half:] = add_low(last_ref[...], from_x_ref[...])
+def join_kernel(first_ref, from_y_ref, last_ref, from_x_ref, grad_ref, out_ref):
+    half, width = grad_ref.shape[0] // 2, grad_ref.shape[1]
+    for ref, columns in ((grad_ref, slice(0, width)), (out_ref, slice(width, 2 * width))):
+        ref[:half] = add_low(first_ref[:, columns], from_y_ref[:, columns])
+        ref[half:] = add_low(last_ref[:, columns], from_x_ref[:, columns])
 
 
 def reduce_home(first, from_y, last, from_x):
     half, width = first.shape
-    half_spec = pl.BlockSpec((half, width), lambda j: (0, 0))
+    like = jax.ShapeDtypeStruct((2 * half, width // 2), first.dtype)
     return pl.pallas_call(
         join_kernel,
         grid=(1,),
-        in_specs=[half_spec] * 4,
-        out_specs=pl.BlockSpec((2 * half, width), lambda j: (0, 0)),
-        out_shape=jax.ShapeDtypeStruct((2 * half, width), first.dtype),
+        in_specs=[pl.BlockSpec((half, width), lambda j: (0, 0))] * 4,
+        out_specs=(pl.BlockSpec(like.shape, lambda j: (0, 0)),) * 2,
+        out_shape=(like, like),
         name="join_halves",
     )(first, from_y, last, from_x)
 
@@ -1010,7 +1011,7 @@
     columns[3], cross, diagonal, swapped = barrier((columns[3], cross, diagonal, swapped))
     far[1] = swap_core(diagonal[1])
     turns = [*range(1, planes), 0]
-    kept, grad_parts = [], []
+    kept, grad_parts, out_joined = [], [], []
     own, keep, send, arrived, from_x, from_y, halves, second = {}, {}, {}, {}, {}, {}, {}, {}
     for stage in range(planes + 3):
         ready, sends, joined = [], None, None
@@ -1026,6 +1027,8 @@
             ready += halves[b]
         if c in second:
             joined = reduce_home(halves[c][0], second[c][0], halves[c][2], second[c][1])
+            joined, out_part = joined
+            out_joined.append(out_part)
             ready += [joined]
             if turns[c] == 0:
                 grad_parts.append(joined)
@@ -1054,6 +1057,8 @@
             kept.append(rest)
             came["kernel"] = (own[stage], keep[stage], send[stage])
         if stage == planes:
+            out_home = {0: shift_z(out_joined[0], -turns[0])}
+            came["output"] = out_home[0]
             xr, gr, dgu, wh, router_parts = zip(*kept)
             came["weights"] = weight_call(xr, gr, (after(dgu[0], *ready),) + dgu[1:], wh)
         if sends:
@@ -1076,6 +1081,7 @@
         if "kernel" in came:
             own[stage], keep[stage], send[stage] = came["kernel"]
         if "weights" in came:
+            out_home[0] = came["output"]
             gate_grad, up_grad, down_grad = came["weights"]
         if "core" in came:
             arrived[a] = came["core"]
@@ -1085,15 +1091,14 @@
             second[b] = came["second"]
         if "home" in came:
             grad_parts.append(came["home"])
-    grad_moe_in = sum(part[:, :width].astype(jnp.float32) for part in grad_parts)
-    expert_sum = sum(part[:, width:].astype(jnp.float32) for part in grad_parts)
-    output = (middle + expert_sum).astype(jnp.bfloat16)
+    grad_moe_in = sum(part.astype(jnp.float32) for part in grad_parts)
     router_part = jnp.roll(sum(router_parts)[:experts_all], owner * local_experts, axis=0)
     grad_out = cotangent.astype(jnp.float32)
     _, norm_two_back = jax.vjp(rms_norm, middle, moe_gain)
     grad_mid_norm, moe_gain_grad = norm_two_back(grad_moe_in)
     grad_middle = grad_out + grad_mid_norm
     branch_parts = gather_pieces(grad_middle.astype(jnp.bfloat16))
+    out_home[1] = shift_z(out_joined[1], -turns[1])
     flat = lambda array: array.reshape(seq_len, -1)
     back, out_grad = branch_back_call(branch_parts, attended, out_weight)
     out_came = swap_y(out_grad[1])
@@ -1101,7 +1106,7 @@
         back, flat(query_val), flat(key_val), flat(value_vectors), normed_all,
         query_matrix, key_matrix, value_matrix, cos_table, sin_table, segment_row, live_row, group_factor,
     )
-    weights, stay, leave, out_came = barrier((weights, stay, leave, out_came))
+    weights, stay, leave, out_came, out_home[1] = barrier((weights, stay, leave, out_came, out_home[1]))
     weights = weights.reshape(2, planes, -1, weights.shape[-1])
     weights_came = swap_y(weights[1])
     out_parts = planes_of(add_low(out_grad[0], out_came))
@@ -1133,8 +1138,12 @@
     weights_half = join_planes(weights_came)
     weights_came = swap_y(weights_half)
     small_came = send_planes([small] * planes)
-    weights_came, small_came = barrier((weights_came, small_came))
+    out_home[2] = shift_z(after(out_joined[2], weights_half), -turns[2])
+    weights_came, small_came, out_home[2] = barrier((weights_came, small_came, out_home[2]))
     small = add_all(small, small_came)
+    expert_sum = sum(out_home[i].astype(jnp.float32) for i in range(planes - 1))
+    expert_sum = expert_sum + out_joined[planes - 1].astype(jnp.float32)
+    output = (middle + expert_sum).astype(jnp.bfloat16)
     out_grad = join_sides(out_half, out_came).reshape(-1, width).astype(jnp.float32)
     weights = join_sides(weights_half, weights_came).reshape(width, -1).astype(jnp.float32)
     q_width, kv_width = query_matrix.shape[1], key_matrix.shape[1]

time: 498 us -> 496 us (level)
  the two profiles are of different devices: /device:TPU:8 before, /device:TPU:0 now
where the time goes in v6:
time: 496 us; the launch traced here: 487 us
  waiting for transfers between devices  158 us (32%)
  Pallas kernels  129 us (26%)
  starting transfers between devices  100 us (20%)
  other arithmetic  48.7 us (10%)
  local copies, waits for them, and re-layouts  23.5 us (5%)
  between operations  16 us (3%)
  matrix products  11.8 us (2%)
    ppermute x24, waiting for transfers between devices, shift_z(): lax.ppermute(value, 'ep', [(i, (i + 2 * step) % owners) for i in range(ow...  92.9 us
    pallas_call x4, Pallas kernels, expert_call(): pl.pallas_call(lambda *refs: expert_kernel((experts, slots, blocks, rows,...  84.1 us
    ppermute x24, starting transfers between devices, shift_z(): lax.ppermute(value, 'ep', [(i, (i + 2 * step) % owners) for i in range(ow...  48.4 us
    ppermute x19, waiting for transfers between devices, swap_x(): return lax.ppermute(value, 'tp', [(i, i ^ 2) for i in range(4)])  29.7 us
    ppermute x19, waiting for transfers between devices, swap_y(): return lax.ppermute(value, 'ep', [(i, i ^ 1) for i in range(owners)])  24.2 us
    ppermute x19, starting transfers between devices, swap_y(): return lax.ppermute(value, 'ep', [(i, i ^ 1) for i in range(owners)])  22.9 us
    ppermute x19, starting transfers between devices, swap_x(): return lax.ppermute(value, 'tp', [(i, i ^ 2) for i in range(4)])  22.7 us
    pallas_call x1, Pallas kernels, weight_call(): pl.pallas_call(lambda *refs: weight_kernel(count, *refs), grid=(experts,)...  17.6 us
  transfers between devices with their start and end apart: 94, of which 29 were waited for; matrix products, arithmetic and copies ran while one was open for 12% of the time, Pallas kernels for 26%

profile of v6, /device:TPU:0, one launch (start us, length us, event | category | flops | bytes accessed | tf_op | source)
XLA Modules:
  0.0 487.2 jit_solution(4492426527825743320)
XLA Ops:
  17.4 6.4 %collective-permute-done.1 = bf16[128,1536]{1,0:T(8,128)(2,1)S(1)} collective-permute-done((bf16[128,1536]{1,0:T(8,128)(2,1)}, bf16[128,1536]{1,0:T(8,128)(2,1)S(1)}, u32[]{:S(2)}, u32[]{:S(2)}) %collective-permute-start.1) | collective-permute-done | bytes 393248 | tf_op jit(solution)/shard_map/ppermute | solution.py:352
  30.0 4.9 %fusion.84 = (f32[2,3,512]{2,1,0:T(4,128)S(1)}, f32[2,3,512,512]{2,3,1,0:T(8,128)}) fusion(pred[512,512]{0,1:T(8,128)(4,1)S(1)} %copy-done.50, bf16[512,2,32]{0,2,1:T(8,128)(2,1)S(1)} %get-tuple-element.376, bf16[512,2,32]{0,2,1:T(8,128)(2,1)S(1)} %get-tuple-element.375, bf16[512,2,3,32]{0,3,2,1:T(8,128)(2,1)S(1)} %get-tuple-element.370, ...), kind=kOutput, calls=%fused_computation.203 | convolution fusion | flops 208667136 | bytes 7090176 | tf_op jit(solution)/shard_map/sub | solution.py:977
  50.7 14.1 %collective-permute-done.4 = bf16[128,1536]{1,0:T(8,128)(2,1)S(1)} collective-permute-done((bf16[128,1536]{1,0:T(8,128)(2,1)S(1)}, bf16[128,1536]{1,0:T(8,128)(2,1)S(1)}, u32[]{:S(2)}, u32[]{:S(2)}) %collective-permute-start.4) | collective-permute-done | bytes 393248 | tf_op jit(solution)/shard_map/ppermute | solution.py:352
  70.5 12.2 %collective-permute-done.5.refs_0_ = bf16[128,1536]{1,0:T(8,128)(2,1)} collective-permute-done((bf16[128,1536]{1,0:T(8,128)(2,1)S(1)}, bf16[128,1536]{1,0:T(8,128)(2,1)}, u32[]{:S(2)}, u32[]{:S(2)}) %collective-permute-start.5) | collective-permute-done | bytes 393248 | tf_op jit(solution)/shard_map/ppermute | solution.py:362
  90.3 13.9 %collective-permute-done.10.refs_2_ = bf16[128,1536]{1,0:T(8,128)(2,1)S(1)} collective-permute-done((bf16[128,1536]{1,0:T(8,128)(2,1)}, bf16[128,1536]{1,0:T(8,128)(2,1)S(1)}, u32[]{:S(2)}, u32[]{:S(2)}) %collective-permute-start.10) | collective-permute-done | bytes 393248 | tf_op jit(solution)/shard_map/ppermute | solution.py:357
  112.6 14.9 %collective-permute-done.11.refs_0_ = bf16[128,1536]{1,0:T(8,128)(2,1)} collective-permute-done((bf16[128,1536]{1,0:T(8,128)(2,1)S(1)}, bf16[128,1536]{1,0:T(8,128)(2,1)}, u32[]{:S(2)}, u32[]{:S(2)}) %collective-permute-start.11) | collective-permute-done | bytes 393248 | tf_op jit(solution)/shard_map/ppermute | solution.py:362
  136.2 21.0 %expert_chunk.4 = (bf16[4,128,3072]{2,1,0:T(8,128)(2,1)}, bf16[2,128,3072]{2,1,0:T(8,128)(2,1)}, bf16[2,128,3072]{2,1,0:T(8,128)(2,1)}, bf16[5,256,1536]{2,1,0:T...) custom-call(bf16[128,1536]{1,0:T(8,128)(2,1)} %collective-permute-do, ...), custom_call_target="tpu_custom_call" | custom-call | flops 20132659200 | bytes 62914560 | tf_op jit(solution)/shard_map/expert_chunk/pallas_call | solution.py:671
  163.7 6.3 %collective-permute-done.30.refs_3_ = bf16[128,1536]{1,0:T(8,128)(2,1)} collective-permute-done((bf16[128,1536]{1,0:T(8,128)(2,1)S(1)}, bf16[128,1536]{1,0:T(8,128)(2,1)}, u32[]{:S(2)}, u32[]{:S(2)}) %collective-permute-start.30) | collective-permute-done | bytes 393248 | tf_op jit(solution)/shard_map/ppermute | solution.py:357
  173.2 21.0 %expert_chunk.5 = (bf16[4,128,3072]{2,1,0:T(8,128)(2,1)}, bf16[2,128,3072]{2,1,0:T(8,128)(2,1)}, bf16[2,128,3072]{2,1,0:T(8,128)(2,1)}, bf16[5,256,1536]{2,1,0:T...) custom-call(bf16[128,1536]{1,0:T(8,128)(2,1)} %copy-done.70, ...), custom_call_target="tpu_custom_call" | custom-call | flops 20132659200 | bytes 62914560 | tf_op jit(solution)/shard_map/expert_chunk/pallas_call | solution.py:671
  206.6 21.0 %expert_chunk.6 = (bf16[4,128,3072]{2,1,0:T(8,128)(2,1)}, bf16[2,128,3072]{2,1,0:T(8,128)(2,1)}, bf16[2,128,3072]{2,1,0:T(8,128)(2,1)}, bf16[5,256,1536]{2,1,0:T...) custom-call(bf16[128,1536]{1,0:T(8,128)(2,1)} %collective-permute-do, ...), custom_call_target="tpu_custom_call" | custom-call | flops 20132659200 | bytes 62914560 | tf_op jit(solution)/shard_map/expert_chunk/pallas_call | solution.py:671
  239.7 4.9 %collective-permute-start.48 = (bf16[128,1536]{1,0:T(8,128)(2,1)}, bf16[128,1536]{1,0:T(8,128)(2,1)S(1)}, u32[]{:S(2)}, u32[]{:S(2)}) collective-permute-start(bf16[128,1536]{1,0:T(8,128)(2,1)} %get-tuple-element.218), channel_id=1, source_target_pairs={{0,24},{4,28},{8,0},{12,4},{16,8},{20,12},{24,16},{28,20},{1,25},{... | collective-permute-start | bytes 1179656 | tf_op jit(solution)/shard_map/ppermute | solution.py:362
  250.2 21.0 %expert_chunk.7 = (bf16[4,128,3072]{2,1,0:T(8,128)(2,1)}, bf16[2,128,3072]{2,1,0:T(8,128)(2,1)}, bf16[2,128,3072]{2,1,0:T(8,128)(2,1)}, bf16[5,256,1536]{2,1,0:T...) custom-call(bf16[128,1536]{1,0:T(8,128)(2,1)} %copy-done.47, ...), custom_call_target="tpu_custom_call" | custom-call | flops 20132659200 | bytes 62914560 | tf_op jit(solution)/shard_map/expert_chunk/pallas_call | solution.py:671
  271.9 4.6 collective-permute-done.53
  292.7 17.6 %expert_weights.1 = (f32[5,1536,128]{2,1,0:T(8,128)}, f32[5,1536,128]{2,1,0:T(8,128)}, f32[5,128,1536]{2,1,0:T(8,128)}) custom-call(bf16[5,256,1536]{2,1,0:T(8,128)(2,1)} %get-tuple-element.239.refs_0_, bf16[5,256,1536]{2,1,0:T(8,128)(2,1)} %get-tuple-element.240.refs_1_, bf16[5,256,1536]{2,1,0:T(8,128)(2,1)} %get-tuple-element.241.refs_2_, ...), custom_call_target="tpu_custom_call" | custom-call | flops 6039797760 | bytes 62914560 | tf_op jit(solution)/shard_map/expert_weights/pallas_call | solution.py:733
  319.8 5.2 %collective-permute-done.61 = bf16[128,1536]{1,0:T(8,128)(2,1)} collective-permute-done((bf16[128,1536]{1,0:T(8,128)(2,1)}, bf16[128,1536]{1,0:T(8,128)(2,1)}, u32[]{:S(2)}, u32[]{:S(2)}) %collective-permute-start.61) | collective-permute-done | bytes 393248 | tf_op jit(solution)/shard_map/ppermute | solution.py:362
  352.2 14.7 %attention_back.1 = (bf16[2,768,640]{2,1,0:T(8,128)(2,1)}, f32[2,128,1536]{2,1,0:T(8,128)S(1)}, bf16[2,128,1536]{2,1,0:T(8,128)(2,1)S(1)}) custom-call(s32[2]{0:T(128)S(1)} %pad_add_fusion.refs_4_.refs_0_, bf16[512,384]{1,0:T(8,128)(2,1)S(1)} %get-tuple-element.272.refs_1_, bf16[512,384]{1,0:T(8,128)(2,1)S(1)} %copy.59.refs_2_, ...), custom_call_target="tpu_custom_call" | custom-call | flops 24159191040 | bytes 62914560 | tf_op jit(solution)/shard_map/attention_back/pallas_call | solution.py:870
  376.1 5.9 %collective-permute-done.71 = bf16[48,1536]{1,0:T(8,128)(2,1)S(1)} collective-permute-done((bf16[48,1536]{1,0:T(8,128)(2,1)S(1)}, bf16[48,1536]{1,0:T(8,128)(2,1)S(1)}, u32[]{:S(2)}, u32[]{:S(2)}) %collective-permute-start.71) | collective-permute-done | bytes 147488 | tf_op jit(solution)/shard_map/ppermute | solution.py:362
  391.1 5.5 %collective-permute-done.76 = bf16[48,1536]{1,0:T(8,128)(2,1)S(1)} collective-permute-done((bf16[48,1536]{1,0:T(8,128)(2,1)S(1)}, bf16[48,1536]{1,0:T(8,128)(2,1)S(1)}, u32[]{:S(2)}, u32[]{:S(2)}) %collective-permute-start.76) | collective-permute-done | bytes 147488 | tf_op jit(solution)/shard_map/ppermute | solution.py:362
  411.3 10.3 %collective-permute-done.79 = bf16[192,640]{1,0:T(8,128)(2,1)S(1)} collective-permute-done((bf16[192,640]{1,0:T(8,128)(2,1)S(1)}, bf16[192,640]{1,0:T(8,128)(2,1)S(1)}, u32[]{:S(2)}, u32[]{:S(2)}) %collective-permute-start.79) | collective-permute-done | bytes 245792 | tf_op jit(solution)/shard_map/ppermute | solution.py:362
  421.8 5.8 %collective-permute-start.84 = (bf16[192,640]{1,0:T(8,128)(2,1)S(1)}, bf16[192,640]{1,0:T(8,128)(2,1)S(1)}, u32[]{:S(2)}, u32[]{:S(2)}) collective-permute-start(bf16[192,640]{1,0:T(8,128)(2,1)S(1)} %fusion.51), channel_id=1, source_target_pairs={{0,8},{4,12},{8,16},{12,20},{16,24},{20,28},{24,0},{28,4},{1,9},{5... | collective-permute-start | bytes 737288 | tf_op jit(solution)/shard_map/ppermute | solution.py:362
  434.3 9.8 %collective-permute-done.85 = bf16[192,640]{1,0:T(8,128)(2,1)S(1)} collective-permute-done((bf16[192,640]{1,0:T(8,128)(2,1)S(1)}, bf16[192,640]{1,0:T(8,128)(2,1)S(1)}, u32[]{:S(2)}, u32[]{:S(2)}) %collective-permute-start.85) | collective-permute-done | bytes 245792 | tf_op jit(solution)/shard_map/ppermute | solution.py:362
  447.2 5.7 %collective-permute-start.92 = (bf16[128,1536]{1,0:T(8,128)(2,1)S(1)}, bf16[128,1536]{1,0:T(8,128)(2,1)S(1)}, u32[]{:S(2)}, u32[]{:S(2)}) collective-permute-start(bf16[128,1536]{1,0:T(8,128)(2,1)S(1)} %copy-done.67), channel_id=1, source_target_pairs={{0,8},{4,12},{8,16},{12,20},{16,24},{20,28},{24,0},{28,4},{1,9},{5... | collective-permute-start | bytes 1179656 | tf_op jit(solution)/shard_map/ppermute | solution.py:362
  458.9 9.4 %collective-permute-done.89 = bf16[42,1536]{1,0:T(8,128)(2,1)S(1)} collective-permute-done((bf16[42,1536]{1,0:T(8,128)(2,1)S(1)}, bf16[42,1536]{1,0:T(8,128)(2,1)S(1)}, u32[]{:S(2)}, u32[]{:S(2)}) %collective-permute-start.89) | collective-permute-done | bytes 129056 | tf_op jit(solution)/shard_map/ppermute | solution.py:362
  468.3 4.8 collective-permute-done.90
  (442 shorter events, 210.4 us)
Async XLA Ops:
  7.2 129.1 %all-gather.2.cloned.1.call-start = ((), (), s32[]{:S(2)}) async-start(), calls=%async_computation | async-start | bytes 14057472 | tf_op jit(solution)/shard_map/all_gather | solution.py:943
  130.3 26.9 %collective-permute-start.19 = (bf16[128,1536]{1,0:T(8,128)(2,1)}, bf16[128,1536]{1,0:T(8,128)(2,1)S(1)}, u32[]{:S(2)}, u32[]{:S(2)}) collective-permute-start(bf16[128,1536]{1,0:T(8,128)(2,1)} %collective-permute-done.11.refs_0_), channel_id=1, source_target_pairs={{0,2},{1,3},{2,0},{3,1},{4,6},{5,7},{6,4},{7,5},{8,10},{9,11},{10,... | collective-permute-start | bytes 1179656 | tf_op jit(solution)/shard_map/ppermute | solution.py:352
  132.5 24.8 %collective-permute-start.20 = (bf16[128,1536]{1,0:T(8,128)(2,1)}, bf16[128,1536]{1,0:T(8,128)(2,1)}, u32[]{:S(2)}, u32[]{:S(2)}) collective-permute-start(bf16[128,1536]{1,0:T(8,128)(2,1)} %collective-permute-done.11.refs_0_), channel_id=1, source_target_pairs={{0,4},{4,0},{8,12},{12,8},{16,20},{20,16},{24,28},{28,24},{1,5},{5... | collective-permute-start | bytes 1179656 | tf_op jit(solution)/shard_map/ppermute | solution.py:357
  132.8 24.4 %collective-permute-start.18 = (bf16[128,1536]{1,0:T(8,128)(2,1)}, bf16[128,1536]{1,0:T(8,128)(2,1)}, u32[]{:S(2)}, u32[]{:S(2)}) collective-permute-start(bf16[128,1536]{1,0:T(8,128)(2,1)} %collective-permute-done.12.refs_1_), channel_id=1, source_target_pairs={{0,4},{4,0},{8,12},{12,8},{16,20},{20,16},{24,28},{28,24},{1,5},{5... | collective-permute-start | bytes 1179656 | tf_op jit(solution)/shard_map/ppermute | solution.py:357
  161.2 33.0 %collective-permute-start.33 = (bf16[128,1536]{1,0:T(8,128)(2,1)}, bf16[128,1536]{1,0:T(8,128)(2,1)}, u32[]{:S(2)}, u32[]{:S(2)}) collective-permute-start(bf16[128,1536]{1,0:T(8,128)(2,1)} %collective-permute-done.20.refs_2_), channel_id=1, source_target_pairs={{0,1},{1,0},{2,3},{3,2},{4,5},{5,4},{6,7},{7,6},{8,9},{9,8},{10,11... | collective-permute-start | bytes 1179656 | tf_op jit(solution)/shard_map/ppermute | solution.py:348
  170.0 24.2 %collective-permute-start.25 = (bf16[2,128,3072]{2,1,0:T(8,128)(2,1)}, bf16[2,128,3072]{2,1,0:T(8,128)(2,1)S(1)}, u32[]{:S(2)}, u32[]{:S(2)}) collective-permute-start(bf16[2,128,3072]{2,1,0:T(8,128)(2,1)} %get-tuple-element.185), channel_id=1, source_target_pairs={{0,1},{1,0},{2,3},{3,2},{4,5},{5,4},{6,7},{7,6},{8,9},{9,8},{10,11... | collective-permute-start | bytes 4718600 | tf_op jit(solution)/shard_map/ppermute | solution.py:348
  170.0 24.2 %collective-permute-start.32 = (bf16[128,1536]{1,0:T(8,128)(2,1)}, bf16[128,1536]{1,0:T(8,128)(2,1)}, u32[]{:S(2)}, u32[]{:S(2)}) collective-permute-start(bf16[128,1536]{1,0:T(8,128)(2,1)} %copy-done.71), channel_id=1, source_target_pairs={{0,1},{1,0},{2,3},{3,2},{4,5},{5,4},{6,7},{7,6},{8,9},{9,8},{10,11... | collective-permute-start | bytes 1179656 | tf_op jit(solution)/shard_map/ppermute | solution.py:348
  170.5 23.7 %collective-permute-start.27 = (bf16[128,3072]{1,0:T(8,128)(2,1)S(1)}, bf16[128,3072]{1,0:T(8,128)(2,1)S(1)}, u32[]{:S(2)}, u32[]{:S(2)}) collective-permute-start(bf16[128,3072]{1,0:T(8,128)(2,1)S(1)} %get-tuple-element.361), channel_id=1, source_target_pairs={{0,2},{1,3},{2,0},{3,1},{4,6},{5,7},{6,4},{7,5},{8,10},{9,11},{10,... | collective-permute-start | bytes 2359304 | tf_op jit(solution)/shard_map/ppermute | solution.py:352
  200.0 27.6 %collective-permute-start.43 = (bf16[64,3072]{1,0:T(8,128)(2,1)}, bf16[64,3072]{1,0:T(8,128)(2,1)}, u32[]{:S(2)}, u32[]{:S(2)}) collective-permute-start(bf16[64,3072]{1,0:T(8,128)(2,1)} %get-tuple-element.357), channel_id=1, source_target_pairs={{0,4},{4,0},{8,12},{12,8},{16,20},{20,16},{24,28},{28,24},{1,5},{5... | collective-permute-start | bytes 1179656 | tf_op jit(solution)/shard_map/ppermute | solution.py:357
  202.5 25.2 %collective-permute-start.44 = (bf16[64,3072]{1,0:T(8,128)(2,1)}, bf16[64,3072]{1,0:T(8,128)(2,1)}, u32[]{:S(2)}, u32[]{:S(2)}) collective-permute-start(bf16[64,3072]{1,0:T(8,128)(2,1)} %get-tuple-element.342), channel_id=1, source_target_pairs={{0,2},{1,3},{2,0},{3,1},{4,6},{5,7},{6,4},{7,5},{8,10},{9,11},{10,... | collective-permute-start | bytes 1179656 | tf_op jit(solution)/shard_map/ppermute | solution.py:352
  204.0 23.7 %collective-permute-start.35 = (bf16[2,128,3072]{2,1,0:T(8,128)(2,1)}, bf16[2,128,3072]{2,1,0:T(8,128)(2,1)S(1)}, u32[]{:S(2)}, u32[]{:S(2)}) collective-permute-start(bf16[2,128,3072]{2,1,0:T(8,128)(2,1)} %get-tuple-element.199), channel_id=1, source_target_pairs={{0,1},{1,0},{2,3},{3,2},{4,5},{5,4},{6,7},{7,6},{8,9},{9,8},{10,11... | collective-permute-start | bytes 4718600 | tf_op jit(solution)/shard_map/ppermute | solution.py:348
  204.2 26.7 %collective-permute-start.37 = (bf16[128,3072]{1,0:T(8,128)(2,1)}, bf16[128,3072]{1,0:T(8,128)(2,1)}, u32[]{:S(2)}, u32[]{:S(2)}) collective-permute-start(bf16[128,3072]{1,0:T(8,128)(2,1)} %get-tuple-element.359), channel_id=1, source_target_pairs={{0,2},{1,3},{2,0},{3,1},{4,6},{5,7},{6,4},{7,5},{8,10},{9,11},{10,... | collective-permute-start | bytes 2359304 | tf_op jit(solution)/shard_map/ppermute | solution.py:352
  205.3 25.6 %collective-permute-start.38 = (bf16[128,3072]{1,0:T(8,128)(2,1)}, bf16[128,3072]{1,0:T(8,128)(2,1)}, u32[]{:S(2)}, u32[]{:S(2)}) collective-permute-start(bf16[128,3072]{1,0:T(8,128)(2,1)} %get-tuple-element.358), channel_id=1, source_target_pairs={{0,4},{4,0},{8,12},{12,8},{16,20},{20,16},{24,28},{28,24},{1,5},{5... | collective-permute-start | bytes 2359304 | tf_op jit(solution)/shard_map/ppermute | solution.py:357
  235.0 36.2 %collective-permute-start.51 = (bf16[64,3072]{1,0:T(8,128)(2,1)}, bf16[64,3072]{1,0:T(8,128)(2,1)S(1)}, u32[]{:S(2)}, u32[]{:S(2)}) collective-permute-start(bf16[64,3072]{1,0:T(8,128)(2,1)} %get-tuple-element.353), channel_id=1, source_target_pairs={{0,4},{4,0},{8,12},{12,8},{16,20},{20,16},{24,28},{28,24},{1,5},{5... | collective-permute-start | bytes 1179656 | tf_op jit(solution)/shard_map/ppermute | solution.py:357
  236.3 34.9 %collective-permute-start.52 = (bf16[64,3072]{1,0:T(8,128)(2,1)}, bf16[64,3072]{1,0:T(8,128)(2,1)}, u32[]{:S(2)}, u32[]{:S(2)}) collective-permute-start(bf16[64,3072]{1,0:T(8,128)(2,1)} %get-tuple-element.338), channel_id=1, source_target_pairs={{0,2},{1,3},{2,0},{3,1},{4,6},{5,7},{6,4},{7,5},{8,10},{9,11},{10,... | collective-permute-start | bytes 1179656 | tf_op jit(solution)/shard_map/ppermute | solution.py:352
  239.7 31.5 %collective-permute-start.48 = (bf16[128,1536]{1,0:T(8,128)(2,1)}, bf16[128,1536]{1,0:T(8,128)(2,1)S(1)}, u32[]{:S(2)}, u32[]{:S(2)}) collective-permute-start(bf16[128,1536]{1,0:T(8,128)(2,1)} %get-tuple-element.218), channel_id=1, source_target_pairs={{0,24},{4,28},{8,0},{12,4},{16,8},{20,12},{24,16},{28,20},{1,25},{... | collective-permute-start | bytes 1179656 | tf_op jit(solution)/shard_map/ppermute | solution.py:362
  279.5 30.7 %collective-permute-start.54 = (bf16[128,3072]{1,0:T(8,128)(2,1)}, bf16[128,3072]{1,0:T(8,128)(2,1)}, u32[]{:S(2)}, u32[]{:S(2)}) collective-permute-start(bf16[128,3072]{1,0:T(8,128)(2,1)} %get-tuple-element.351), channel_id=1, source_target_pairs={{0,2},{1,3},{2,0},{3,1},{4,6},{5,7},{6,4},{7,5},{8,10},{9,11},{10,... | collective-permute-start | bytes 2359304 | tf_op jit(solution)/shard_map/ppermute | solution.py:352
  280.5 29.8 %collective-permute-start.55 = (bf16[128,3072]{1,0:T(8,128)(2,1)}, bf16[128,3072]{1,0:T(8,128)(2,1)}, u32[]{:S(2)}, u32[]{:S(2)}) collective-permute-start(bf16[128,3072]{1,0:T(8,128)(2,1)} %get-tuple-element.350), channel_id=1, source_target_pairs={{0,4},{4,0},{8,12},{12,8},{16,20},{20,16},{24,28},{28,24},{1,5},{5... | collective-permute-start | bytes 2359304 | tf_op jit(solution)/shard_map/ppermute | solution.py:357
  283.1 27.2 %collective-permute-start.58 = (bf16[64,3072]{1,0:T(8,128)(2,1)}, bf16[64,3072]{1,0:T(8,128)(2,1)}, u32[]{:S(2)}, u32[]{:S(2)}) collective-permute-start(bf16[64,3072]{1,0:T(8,128)(2,1)} %get-tuple-element.348), channel_id=1, source_target_pairs={{0,4},{4,0},{8,12},{12,8},{16,20},{20,16},{24,28},{28,24},{1,5},{5... | collective-permute-start | bytes 1179656 | tf_op jit(solution)/shard_map/ppermute | solution.py:357
  286.6 23.7 %collective-permute-start.59 = (bf16[64,3072]{1,0:T(8,128)(2,1)}, bf16[64,3072]{1,0:T(8,128)(2,1)}, u32[]{:S(2)}, u32[]{:S(2)}) collective-permute-start(bf16[64,3072]{1,0:T(8,128)(2,1)} %get-tuple-element.335), channel_id=1, source_target_pairs={{0,2},{1,3},{2,0},{3,1},{4,6},{5,7},{6,4},{7,5},{8,10},{9,11},{10,... | collective-permute-start | bytes 1179656 | tf_op jit(solution)/shard_map/ppermute | solution.py:352
  371.6 25.1 %collective-permute-start.69 = (bf16[4,192,640]{2,1,0:T(8,128)(2,1)S(1)}, bf16[4,192,640]{2,1,0:T(8,128)(2,1)S(1)}, u32[]{:S(2)}, u32[]{:S(2)}) collective-permute-start(bf16[4,192,640]{2,1,0:T(8,128)(2,1)S(1)} %bitcast.240), channel_id=1, source_target_pairs={{0,4},{4,0},{8,12},{12,8},{16,20},{20,16},{24,28},{28,24},{1,5},{5... | collective-permute-start | bytes 2949128 | tf_op jit(solution)/shard_map/ppermute | solution.py:357
  396.8 24.8 %collective-permute-start.83 = (bf16[4,48,1536]{2,1,0:T(8,128)(2,1)S(1)}, bf16[4,48,1536]{2,1,0:T(8,128)(2,1)S(1)}, u32[]{:S(2)}, u32[]{:S(2)}) collective-permute-start(bf16[4,48,1536]{2,1,0:T(8,128)(2,1)S(1)} %bitcast_dynamic-update-slice_fusion.8), channel_id=1, source_target_pairs={{0,4},{4,0},{8,12},{12,8},{16,20},{20,16},{24,28},{28,24},{1,5},{5... | collective-permute-start | bytes 1769480 | tf_op jit(solution)/shard_map/ppermute | solution.py:357
  444.3 28.8 %collective-permute-start.88 = (bf16[4,192,640]{2,1,0:T(8,128)(2,1)S(1)}, bf16[4,192,640]{2,1,0:T(8,128)(2,1)S(1)}, u32[]{:S(2)}, u32[]{:S(2)}) collective-permute-start(bf16[4,192,640]{2,1,0:T(8,128)(2,1)S(1)} %bitcast_dynamic-update-slice_fusion.4), channel_id=1, source_target_pairs={{0,4},{4,0},{8,12},{12,8},{16,20},{20,16},{24,28},{28,24},{1,5},{5... | collective-permute-start | bytes 2949128 | tf_op jit(solution)/shard_map/ppermute | solution.py:357
  447.2 26.0 %collective-permute-start.92 = (bf16[128,1536]{1,0:T(8,128)(2,1)S(1)}, bf16[128,1536]{1,0:T(8,128)(2,1)S(1)}, u32[]{:S(2)}, u32[]{:S(2)}) collective-permute-start(bf16[128,1536]{1,0:T(8,128)(2,1)S(1)} %copy-done.67), channel_id=1, source_target_pairs={{0,8},{4,12},{8,16},{12,20},{16,24},{20,28},{24,0},{28,4},{1,9},{5... | collective-permute-start | bytes 1179656 | tf_op jit(solution)/shard_map/ppermute | solution.py:362
  (149 other events, 1919.5 us)
Sparse Core Ops, SparseCore 0:
  11.4 124.7 all-gather.1
